TPU v7x, 128 devices: a whole 4x4x4 slice. The times are simulated.
128 devices in a mesh: section: 2 (over core), expert: 16 (over z, y), tensor: 4 (over x).
Axes of the slice: x: 4, y: 4, z: 4, core: 2. Of those that a mesh axis runs over, the one named last changes fastest.
Arguments:
- block_input: bfloat16 [2, 1536, 2048], P(None, 'expert'), may hold values from -6 to 6
- cotangent: bfloat16 [2, 1536, 2048], P(None, 'expert'), may hold values from -6 to 6
- segments: int32 [2, 16, 96], P(None, 'expert'), may hold values from 0 to 1, as said below
- routes: int32 [2, 2, 1536, 8], P('section', None, 'expert'), may hold values from 0 to 31, all different within a row; in each aligned block of 24 rows (0 to 23, 24 to 47, ..., all dimensions but the last counted through in order) at most 9 rows name the same one
- norm_attn: bfloat16 [2, 2048], P('section'), may hold values from 0.5 to 1.5
- w_query: bfloat16 [2, 2048, 4096], P('section', None, 'tensor'), may hold values from -0.125 to 0.125
- key_matrix: bfloat16 [2, 2048, 512], P('section', None, 'tensor'), may hold values from -0.125 to 0.125
- value_matrix: bfloat16 [2, 2048, 512], P('section', None, 'tensor'), may hold values from -0.125 to 0.125
- norm_query: bfloat16 [2, 128], P('section'), may hold values from 0.5 to 1.5
- norm_key: bfloat16 [2, 128], P('section'), may hold values from 0.5 to 1.5
- w_output: bfloat16 [2, 4096, 2048], P('section', 'tensor'), may hold values from -0.375 to 0.375
- norm_moe: bfloat16 [2, 2048], P('section'), may hold values from 0.5 to 1.5
- w_router: bfloat16 [2, 2048, 32], P('section'), may hold values from -0.0625 to 0.0625
- w_gate: bfloat16 [2, 32, 2048, 768], P('section', 'expert', None, 'tensor'), may hold values from -0.125 to 0.125
- w_up: bfloat16 [2, 32, 2048, 768], P('section', 'expert', None, 'tensor'), may hold values from -0.125 to 0.125
- w_down: bfloat16 [2, 32, 768, 2048], P('section', 'expert', 'tensor'), may hold values from -0.875 to 0.875
Outputs:
- block_output: bfloat16 [2, 2, 1536, 2048], P('section', None, 'expert')
- input_grad: float32 [2, 2, 1536, 2048], P('section', None, 'expert')
- grad_norm_attn: float32 [2, 2048], P('section')
- grad_query: float32 [2, 2048, 4096], P('section', None, 'tensor')
- grad_key: float32 [2, 2048, 512], P('section', None, 'tensor')
- grad_value: float32 [2, 2048, 512], P('section', None, 'tensor')
- grad_norm_query: float32 [2, 128], P('section')
- grad_norm_key: float32 [2, 128], P('section')
- grad_output: float32 [2, 4096, 2048], P('section', 'tensor')
- grad_norm_moe: float32 [2, 2048], P('section')
- grad_router: float32 [2, 2048, 32], P('section')
- grad_gate: float32 [2, 32, 2048, 768], P('section', 'expert', None, 'tensor')
- grad_up: float32 [2, 32, 2048, 768], P('section', 'expert', None, 'tensor')
- grad_down: float32 [2, 32, 768, 2048], P('section', 'expert', 'tensor')
Inputs may be any that keep to these rules, and one draw needn't show every extreme that they name: In each aligned block of 24 rows (the routes of one device of a data group), the 8 experts of a row differ and no expert is named more than 9 times; in every draw some expert is named exactly 9 times in some block. `segments`: along each group's 96 positions the numbers never fall: the first sequence, then the second. Each sequence has 32 to 64 tokens, and in every draw some sequence has exactly 64.
All inputs are finite; a program needn't handle non-finite values.
Results may differ from a plain program's by a relative error of at most 0.04.
Values may be sent and summed in bfloat16 or wider, within the bound.
A program may use at most 320 MiB of HBM per device.

v0:
```python
import math

import jax
import jax.numpy as jnp
from jax import lax
from jax.sharding import PartitionSpec as P

EPS = 1e-06
THETA = 1000000.0
MASKED = -1e30


def swapped(block, axis, bit):
    count = lax.axis_size(axis)
    route = []
    for low in range(count):
        high = low | 1 << bit
        if high != low and high < count:
            route += [(low, high), (high, low)]
    return lax.ppermute(block, axis, route)


def rms_scale(vector, gain_vec):
    mean_sq = jnp.mean(vector * vector, axis=-1, keepdims=True)
    return vector * lax.rsqrt(mean_sq + EPS) * gain_vec


def rotary(vector, cosine, sine_table):
    half_dim = vector.shape[-1] // 2
    first_half = vector[..., :half_dim]
    second_half = vector[..., half_dim:]
    return jnp.concatenate(
        [
            first_half * cosine - second_half * sine_table,
            second_half * cosine + first_half * sine_table,
        ],
        axis=-1,
    )


def seq_tables(seg_ids, half_dim):
    row_ids = jnp.arange(seg_ids.shape[0], dtype=jnp.int32)
    earlier = jnp.sum((seg_ids[None, :] < seg_ids[:, None]).astype(jnp.int32), axis=1)
    position = (row_ids - earlier).astype(jnp.float32)
    inv_freq = jnp.exp(jnp.arange(half_dim, dtype=jnp.float32) * (-math.log(THETA) / half_dim))
    angles = position[:, None] * inv_freq[None, :]
    allowed = (seg_ids[None, :] == seg_ids[:, None]) & (row_ids[None, :] <= row_ids[:, None])
    return (jnp.cos(angles)[:, None, :], jnp.sin(angles)[:, None, :], allowed)


def query_key(query_raw, key_raw, gain_query, gain_key, cosine, sine_table):
    return (
        rotary(rms_scale(query_raw, gain_query), cosine, sine_table),
        rotary(rms_scale(key_raw, gain_key), cosine, sine_table),
    )


def attend(queries, key_rows, value_rows, allowed, score_scale):
    scores = (
        jnp.einsum("qjrd,kjd->jrqk", queries, key_rows, preferred_element_type=jnp.float32)
        * score_scale
    )
    scores = jnp.where(allowed, scores, MASKED)
    row_max = jnp.max(scores, axis=-1, keepdims=True)
    raised = jnp.exp(scores - row_max)
    row_total = jnp.sum(raised, axis=-1, keepdims=True)
    probs_low = (raised / row_total).astype(jnp.bfloat16)
    attended = jnp.einsum(
        "jrqk,kjd->qjrd", probs_low, value_rows, preferred_element_type=jnp.float32
    )
    return (attended, row_max + jnp.log(row_total))


def attend_back(queries, key_rows, value_rows, allowed, score_scale, log_total, d_attended):
    scores = (
        jnp.einsum("qjrd,kjd->jrqk", queries, key_rows, preferred_element_type=jnp.float32)
        * score_scale
    )
    scores = jnp.where(allowed, scores, MASKED)
    probs = jnp.exp(scores - log_total)
    d_probs = jnp.einsum(
        "qjrd,kjd->jrqk", d_attended, value_rows, preferred_element_type=jnp.float32
    )
    d_values = jnp.einsum(
        "jrqk,qjrd->kjd", probs.astype(jnp.bfloat16), d_attended, preferred_element_type=jnp.float32
    )
    d_scores = (probs * (d_probs - jnp.sum(d_probs * probs, axis=-1, keepdims=True))).astype(
        jnp.bfloat16
    )
    d_queries = (
        jnp.einsum("jrqk,kjd->qjrd", d_scores, key_rows, preferred_element_type=jnp.float32)
        * score_scale
    )
    d_keys = (
        jnp.einsum("jrqk,qjrd->kjd", d_scores, queries, preferred_element_type=jnp.float32)
        * score_scale
    )
    return (d_queries, d_keys, d_values)


def slot_places(chosen, expert_count, group_count, capacity):
    flat_routes = chosen.reshape(-1)
    onehot = (flat_routes[:, None] == jnp.arange(expert_count, dtype=jnp.int32)[None, :]).astype(
        jnp.int32
    )
    slot_index = jnp.sum(onehot * jnp.cumsum(onehot, axis=0), axis=1) - 1
    per_group = expert_count // group_count
    return (
        flat_routes % per_group * group_count + flat_routes // per_group
    ) * capacity + slot_index


def expert_forward(slot_rows, gate_w, up_w, down_w):
    gate_act = jnp.einsum("erd,edf->erf", slot_rows, gate_w, preferred_element_type=jnp.float32)
    up_act = jnp.einsum("erd,edf->erf", slot_rows, up_w, preferred_element_type=jnp.float32)
    hidden = (jax.nn.silu(gate_act) * up_act).astype(jnp.bfloat16)
    return jnp.einsum("erf,efd->erd", hidden, down_w, preferred_element_type=jnp.float32)


def expert_back(slot_rows, d_produced, gate_w, up_w, down_w):
    gate_act = jnp.einsum("erd,edf->erf", slot_rows, gate_w, preferred_element_type=jnp.float32)
    up_act = jnp.einsum("erd,edf->erf", slot_rows, up_w, preferred_element_type=jnp.float32)
    silu_value, silu_back = jax.vjp(jax.nn.silu, gate_act)
    hidden = (silu_value * up_act).astype(jnp.bfloat16)
    grad_down = jnp.einsum("erf,erd->efd", hidden, d_produced, preferred_element_type=jnp.float32)
    d_hidden = jnp.einsum("erd,efd->erf", d_produced, down_w, preferred_element_type=jnp.float32)
    d_gate = silu_back(d_hidden * up_act)[0].astype(jnp.bfloat16)
    d_up = (d_hidden * silu_value).astype(jnp.bfloat16)
    grad_gate = jnp.einsum("erd,erf->edf", slot_rows, d_gate, preferred_element_type=jnp.float32)
    grad_up = jnp.einsum("erd,erf->edf", slot_rows, d_up, preferred_element_type=jnp.float32)
    d_rows = jnp.einsum("erf,edf->erd", d_gate, gate_w, preferred_element_type=jnp.float32)
    d_rows = d_rows + jnp.einsum("erf,edf->erd", d_up, up_w, preferred_element_type=jnp.float32)
    return (d_rows, grad_gate, grad_up, grad_down)


def send_rows(buffer):
    return lax.all_to_all(buffer, "expert", split_axis=1, concat_axis=1, tiled=True)


def return_rows(buffer):
    return lax.all_to_all(buffer, "expert", split_axis=1, concat_axis=1, tiled=True)


def swap_section(vector):
    return swapped(vector, "section", 0)


def pick_state(flag, first_state, second_state):
    return jax.tree.map(
        lambda left_arr, right_arr: jnp.where(flag, left_arr, right_arr), first_state, second_state
    )


def body(
    block_input,
    cotangent,
    segments,
    routes,
    norm_attn,
    w_query,
    key_matrix,
    value_matrix,
    norm_query,
    norm_key,
    w_output,
    norm_moe,
    w_router,
    w_gate,
    w_up,
    w_down,
):
    tensor_count = lax.axis_size("tensor")
    group_count = lax.axis_size("expert")
    section_index = lax.axis_index("section")
    tensor_index = lax.axis_index("tensor")
    micro_count, group_rows, model_width = block_input.shape
    top_count = routes.shape[3]
    expert_count = w_router.shape[2]
    local_experts = w_gate.shape[1]
    quarter_rows = group_rows // tensor_count
    capacity = max(2, min(quarter_rows, 3 * quarter_rows * top_count // (2 * expert_count)))
    head_dim = norm_query.shape[1]
    kv_heads = key_matrix.shape[2] // head_dim
    q_heads = w_query.shape[2] // head_dim
    heads_per_group = q_heads // kv_heads
    score_scale = 1.0 / math.sqrt(head_dim)
    quarter_start = tensor_index * quarter_rows
    slot_shape = (local_experts, group_count, capacity, model_width)
    gain_attn = norm_attn[0]
    query_w = w_query[0]
    key_w = key_matrix[0]
    value_w = value_matrix[0]
    gain_query = norm_query[0]
    gain_key = norm_key[0]
    output_w = w_output[0]
    gain_moe = norm_moe[0]
    router_w = w_router[0]

    def spread(slot_rows):
        return lax.all_gather(slot_rows, "tensor", axis=1, tiled=True)

    def collect(partial_rows):
        return lax.psum_scatter(
            partial_rows.astype(jnp.bfloat16), "tensor", scatter_dimension=1, tiled=True
        ).astype(jnp.float32)

    expert_gate, expert_up, expert_down = (w_gate[0], w_up[0], w_down[0])

    def micro_tables(micro_index):
        seg_ids = lax.dynamic_index_in_dim(segments, micro_index, 0, keepdims=False)[0]
        cosine, sine_table, allowed = seq_tables(seg_ids, head_dim // 2)
        chosen = lax.dynamic_index_in_dim(routes[0], micro_index, 0, keepdims=False)
        chosen = lax.dynamic_slice_in_dim(chosen, quarter_start, quarter_rows, 0)
        places = slot_places(chosen, expert_count, group_count, capacity)
        return (cosine, sine_table, allowed, chosen, places)

    def project(normed_low):
        query_raw = jnp.dot(normed_low, query_w, preferred_element_type=jnp.float32).reshape(
            group_rows, q_heads, head_dim
        )
        key_raw = jnp.dot(normed_low, key_w, preferred_element_type=jnp.float32).reshape(
            group_rows, kv_heads, head_dim
        )
        value_low = (
            jnp.dot(normed_low, value_w, preferred_element_type=jnp.float32)
            .reshape(group_rows, kv_heads, head_dim)
            .astype(jnp.bfloat16)
        )
        return (query_raw, key_raw, value_low)

    def route_gates(moe_in, chosen):
        logits = jnp.dot(moe_in, router_w, preferred_element_type=jnp.float32)
        return jax.nn.softmax(jnp.take_along_axis(logits, chosen, axis=1), axis=-1)

    def layer_backward(input_low, tables, saved_state, grad_out):
        cosine, sine_table, allowed, chosen, places = tables
        attn_total, log_total, attended_low, slot_rows, picked = saved_state
        residual = input_low.astype(jnp.float32)
        mid_resid = residual + attn_total
        mid_part = lax.dynamic_slice_in_dim(mid_resid, quarter_start, quarter_rows, 0)
        moe_normed, moe_norm_back = jax.vjp(rms_scale, mid_part, gain_moe.astype(jnp.float32))
        moe_in = moe_normed.astype(jnp.bfloat16)
        gate_weights = route_gates(moe_in, chosen)
        grad_part = lax.dynamic_slice_in_dim(grad_out, quarter_start, quarter_rows, 0)
        d_gates = jnp.sum(grad_part[:, None, :] * picked.astype(jnp.float32), axis=2)
        d_chosen = gate_weights * (d_gates - jnp.sum(d_gates * gate_weights, axis=1, keepdims=True))
        onehot = (
            chosen[:, :, None] == jnp.arange(expert_count, dtype=jnp.int32)[None, None, :]
        ).astype(jnp.float32)
        d_logits = jnp.sum(d_chosen[:, :, None] * onehot, axis=1).astype(jnp.bfloat16)
        router_term = jnp.dot(moe_in.T, d_logits, preferred_element_type=jnp.float32)
        d_moe_in = jnp.dot(d_logits, router_w.T, preferred_element_type=jnp.float32)
        d_picked = (gate_weights[:, :, None] * grad_part[:, None, :]).astype(jnp.bfloat16)
        buffer = (
            jnp.zeros((expert_count * capacity, model_width), jnp.bfloat16)
            .at[places]
            .set(d_picked.reshape(-1, model_width))
        )
        arrived = send_rows(buffer.reshape(slot_shape))
        d_slots = spread(arrived.reshape(local_experts, group_count * capacity, model_width))
        d_rows, grad_gate, grad_up, grad_down = expert_back(
            slot_rows, d_slots, expert_gate, expert_up, expert_down
        )
        returned = return_rows(collect(d_rows).astype(jnp.bfloat16).reshape(slot_shape))
        d_copies = returned.reshape(-1, model_width)[places].reshape(
            quarter_rows, top_count, model_width
        )
        d_moe_in = d_moe_in + jnp.sum(d_copies.astype(jnp.float32), axis=1)
        d_mid_part, gain_moe_term = moe_norm_back(d_moe_in)
        d_mid_all, router_terms, gain_terms = (
            lax.all_gather(d_mid_part.astype(jnp.bfloat16), "tensor", axis=0, tiled=True).astype(
                d_mid_part.dtype
            ),
            lax.all_gather(
                router_term[None].astype(jnp.bfloat16), "tensor", axis=0, tiled=True
            ).astype(jnp.float32),
            lax.all_gather(
                gain_moe_term[None].astype(jnp.bfloat16), "tensor", axis=0, tiled=True
            ).astype(jnp.float32),
        )
        d_mid = grad_out + d_mid_all
        normed, attn_norm_back = jax.vjp(rms_scale, residual, gain_attn.astype(jnp.float32))
        normed_low = normed.astype(jnp.bfloat16)
        query_raw, key_raw, value_low = project(normed_low)

        def rotate_local(query_in, key_in, gain_q, gain_k):
            return query_key(query_in, key_in, gain_q, gain_k, cosine, sine_table)

        rotated, rotate_back = jax.vjp(
            rotate_local,
            query_raw,
            key_raw,
            gain_query.astype(jnp.float32),
            gain_key.astype(jnp.float32),
        )
        query_low = (
            rotated[0].astype(jnp.bfloat16).reshape(group_rows, kv_heads, heads_per_group, head_dim)
        )
        key_low = rotated[1].astype(jnp.bfloat16)
        d_attn_low = d_mid.astype(jnp.bfloat16)
        grad_output = jnp.dot(attended_low.T, d_attn_low, preferred_element_type=jnp.float32)
        d_attended = jnp.dot(d_attn_low, output_w.T, preferred_element_type=jnp.float32).astype(
            jnp.bfloat16
        )
        d_attended = d_attended.reshape(group_rows, kv_heads, heads_per_group, head_dim)
        d_query_rot, d_key_rot, d_value = attend_back(
            query_low, key_low, value_low, allowed, score_scale, log_total, d_attended
        )
        d_query_raw, d_key_raw, d_gain_q, d_gain_k = rotate_back(
            (d_query_rot.reshape(group_rows, q_heads, head_dim), d_key_rot)
        )
        d_query = d_query_raw.astype(jnp.bfloat16).reshape(group_rows, q_heads * head_dim)
        d_key = d_key_raw.astype(jnp.bfloat16).reshape(group_rows, kv_heads * head_dim)
        d_value = d_value.astype(jnp.bfloat16).reshape(group_rows, kv_heads * head_dim)
        grad_query = jnp.dot(normed_low.T, d_query, preferred_element_type=jnp.float32)
        grad_key = jnp.dot(normed_low.T, d_key, preferred_element_type=jnp.float32)
        grad_value = jnp.dot(normed_low.T, d_value, preferred_element_type=jnp.float32)
        d_normed = jnp.dot(d_query, query_w.T, preferred_element_type=jnp.float32)
        d_normed = d_normed + jnp.dot(d_key, key_w.T, preferred_element_type=jnp.float32)
        d_normed = d_normed + jnp.dot(d_value, value_w.T, preferred_element_type=jnp.float32)
        d_normed, d_gain_q, d_gain_k = (
            lax.psum(d_normed.astype(jnp.bfloat16), "tensor").astype(jnp.float32),
            lax.psum(d_gain_q.astype(jnp.bfloat16), "tensor").astype(jnp.float32),
            lax.psum(d_gain_k.astype(jnp.bfloat16), "tensor").astype(jnp.float32),
        )
        d_residual, grad_gain_attn = attn_norm_back(d_normed)
        grad_terms = (
            grad_gain_attn,
            grad_query,
            grad_key,
            grad_value,
            d_gain_q,
            d_gain_k,
            grad_output,
            jnp.sum(gain_terms, axis=0),
            jnp.sum(router_terms, axis=0),
            grad_gate,
            grad_up,
            grad_down,
        )
        return (d_mid + d_residual, grad_terms)

    ticks = micro_count + 1
    incoming = jnp.zeros((group_rows, model_width), jnp.bfloat16)
    outputs = jnp.zeros((micro_count, group_rows, model_width), jnp.bfloat16)
    saved_list = []
    for tick_index in range(ticks):
        micro_index = tick_index - section_index
        live_flag = (micro_index >= 0) & (micro_index < micro_count)
        clamped = jnp.clip(micro_index, 0, micro_count - 1)
        layer_in = jnp.where(
            section_index == 0, block_input[min(tick_index, micro_count - 1)], incoming
        )
        layer_cosine, layer_sine_table, layer_allowed, layer_chosen, layer_places = micro_tables(
            clamped
        )
        layer_residual = layer_in.astype(jnp.float32)
        layer_normed_low = rms_scale(layer_residual, gain_attn).astype(jnp.bfloat16)
        layer_query_raw, layer_key_raw, layer_value_low = project(layer_normed_low)
        query_rot, key_rot = query_key(
            layer_query_raw, layer_key_raw, gain_query, gain_key, layer_cosine, layer_sine_table
        )
        layer_query_low = query_rot.astype(jnp.bfloat16).reshape(
            group_rows, kv_heads, heads_per_group, head_dim
        )
        attended, layer_log_total = attend(
            layer_query_low,
            key_rot.astype(jnp.bfloat16),
            layer_value_low,
            layer_allowed,
            score_scale,
        )
        layer_attended_low = attended.astype(jnp.bfloat16).reshape(group_rows, q_heads * head_dim)
        layer_attn_total = lax.psum(
            jnp.dot(layer_attended_low, output_w, preferred_element_type=jnp.float32).astype(
                jnp.bfloat16
            ),
            "tensor",
        ).astype(jnp.float32)
        layer_mid_resid = layer_residual + layer_attn_total
        layer_mid_part = lax.dynamic_slice_in_dim(layer_mid_resid, quarter_start, quarter_rows, 0)
        layer_moe_in = rms_scale(layer_mid_part, gain_moe).astype(jnp.bfloat16)
        layer_gate_weights = route_gates(layer_moe_in, layer_chosen)
        layer_buffer = (
            jnp.zeros((expert_count * capacity, model_width), jnp.bfloat16)
            .at[layer_places]
            .set(jnp.repeat(layer_moe_in, top_count, axis=0))
        )
        layer_arrived = send_rows(layer_buffer.reshape(slot_shape))
        layer_slot_rows = spread(
            layer_arrived.reshape(local_experts, group_count * capacity, model_width)
        )
        produced = collect(expert_forward(layer_slot_rows, expert_gate, expert_up, expert_down))
        layer_returned = return_rows(produced.astype(jnp.bfloat16).reshape(slot_shape))
        layer_picked = layer_returned.reshape(-1, model_width)[layer_places].reshape(
            quarter_rows, top_count, model_width
        )
        moe_part = jnp.sum(
            layer_gate_weights[:, :, None] * layer_picked.astype(jnp.float32), axis=1
        )
        moe_all = lax.all_gather(moe_part.astype(jnp.bfloat16), "tensor", axis=0, tiled=True)
        output = layer_mid_resid + moe_all.astype(jnp.float32)
        output, saved_state = (
            output,
            (layer_attn_total, layer_log_total, layer_attended_low, layer_slot_rows, layer_picked),
        )
        output_low = output.astype(jnp.bfloat16)
        outputs = jnp.where(
            live_flag, lax.dynamic_update_index_in_dim(outputs, output_low, clamped, 0), outputs
        )
        saved_list.append((layer_in, saved_state))
        if tick_index + 1 < ticks:
            incoming = swap_section(output_low)
    returning = jnp.zeros((group_rows, model_width), jnp.bfloat16)
    input_grads = jnp.zeros((micro_count, group_rows, model_width), jnp.float32)
    totals = None
    for tick_index in range(ticks):
        micro_index = tick_index - 1 + section_index
        live_flag = (micro_index >= 0) & (micro_index < micro_count)
        clamped = jnp.clip(micro_index, 0, micro_count - 1)
        upstream = jnp.where(
            section_index == 1,
            cotangent[min(tick_index, micro_count - 1)].astype(jnp.float32),
            returning.astype(jnp.float32),
        )
        layer_in, saved_state = pick_state(
            section_index == 0,
            saved_list[max(tick_index - 1, 0)],
            saved_list[min(tick_index + 1, micro_count)],
        )
        d_input, grad_terms = layer_backward(layer_in, micro_tables(clamped), saved_state, upstream)
        grad_terms = tuple((jnp.where(live_flag, term, 0.0) for term in grad_terms))
        if totals is None:
            totals = grad_terms
        else:
            totals = tuple((running + term for running, term in zip(totals, grad_terms)))
        input_grads = jnp.where(
            live_flag,
            lax.dynamic_update_index_in_dim(input_grads, d_input, clamped, 0),
            input_grads,
        )
        if tick_index + 1 < ticks:
            returning = swap_section(d_input.astype(jnp.bfloat16))
    shared = (
        lax.psum(totals[0].astype(jnp.bfloat16), "expert").astype(jnp.float32),
        lax.psum(totals[1].astype(jnp.bfloat16), "expert").astype(jnp.float32),
        lax.psum(totals[2].astype(jnp.bfloat16), "expert").astype(jnp.float32),
        lax.psum(totals[3].astype(jnp.bfloat16), "expert").astype(jnp.float32),
        lax.psum(totals[4].astype(jnp.bfloat16), "expert").astype(jnp.float32),
        lax.psum(totals[5].astype(jnp.bfloat16), "expert").astype(jnp.float32),
        lax.psum(totals[6].astype(jnp.bfloat16), "expert").astype(jnp.float32),
        lax.psum(totals[7].astype(jnp.bfloat16), "expert").astype(jnp.float32),
        lax.psum(totals[8].astype(jnp.bfloat16), "expert").astype(jnp.float32),
    )
    expert_grads = (totals[9], totals[10], totals[11])
    return (
        outputs[None],
        input_grads[None],
        shared[0][None],
        shared[1][None],
        shared[2][None],
        shared[3][None],
        shared[4][None],
        shared[5][None],
        shared[6][None],
        shared[7][None],
        shared[8][None],
        expert_grads[0][None],
        expert_grads[1][None],
        expert_grads[2][None],
    )


def solution(mesh):
    placed = (
        P(None, "expert", None),
        P(None, "expert", None),
        P(None, "expert", None),
        P("section", None, "expert", None),
        P("section", None),
        P("section", None, "tensor"),
        P("section", None, "tensor"),
        P("section", None, "tensor"),
        P("section", None),
        P("section", None),
        P("section", "tensor", None),
        P("section", None),
        P("section", None, None),
        P("section", "expert", None, "tensor"),
        P("section", "expert", None, "tensor"),
        P("section", "expert", "tensor", None),
    )
    return jax.shard_map(
        body,
        mesh=mesh,
        in_specs=placed,
        out_specs=(
            P("section", None, "expert", None),
            P("section", None, "expert", None),
            P("section", None),
            P("section", None, "tensor"),
            P("section", None, "tensor"),
            P("section", None, "tensor"),
            P("section", None),
            P("section", None),
            P("section", "tensor", None),
            P("section", None),
            P("section", None, None),
            P("section", "expert", None, "tensor"),
            P("section", "expert", None, "tensor"),
            P("section", "expert", "tensor", None),
        ),
        check_vma=False,
    )
```

profile of v0, /device:TPU:0, one launch (start us, length us, event | category | flops | bytes accessed | tf_op | source)
XLA Modules:
  0.0 1780.1 jit_solution(7347346123797221550)
XLA Ops:
  32.8 42.7 %all-reduce.29.cloned.1.call-done = bf16[96,2048]{1,0:T(8,128)(2,1)} async-done(((bf16[96,2048]{1,0:T(8,128)(2,1)}), bf16[96,2048]{1,0:T(8,128)(2,1)}) %all-reduce.29.cloned.1.call-update) | async-done | bytes 393232 | tf_op jit(solution)/shard_map/psum | solution.py:374
  84.2 23.4 %all_to_all.60 = bf16[2,16,9,2048]{3,0,2,1:T(2,128)(2,1)S(1)} all-to-all(bf16[2,16,9,2048]{3,0,2,1:T(2,128)(2,1)S(1)} %copy.301), channel_id=1, replica_groups=mesh['section'=2,'expert'=16,'tensor'=4] {'expert'}, dimensions={1} | all-to-all | bytes 2359296 | tf_op jit(solution)/shard_map/all_to_all | solution.py:137
  109.3 49.5 %all-gather.13.cloned.1.call-done = bf16[2,576,2048]{2,1,0:T(8,128)(2,1)} async-done(((bf16[2,144,2048]{2,1,0:T(8,128)(2,1)}), bf16[2,576,2048]{2,1,0:T(8,128)(2,1)}) %all-gather.13.cloned.1.call-update) | async-done | bytes 4718608 | tf_op jit(solution)/shard_map/all_gather | solution.py:200
  172.5 51.4 %reduce-scatter.7.cloned.1.call-done = bf16[2,144,2048]{2,1,0:T(8,128)(2,1)} async-done(((bf16[2,576,2048]{2,1,0:T(8,128)(2,1)}), bf16[2,144,2048]{2,1,0:T(8,128)(2,1)}) %reduce-scatter.7.cloned.1.call-update) | async-done | bytes 1179664 | tf_op jit(solution)/shard_map/reduce_scatter | solution.py:203
  238.1 15.7 all-to-all-done.1
  305.9 37.2 %all-reduce.31.cloned.1.call-done = bf16[96,2048]{1,0:T(8,128)(2,1)} async-done(((bf16[96,2048]{1,0:T(8,128)(2,1)}), bf16[96,2048]{1,0:T(8,128)(2,1)}) %all-reduce.31.cloned.1.call-update) | async-done | bytes 393232 | tf_op jit(solution)/shard_map/psum | solution.py:374
  354.0 23.3 %all_to_all.61 = bf16[2,16,9,2048]{3,0,2,1:T(2,128)(2,1)S(1)} all-to-all(bf16[2,16,9,2048]{3,0,2,1:T(2,128)(2,1)S(1)} %copy.315), channel_id=1, replica_groups=mesh['section'=2,'expert'=16,'tensor'=4] {'expert'}, dimensions={1} | all-to-all | bytes 2359296 | tf_op jit(solution)/shard_map/all_to_all | solution.py:137
  379.0 49.4 %all-gather.15.cloned.1.call-done = bf16[2,576,2048]{2,1,0:T(8,128)(2,1)} async-done(((bf16[2,144,2048]{2,1,0:T(8,128)(2,1)}), bf16[2,576,2048]{2,1,0:T(8,128)(2,1)}) %all-gather.15.cloned.1.call-update) | async-done | bytes 4718608 | tf_op jit(solution)/shard_map/all_gather | solution.py:200
  548.3 21.3 %all_to_all.62 = bf16[2,16,9,2048]{3,0,2,1:T(2,128)(2,1)S(1)} all-to-all(bf16[2,16,9,2048]{3,0,2,1:T(2,128)(2,1)S(1)} %copy.341), channel_id=1, replica_groups=mesh['section'=2,'expert'=16,'tensor'=4] {'expert'}, dimensions={1} | all-to-all | bytes 2359296 | tf_op jit(solution)/shard_map/all_to_all | solution.py:137
  579.8 40.0 %all-gather.19.cloned.1.call-done = bf16[2,576,2048]{2,1,0:T(8,128)(2,1)} async-done(((bf16[2,144,2048]{2,1,0:T(8,128)(2,1)}), bf16[2,576,2048]{2,1,0:T(8,128)(2,1)}) %all-gather.19.cloned.1.call-update) | async-done | bytes 4718608 | tf_op jit(solution)/shard_map/all_gather | solution.py:200
  666.4 18.4 %reduce-scatter.13.cloned.1.call-done = bf16[2,144,2048]{2,1,0:T(8,128)(2,1)} async-done(((bf16[2,576,2048]{2,1,0:T(8,128)(2,1)}), bf16[2,144,2048]{2,1,0:T(8,128)(2,1)}) %reduce-scatter.13.cloned.1.call-update) | async-done | bytes 1179664 | tf_op jit(solution)/shard_map/reduce_scatter | solution.py:203
  771.1 40.8 %all-reduce.39.cloned.1.call-done = (bf16[96,2048]{1,0:T(8,128)(2,1)}, bf16[96,2048]{1,0:T(8,128)(2,1)}) async-done(((bf16[96,2048]{1,0:T(8,128)(2,1)}, bf16[96,2048]{1,0:T(8,128)(2,1)}), (bf16[96,2048]{1,0:T(8,128)(2,1)}, bf16[96,2048]{1,0:T(8,128)(2,1)})) %all-reduce.39.cloned.1.call-update) | async-done | bytes 786448 | tf_op jit(solution)/shard_map/psum | solution.py:374
  824.5 23.7 %all_to_all.63 = bf16[2,16,9,2048]{3,0,2,1:T(2,128)(2,1)S(1)} all-to-all(bf16[2,16,9,2048]{3,0,2,1:T(2,128)(2,1)S(1)} %copy.329), channel_id=1, replica_groups=mesh['section'=2,'expert'=16,'tensor'=4] {'expert'}, dimensions={1} | all-to-all | bytes 2359296 | tf_op jit(solution)/shard_map/all_to_all | solution.py:137
  849.9 49.3 %all-gather.17.cloned.1.call-done = bf16[2,576,2048]{2,1,0:T(8,128)(2,1)} async-done(((bf16[2,144,2048]{2,1,0:T(8,128)(2,1)}), bf16[2,576,2048]{2,1,0:T(8,128)(2,1)}) %all-gather.17.cloned.1.call-update) | async-done | bytes 4718608 | tf_op jit(solution)/shard_map/all_gather | solution.py:200
  940.6 23.8 %reduce-scatter.11.cloned.1.call-done = bf16[2,144,2048]{2,1,0:T(8,128)(2,1)} async-done(((bf16[2,576,2048]{2,1,0:T(8,128)(2,1)}), bf16[2,144,2048]{2,1,0:T(8,128)(2,1)}) %reduce-scatter.11.cloned.1.call-update) | async-done | bytes 1179664 | tf_op jit(solution)/shard_map/reduce_scatter | solution.py:203
  1017.7 21.6 %all_to_all.64 = bf16[2,16,9,2048]{3,0,2,1:T(2,128)(2,1)S(1)} all-to-all(bf16[2,16,9,2048]{3,0,2,1:T(2,128)(2,1)S(1)} %copy.358), channel_id=1, replica_groups=mesh['section'=2,'expert'=16,'tensor'=4] {'expert'}, dimensions={1} | all-to-all | bytes 2359296 | tf_op jit(solution)/shard_map/all_to_all | solution.py:137
  1059.3 30.2 %all-gather.21.cloned.1.call-done = bf16[2,576,2048]{2,1,0:T(8,128)(2,1)} async-done(((bf16[2,144,2048]{2,1,0:T(8,128)(2,1)}), bf16[2,576,2048]{2,1,0:T(8,128)(2,1)}) %all-gather.21.cloned.1.call-update) | async-done | bytes 4718608 | tf_op jit(solution)/shard_map/all_gather | solution.py:200
  1130.8 21.1 %reduce-scatter.15.cloned.1.call-done = bf16[2,144,2048]{2,1,0:T(8,128)(2,1)} async-done(((bf16[2,576,2048]{2,1,0:T(8,128)(2,1)}), bf16[2,144,2048]{2,1,0:T(8,128)(2,1)}) %reduce-scatter.15.cloned.1.call-update) | async-done | bytes 1179664 | tf_op jit(solution)/shard_map/reduce_scatter | solution.py:203
  1246.8 29.9 %all-reduce.33.cloned.1.call-done = bf16[96,2048]{1,0:T(8,128)(2,1)} async-done(((bf16[96,2048]{1,0:T(8,128)(2,1)}), bf16[96,2048]{1,0:T(8,128)(2,1)}) %all-reduce.33.cloned.1.call-update) | async-done | bytes 393232 | tf_op jit(solution)/shard_map/psum | solution.py:322
  1302.9 25.7 %all_to_all.65 = bf16[2,16,9,2048]{3,0,2,1:T(2,128)(2,1)S(1)} all-to-all(bf16[2,16,9,2048]{3,0,2,1:T(2,128)(2,1)S(1)} %copy.375), channel_id=1, replica_groups=mesh['section'=2,'expert'=16,'tensor'=4] {'expert'}, dimensions={1} | all-to-all | bytes 2359296 | tf_op jit(solution)/shard_map/all_to_all | solution.py:137
  1341.0 38.7 %all-gather.23.cloned.1.call-done = bf16[2,576,2048]{2,1,0:T(8,128)(2,1)} async-done(((bf16[2,144,2048]{2,1,0:T(8,128)(2,1)}), bf16[2,576,2048]{2,1,0:T(8,128)(2,1)}) %all-gather.23.cloned.1.call-update) | async-done | bytes 4718608 | tf_op jit(solution)/shard_map/all_gather | solution.py:200
  1392.4 16.1 all-gather.3
  1426.5 16.4 all-gather.4
  1678.6 75.5 %all-reduce.18 = (bf16[1,2048]{1,0:T(2,128)(2,1)S(1)}, bf16[1,128]{1,0:T(2,128)(2,1)S(1)}, bf16[1,128]{1,0:T(2,128)(2,1)S(1)}, bf16[1,2048]{1,0:T(2,128)(2,1)S(1)}) all-reduce(bf16[1,2048]{1,0:T(2,128)(2,1)S(1)} %broadcast_in_dim.420, ...), channel_id=1, replica_groups=mesh['section'=2,'expert'=16,'tensor'=4] {'expert'}, use_global_device_ids=true, to_apply=%region_117.119 | all-reduce | flops 4352 | bytes 17408 | tf_op jit(solution)/shard_map/psum | solution.py:445
  (1172 shorter events, 976.2 us)
Async XLA Ops:
  7.2 68.3 %all-reduce.29.cloned.1.call-start = ((), (), s32[]{:S(2)}) async-start(), calls=%async_computation.18 | async-start | bytes 786432 | tf_op jit(solution)/shard_map/psum | solution.py:374
  30.7 128.0 %all-gather.13.cloned.1.call-start = ((), (), s32[]{:S(2)}) async-start(), calls=%async_computation.19 | async-start | bytes 5898240 | tf_op jit(solution)/shard_map/all_gather | solution.py:200
  109.0 114.9 %reduce-scatter.7.cloned.1.call-start = ((), (), s32[]{:S(2)}) async-start(), calls=%async_computation.20 | async-start | bytes 5898240 | tf_op jit(solution)/shard_map/reduce_scatter | solution.py:203
  234.5 108.6 %all-reduce.31.cloned.1.call-start = ((), (), s32[]{:S(2)}) async-start(), calls=%async_computation.21 | async-start | bytes 786432 | tf_op jit(solution)/shard_map/psum | solution.py:374
  304.5 124.0 %all-gather.15.cloned.1.call-start = ((), (), s32[]{:S(2)}) async-start(), calls=%async_computation.22 | async-start | bytes 5898240 | tf_op jit(solution)/shard_map/all_gather | solution.py:200
  378.7 114.9 %reduce-scatter.9.cloned.1.call-start = ((), (), s32[]{:S(2)}) async-start(), calls=%async_computation.23 | async-start | bytes 5898240 | tf_op jit(solution)/shard_map/reduce_scatter | solution.py:203
  497.1 26.4 %all-to-all-start.3 = ((bf16[2,16,9,2048]{3,0,2,1:T(2,128)(2,1)}), bf16[2,16,9,2048]{3,0,2,1:T(2,128)(2,1)}, u32[]{:S(2)}, u32[]{:S(2)}) async-start(bf16[2,16,9,2048]{3,0,2,1:T(2,128)(2,1)} %bitcast.1131), calls=%async_computation.5 | async-start | bytes 2359296 | tf_op jit(solution)/shard_map/all_to_all | solution.py:141
  504.2 115.7 %all-gather.19.cloned.1.call-start = ((), (), s32[]{:S(2)}) async-start(), calls=%async_computation.26 | async-start | bytes 5898240 | tf_op jit(solution)/shard_map/all_gather | solution.py:200
  571.1 113.7 %reduce-scatter.13.cloned.1.call-start = ((), (), s32[]{:S(2)}) async-start(), calls=%async_computation.27 | async-start | bytes 5898240 | tf_op jit(solution)/shard_map/reduce_scatter | solution.py:203
  688.3 26.8 %all-to-all-start.7 = ((bf16[2,16,9,2048]{3,0,2,1:T(2,128)(2,1)}), bf16[2,16,9,2048]{3,0,2,1:T(2,128)(2,1)}, u32[]{:S(2)}, u32[]{:S(2)}) async-start(bf16[2,16,9,2048]{3,0,2,1:T(2,128)(2,1)} %bitcast.1129), calls=%async_computation.11 | async-start | bytes 2359296 | tf_op jit(solution)/shard_map/all_to_all | solution.py:141
  695.4 116.5 %all-reduce.39.cloned.1.call-start = ((), (), s32[]{:S(2)}) async-start(), calls=%async_computation.35 | async-start | bytes 1572864 | tf_op jit(solution)/shard_map/psum | solution.py:374
  771.1 128.2 %all-gather.17.cloned.1.call-start = ((), (), s32[]{:S(2)}) async-start(), calls=%async_computation.24 | async-start | bytes 5898240 | tf_op jit(solution)/shard_map/all_gather | solution.py:200
  849.7 114.7 %reduce-scatter.11.cloned.1.call-start = ((), (), s32[]{:S(2)}) async-start(), calls=%async_computation.25 | async-start | bytes 5898240 | tf_op jit(solution)/shard_map/reduce_scatter | solution.py:203
  936.9 44.8 %collective-permute-start.2 = (bf16[96,2048]{1,0:T(8,128)(2,1)}, bf16[96,2048]{1,0:T(8,128)(2,1)}, u32[]{:S(2)}, u32[]{:S(2)}) collective-permute-start(bf16[96,2048]{1,0:T(8,128)(2,1)} %fusion.624), channel_id=1, source_target_pairs={{0,64},{64,0},{1,65},{65,1},{2,66},{66,2},{3,67},{67,3},{4,68},{68... | collective-permute-start | bytes 1179656 | tf_op jit(solution)/shard_map/ppermute | solution.py:20
  967.9 26.4 %all-to-all-start.5 = ((bf16[2,16,9,2048]{3,0,2,1:T(2,128)(2,1)}), bf16[2,16,9,2048]{3,0,2,1:T(2,128)(2,1)}, u32[]{:S(2)}, u32[]{:S(2)}) async-start(bf16[2,16,9,2048]{3,0,2,1:T(2,128)(2,1)} %bitcast.1133), calls=%async_computation.8 | async-start | bytes 2359296 | tf_op jit(solution)/shard_map/all_to_all | solution.py:141
  975.0 114.5 %all-gather.21.cloned.1.call-start = ((), (), s32[]{:S(2)}) async-start(), calls=%async_computation.28 | async-start | bytes 5898240 | tf_op jit(solution)/shard_map/all_gather | solution.py:200
  1040.7 111.1 %reduce-scatter.15.cloned.1.call-start = ((), (), s32[]{:S(2)}) async-start(), calls=%async_computation.29 | async-start | bytes 5898240 | tf_op jit(solution)/shard_map/reduce_scatter | solution.py:203
  1155.3 26.4 %all-to-all-start.9 = ((bf16[2,16,9,2048]{3,0,2,1:T(2,128)(2,1)}), bf16[2,16,9,2048]{3,0,2,1:T(2,128)(2,1)}, u32[]{:S(2)}, u32[]{:S(2)}) async-start(bf16[2,16,9,2048]{3,0,2,1:T(2,128)(2,1)} %bitcast.1130), calls=%async_computation.14 | async-start | bytes 2359296 | tf_op jit(solution)/shard_map/all_to_all | solution.py:141
  1162.4 114.3 %all-reduce.33.cloned.1.call-start = ((), (), s32[]{:S(2)}) async-start(), calls=%async_computation.30 | async-start | bytes 786432 | tf_op jit(solution)/shard_map/psum | solution.py:322
  1238.1 141.6 %all-gather.23.cloned.1.call-start = ((), (), s32[]{:S(2)}) async-start(), calls=%async_computation.31 | async-start | bytes 5898240 | tf_op jit(solution)/shard_map/all_gather | solution.py:200
  1330.1 129.2 %reduce-scatter.17.cloned.1.call-start = ((), (), s32[]{:S(2)}) async-start(), calls=%async_computation.32 | async-start | bytes 5898240 | tf_op jit(solution)/shard_map/reduce_scatter | solution.py:203
  1462.9 26.7 %all-to-all-start.11 = ((bf16[2,16,9,2048]{3,0,2,1:T(2,128)(2,1)}), bf16[2,16,9,2048]{3,0,2,1:T(2,128)(2,1)}, u32[]{:S(2)}, u32[]{:S(2)}) async-start(bf16[2,16,9,2048]{3,0,2,1:T(2,128)(2,1)} %bitcast.1132), calls=%async_computation.17 | async-start | bytes 2359296 | tf_op jit(solution)/shard_map/all_to_all | solution.py:141
  1470.0 207.1 %all-reduce.35.cloned.1.call-start = ((), (), s32[]{:S(2)}) async-start(), calls=%async_computation.33 | async-start | bytes 786432 | tf_op jit(solution)/shard_map/psum | solution.py:322
  1542.0 216.8 %all-reduce.37.cloned.1.call-start = ((), (), s32[]{:S(2)}) async-start(), calls=%async_computation.34 | async-start | bytes 19136512 | tf_op jit(solution)/shard_map/psum | solution.py:446
  (310 other events, 4383.7 us)
Sparse Core Ops, SparseCore 0:
  30.9 44.5 all-reduce.28
  109.2 49.5 all-gather.12
  172.5 51.4 reduce-scatter.6
  304.6 38.5 all-reduce.30
  378.8 49.5 all-gather.14
  442.1 51.4 reduce-scatter.8
  571.2 48.6 all-gather.18
  630.6 54.1 reduce-scatter.12
  771.2 40.7 all-reduce.38
  849.8 49.3 all-gather.16
  912.9 51.4 reduce-scatter.10
  1040.8 48.5 all-gather.20
  1100.3 51.4 reduce-scatter.14
  1238.3 38.3 all-reduce.32
  1330.2 49.4 all-gather.22
  1390.4 57.0 reduce-scatter.16
  1542.1 42.1 all-reduce.34
  1589.4 154.1 all-reduce.36
where the time goes:
time: 1800 us; the launch traced here: 1780 us
  waiting for transfers between devices  586 us (33%)
  blocking collectives  384 us (21%)
  matrix products  289 us (16%)
  local copies, waits for them, and re-layouts  239 us (13%)
  other arithmetic  217 us (12%)
  starting transfers between devices  46 us (3%)
  between operations  18.6 us (1%)
    all_gather x6, waiting for transfers between devices, spread(): return lax.all_gather(slot_rows, 'tensor', axis=1, tiled=True)  257 us
    all_to_all x6, blocking collectives, send_rows(): lax.all_to_all(buffer, 'expert', split_axis=1, concat_axis=1, tiled=True)  139 us
    reduce_scatter x6, waiting for transfers between devices, collect(): lax.psum_scatter(partial_rows.astype(jnp.bfloat16), 'tensor', scatter_dim...  130 us
    psum x3, waiting for transfers between devices, body(): lax.psum(jnp.dot(layer_attended_low, output_w, preferred_element_type=jnp...  121 us
    psum x1, blocking collectives, body(): lax.psum(totals[0].astype(jnp.bfloat16), 'expert').astype(jnp.float32)  75.5 us
    all_to_all x6, waiting for transfers between devices, return_rows(): lax.all_to_all(buffer, 'expert', split_axis=1, concat_axis=1, tiled=True)  47.6 us
    all_gather x3, blocking collectives, layer_backward(): lax.all_gather(router_term[None].astype(jnp.bfloat16), 'tensor', axis=0,...  46.2 us
    all_to_all x6, starting transfers between devices, return_rows(): lax.all_to_all(buffer, 'expert', split_axis=1, concat_axis=1, tiled=True)  42.4 us
  transfers between devices with their start and end apart: 28, of which 21 were waited for; matrix products, arithmetic and copies ran while one was open for 19% of the time, Pallas kernels for 0%

commit v1 on v0

v1 whole, which is shorter than its diff:
```python
import functools
import math

import jax
import jax.numpy as jnp
from jax import lax
from jax.experimental import pallas as pl
from jax.experimental.pallas import tpu as pltpu
from jax.sharding import PartitionSpec as P

RING = 4
BF16 = jnp.bfloat16
F32 = jnp.float32


def wrap(value):
    return lax.rem(value + 2 * RING, RING)


class Place:
    def __init__(self):
        self.section = lax.axis_index("section")
        expert = lax.axis_index("expert")
        self.x = lax.axis_index("tensor")
        self.z = lax.div(expert, RING)
        self.y = lax.rem(expert, RING)

    def index(self, axis):
        return getattr(self, axis)

    def device(self, axis, delta):
        at = {"x": self.x, "y": self.y, "z": self.z}
        at[axis] = wrap(at[axis] + delta)
        return (self.section, at["z"] * RING + at["y"], at["x"])

    def peer(self):
        return (1 - self.section, self.z * RING + self.y, self.x)


def meet(devices):
    barrier = pltpu.get_barrier_semaphore()
    for device in devices:
        pl.semaphore_signal(barrier, inc=1, device_id=device, device_id_type=pl.DeviceIdType.MESH)
    pl.semaphore_wait(barrier, len(devices))


class Sender:
    def __init__(self, send_sems, recv_sems):
        self.send_sems, self.recv_sems = send_sems, recv_sems
        self.used = 0
        self.started = []

    def send(self, source, target, device):
        copy = pltpu.make_async_remote_copy(
            src_ref=source,
            dst_ref=target,
            send_sem=self.send_sems.at[self.used],
            recv_sem=self.recv_sems.at[self.used],
            device_id=device,
            device_id_type=pl.DeviceIdType.MESH,
        )
        self.used += 1
        copy.start()
        self.started.append(copy)
        return copy

    def send_either(self, flag, source, otherwise, target, device):
        first, second = [
            pltpu.make_async_remote_copy(
                src_ref=origin,
                dst_ref=target,
                send_sem=self.send_sems.at[self.used],
                recv_sem=self.recv_sems.at[self.used],
                device_id=device,
                device_id_type=pl.DeviceIdType.MESH,
            )
            for origin in (source, otherwise)
        ]
        self.used += 1
        pl.when(flag)(first.start)
        pl.when(jnp.logical_not(flag))(second.start)
        self.started.append(first)
        return first

    def finish(self):
        for copy in self.started:
            copy.wait_send()


def cut(width, count):
    tiles = width // 128
    edges = [tiles * i // count for i in range(count + 1)]
    return [(128 * a, 128 * (b - a)) for a, b in zip(edges[:-1], edges[1:])]


def region(place, order, phase, at, columns):
    spot = {}
    for i, axis in enumerate(order):
        spot[axis] = slice(None) if i < phase else (at if i == phase else place.index(axis))
    return (*[spot[axis] for axis in "zyx" if axis in spot], slice(None), pl.ds(*columns))


SENDS = 3 * (3 + 3 + 6)


def halves(columns):
    left, right = cut(columns[1], 2)
    return (columns[0] + left[0], left[1]), (columns[0] + right[0], right[1])


def thirds(buffer):
    return [(buffer, order, columns) for order, columns in zip(("xyz", "yzx", "zxy"), cut(buffer.shape[-1], 3))]


def gather(place, sender, plans, own=None, settle=None, beside=()):
    last_phase = len(plans[0][1]) - 1
    for phase in range(last_phase + 1):
        waits = []
        for buffer, order, columns in plans:
            axis = order[phase]
            me = place.index(axis)

            def push(delta, piece):
                here = buffer.at[region(place, order, phase, me, piece)]
                source = own.at[:, pl.ds(*piece)] if own is not None and phase == 0 else here
                return sender.send(source, here, place.device(axis, delta))

            if phase == last_phase:
                left, right = halves(columns)
                onward = (push(1, left), push(-1, right))
                waits += [push(1, right), push(-1, left)]
                waits.append((onward, buffer, order, axis, me, left, right))
            else:
                waits += [push(1, columns), push(-1, columns), push(2, columns)]
        if phase < len(beside):
            beside[phase]()
        last = []
        for wait in waits:
            if isinstance(wait, tuple):
                (up, down), buffer, order, axis, me, left, right = wait
                up.wait_recv()
                passing = buffer.at[region(place, order, phase, wrap(me - 1), left)]
                last.append(sender.send(passing, passing, place.device(axis, 1)))
                down.wait_recv()
                passing = buffer.at[region(place, order, phase, wrap(me + 1), right)]
                last.append(sender.send(passing, passing, place.device(axis, -1)))
            else:
                last.append(wait)
        for copy in last:
            copy.wait_recv()
        if phase == 0 and settle is not None:
            settle()


def neighbours(place, axes="xyz"):
    return [place.device(axis, delta) for axis in axes for delta in (1, -1, 2)]


def reduce(place, sender, plans, slots, beside=()):
    last_phase = len(plans[0][1]) - 1
    for turn_number, phase in enumerate(range(last_phase, -1, -1)):
        waits = []
        for (buffer, order, columns), slot in zip(plans, slots):
            axis, slot = order[phase], slot[phase]
            me = place.index(axis)

            def push(delta, at, piece, target, buffer=buffer, order=order, axis=axis, me=me):
                source = buffer.at[region(place, order, phase, wrap(me + at), piece)]
                return sender.send(source, target, place.device(axis, delta))

            if phase == last_phase:
                left, right = halves(columns)
                up, down = push(1, 2, left, slot[0]), push(-1, 2, right, slot[1])
                near = push(1, 1, right, slot[2]), push(-1, -1, left, slot[3])
                waits.append((push, up, down, near))
            else:
                waits.append([push(delta, delta, columns, slot[i]) for i, delta in enumerate((1, -1, 2))])
        if turn_number < len(beside):
            beside[turn_number]()
        if phase == last_phase:
            later = []
            for (buffer, order, columns), slot, (push, up, down, near) in zip(plans, slots, waits):
                slot = slot[phase]
                me = place.index(order[phase])
                left, right = halves(columns)
                up.wait_recv()
                add_into(buffer, region(place, order, phase, wrap(me + 1), left), slot[0])
                on_up = push(1, 1, left, slot[4])
                down.wait_recv()
                add_into(buffer, region(place, order, phase, wrap(me - 1), right), slot[1])
                on_down = push(-1, -1, right, slot[5])
                later.append((*near, on_up, on_down))
            for (buffer, order, columns), slot, copies in zip(plans, slots, later):
                slot = slot[phase]
                me = place.index(order[phase])
                left, right = halves(columns)
                for copy in copies:
                    copy.wait_recv()
                add_into(buffer, region(place, order, phase, me, left), slot[3], slot[4])
                add_into(buffer, region(place, order, phase, me, right), slot[2], slot[5])
        else:
            for (buffer, order, columns), slot, copies in zip(plans, slots, waits):
                for copy in copies:
                    copy.wait_recv()
                add_into(buffer, region(place, order, phase, place.index(order[phase]), columns), *slot[phase])


def slot_scratch(plans):
    scratch = []
    for rows, axes, columns in plans:
        left, right = halves(columns)
        for phase in range(axes):
            widths = (left, right, right, left, left, right) if phase == axes - 1 else (columns,) * 3
            scratch += [pltpu.VMEM((RING,) * phase + (rows, width), BF16) for _, width in widths]
    return scratch


def third_slots(rows, columns):
    return slot_scratch([(rows, 3, piece) for piece in cut(columns, 3)])


def sort_slots(refs, plans, axes):
    refs = list(refs)
    counts = [6 if phase == axes - 1 else 3 for phase in range(axes)]
    return [[[refs.pop(0) for _ in range(count)] for count in counts] for _ in range(plans)]


def add_into(buffer, at, *terms):
    *spots, rows, columns = at
    free = [i for i, spot in enumerate(spots) if isinstance(spot, slice)]

    def one(n, _):
        spot = list(spots)
        picks = []
        for i in reversed(free):
            spot[i] = lax.rem(n, RING)
            picks.insert(0, spot[i])
            n = lax.div(n, RING)
        here = (*spot, rows, columns)
        total = buffer[here].astype(F32)
        for term in terms:
            total = total + term[(*picks, slice(None), slice(None))].astype(F32)
        buffer[here] = total.astype(BF16)
        return 0

    if free:
        lax.fori_loop(0, RING ** len(free), one, 0)
    else:
        one(0, 0)


EPS = 1e-06
THETA = 1000000.0
MASKED = -1e30
GATED = 128
VMEM_LIMIT = 56 << 20


def params(number):
    return pltpu.CompilerParams(collective_id=number, has_side_effects=True, vmem_limit_bytes=VMEM_LIMIT)


IN_VMEM = pl.BlockSpec(memory_space=pltpu.VMEM)
ANYWHERE = pl.BlockSpec(memory_space=pl.ANY)


def copy_sems(count):
    return [pltpu.SemaphoreType.DMA((count,)), pltpu.SemaphoreType.DMA((count,))]


def dot_nn(left, right):
    return lax.dot_general(left, right, (((1,), (0,)), ((), ())), preferred_element_type=F32)


def dot_nt(left, right):
    return lax.dot_general(left, right, (((1,), (1,)), ((), ())), preferred_element_type=F32)


def dot_tn(left, right):
    return lax.dot_general(left, right, (((0,), (0,)), ((), ())), preferred_element_type=F32)


def inverse_rms(rows):
    return lax.rsqrt(jnp.mean(rows * rows, axis=-1, keepdims=True) + EPS)


def rms_back(rows, gain, grad):
    scale = inverse_rms(rows)
    unit = rows * scale
    lifted = grad * gain
    return scale * (lifted - unit * jnp.mean(lifted * unit, axis=-1, keepdims=True)), grad * unit


def scatter_x(place, sender, part, slots):
    copies = [
        sender.send(part.at[wrap(place.x + delta)], slots.at[i], place.device("x", delta))
        for i, delta in enumerate((1, -1, 2))
    ]
    for copy in copies:
        copy.wait_recv()
    total = part[place.x].astype(F32)
    for i in range(3):
        total = total + slots[i].astype(F32)
    return total


def gather_x(place, sender, whole):
    mine = whole.at[place.x]
    copies = [sender.send(mine, mine, place.device("x", delta)) for delta in (1, -1, 2)]
    for copy in copies:
        copy.wait_recv()


def mix_kernel(layer, part, resid, pack0, pack1, routes0, routes1, mid, gates, rows_all, own, slots, send, recv, local):
    place = Place()
    meet(neighbours(place))
    sender = Sender(send, recv)
    chosen = of_layer(layer, routes0[place.x], routes1[place.x])
    lanes = lax.broadcasted_iota(jnp.int32, gates.shape, 1)
    named = chosen[:, 0:1] == lanes
    for i in range(1, chosen.shape[1]):
        named = named | (chosen[:, i : i + 1] == lanes)
    gain = of_layer(layer, pack0[PACK_ROUTER + 1 : PACK_ROUTER + 2], pack1[PACK_ROUTER + 1 : PACK_ROUTER + 2])
    router = of_layer(layer, pack0[:PACK_ROUTER], pack1[:PACK_ROUTER])
    total = scatter_x(place, sender, part, slots)
    mid_rows = resid[place.x].astype(F32) + total
    mid[...] = mid_rows
    moe_in = (mid_rows * inverse_rms(mid_rows) * gain.astype(F32)).astype(BF16)
    logits = jnp.where(named, dot_nt(moe_in, router), MASKED)
    raised = jnp.where(named, jnp.exp(logits - jnp.max(logits, axis=-1, keepdims=True)), 0.0)
    weights = raised / jnp.sum(raised, axis=-1, keepdims=True)
    gates[...] = weights
    own[:, : moe_in.shape[1]] = moe_in
    own[:, moe_in.shape[1] :] = weights.astype(BF16)
    keep = pltpu.make_async_copy(own, rows_all.at[place.z, place.y, place.x], local)
    keep.start()
    gather(place, sender, thirds(rows_all), own, keep.wait)
    sender.finish()


def mix(layer, part, resid, packs, routes):
    _, rows, width = part.shape
    return pl.pallas_call(
        functools.partial(mix_kernel, layer),
        name="mix",
        out_shape=(
            jax.ShapeDtypeStruct((rows, width), F32),
            jax.ShapeDtypeStruct((rows, GATED), F32),
            jax.ShapeDtypeStruct((RING, RING, RING, rows, width + GATED), BF16),
        ),
        in_specs=[IN_VMEM] * 6,
        out_specs=(IN_VMEM, IN_VMEM, ANYWHERE),
        scratch_shapes=[
            pltpu.VMEM((rows, width + GATED), BF16),
            pltpu.VMEM((3, rows, width), BF16),
            *copy_sems(3 + SENDS),
            pltpu.SemaphoreType.DMA,
        ],
        compiler_params=params(1 + layer),
    )(part, resid, *packs, *routes)


def settle_kernel(partial, mid, out, buffer, send, recv, local, *slots):
    place = Place()
    load = pltpu.make_async_copy(partial, buffer, local)
    load.start()
    meet(neighbours(place))
    sender = Sender(send, recv)
    load.wait()
    reduce(place, sender, thirds(buffer), sort_slots(slots, 3, 3))
    moe_rows = buffer[place.z, place.y, place.x].astype(F32)
    out[place.x] = (mid[...] + moe_rows).astype(BF16)
    gather_x(place, sender, out)
    sender.finish()


def settle_layer(partial, mid):
    rows, width = partial.shape[-2:]
    return pl.pallas_call(
        settle_kernel,
        name="settle",
        out_shape=jax.ShapeDtypeStruct((RING, rows, width), BF16),
        in_specs=[ANYWHERE, IN_VMEM],
        out_specs=IN_VMEM,
        scratch_shapes=[
            pltpu.VMEM(partial.shape, BF16),
            *copy_sems(3 + SENDS),
            pltpu.SemaphoreType.DMA,
            *third_slots(rows, width),
        ],
        compiler_params=params(3),
    )(partial, mid)


def share_kernel(rows_in, rows_all, send, recv, local):
    place = Place()
    meet(neighbours(place))
    sender = Sender(send, recv)
    own = rows_in.at[place.x]
    keep = pltpu.make_async_copy(own, rows_all.at[place.z, place.y, place.x], local)
    keep.start()
    gather(place, sender, thirds(rows_all), own, keep.wait)
    sender.finish()


def share_rows(rows_in):
    _, rows, width = rows_in.shape
    return pl.pallas_call(
        share_kernel,
        name="share",
        out_shape=jax.ShapeDtypeStruct((RING, RING, RING, rows, width), BF16),
        in_specs=[IN_VMEM],
        out_specs=ANYWHERE,
        scratch_shapes=[*copy_sems(SENDS), pltpu.SemaphoreType.DMA],
        compiler_params=params(4),
    )(rows_in)


def moe_back_kernel(layer, partial, mid, gates, pack0, pack1, d_part, gain_term, router_term, buffer, send, recv, local, *slots):
    place = Place()
    load = pltpu.make_async_copy(partial, buffer, local)
    load.start()
    meet(neighbours(place))
    sender = Sender(send, recv)
    gain = of_layer(layer, pack0[PACK_ROUTER + 1 : PACK_ROUTER + 2], pack1[PACK_ROUTER + 1 : PACK_ROUTER + 2]).astype(F32)
    router = of_layer(layer, pack0[:PACK_ROUTER], pack1[:PACK_ROUTER])
    load.wait()
    reduce(place, sender, thirds(buffer), sort_slots(slots, 3, 3))
    width = mid.shape[1]
    sums = buffer[place.z, place.y, place.x].astype(F32)
    weights = gates[...]
    d_gates = sums[:, width:]
    d_logits = (weights * (d_gates - jnp.sum(d_gates * weights, axis=-1, keepdims=True))).astype(BF16)
    d_moe_in = sums[:, :width] + dot_nn(d_logits, router)
    mid_rows = mid[...]
    d_mid, terms = rms_back(mid_rows, gain, d_moe_in)
    d_part[place.x] = d_mid.astype(BF16)
    gather_x(place, sender, d_part)
    gain_term[...] = jnp.sum(terms, axis=0, keepdims=True)
    moe_in = (mid_rows * inverse_rms(mid_rows) * gain).astype(BF16)
    router_term[...] = dot_tn(d_logits, moe_in)[: router_term.shape[0]]
    sender.finish()


def moe_back(layer, partial, mid, gates, packs, expert_count):
    rows, width = mid.shape
    return pl.pallas_call(
        functools.partial(moe_back_kernel, layer),
        name="moe_back",
        out_shape=(
            jax.ShapeDtypeStruct((RING, rows, width), BF16),
            jax.ShapeDtypeStruct((1, width), F32),
            jax.ShapeDtypeStruct((expert_count, width), F32),
        ),
        in_specs=[ANYWHERE] + [IN_VMEM] * 4,
        out_specs=(IN_VMEM,) * 3,
        scratch_shapes=[
            pltpu.VMEM(partial.shape, BF16),
            *copy_sems(3 + SENDS),
            pltpu.SemaphoreType.DMA,
            *third_slots(rows, width + GATED),
        ],
        compiler_params=params(5 + layer),
    )(partial, mid, gates, *packs)


def attn_back_kernel(layer, part, resid, pack0, pack1, d_mid, d_input, gain_term, own, slots, send, recv, local):
    place = Place()
    last = layer == 0
    meet(neighbours(place, "x" if last else "xyz"))
    sender = Sender(send, recv)
    total = scatter_x(place, sender, part, slots)
    gain = of_layer(layer, pack0[PACK_ROUTER : PACK_ROUTER + 1], pack1[PACK_ROUTER : PACK_ROUTER + 1]).astype(F32)
    d_resid, terms = rms_back(resid[place.x].astype(F32), gain, total)
    gain_term[...] = jnp.sum(terms, axis=0, keepdims=True)
    d_rows = (d_mid[place.x].astype(F32) + d_resid).astype(BF16)
    if last:
        d_input[place.x] = d_rows
        gather_x(place, sender, d_input)
    else:
        own[...] = d_rows
        keep = pltpu.make_async_copy(own, d_input.at[place.z, place.y, place.x], local)
        keep.start()
        gather(place, sender, thirds(d_input), own, keep.wait)
    sender.finish()


def attn_back_rows(layer, part, resid, packs, d_mid):
    _, rows, width = part.shape
    last = layer == 0
    out = (RING, rows, width) if last else (RING, RING, RING, rows, width)
    return pl.pallas_call(
        functools.partial(attn_back_kernel, layer),
        name="attn_back_last" if last else "attn_back",
        out_shape=(jax.ShapeDtypeStruct(out, BF16), jax.ShapeDtypeStruct((1, width), F32)),
        in_specs=[IN_VMEM] * 5,
        out_specs=(IN_VMEM if last else ANYWHERE, IN_VMEM),
        scratch_shapes=[
            pltpu.VMEM((rows, width), BF16),
            pltpu.VMEM((3, rows, width), BF16),
            *copy_sems(6 if last else 3 + SENDS),
            pltpu.SemaphoreType.DMA,
        ],
        compiler_params=params(7 + layer),
    )(part, resid, *packs, d_mid)


TILE = 256


def load_weights(layer, own, other, targets, sems):
    gate, up, down = targets
    half = gate.shape[0] // 2
    section = lax.axis_index("section")

    def pairs(source):
        return [
            (source[0].at[0], gate.at[pl.ds(0, half)]),
            (source[0].at[1], gate.at[pl.ds(half, half)]),
            (source[1].at[0], up.at[pl.ds(0, half)]),
            (source[1].at[1], up.at[pl.ds(half, half)]),
            (source[2].at[0], down.at[pl.ds(0, half)]),
            (source[2].at[1], down.at[pl.ds(half, half)]),
        ]

    @pl.when(section == layer)
    def _():
        for i, (source, target) in enumerate(pairs(own)):
            pltpu.make_async_copy(source, target, sems.at[i]).start()

    @pl.when(section != layer)
    def _():
        for i, (source, target) in enumerate(pairs(other)):
            pltpu.make_async_copy(source, target, sems.at[i]).start()

    return [pltpu.make_async_copy(source, target, sems.at[i]) for i, (source, target) in enumerate(pairs(own))]


def gate_columns(table, half):
    first = 2 * lax.axis_index("expert")
    lanes = lax.broadcasted_iota(jnp.int32, table.shape, 1)
    table = table.astype(F32)
    one = jnp.sum(jnp.where(lanes == first, table, 0.0), axis=1, keepdims=True)
    two = jnp.sum(jnp.where(lanes == first + 1, table, 0.0), axis=1, keepdims=True)
    units = lax.broadcasted_iota(jnp.int32, (table.shape[0], 2 * half), 1)
    return jnp.where(units < half, one, two)


def expert_kernel(layer, rows, own0, own1, own2, other0, other1, other2, out, acts, gate, up, down, sems):
    width = out.shape[1]
    step = pl.program_id(0)

    @pl.when(step == 0)
    def _():
        for copy in load_weights(layer, (own0, own1, own2), (other0, other1, other2), (gate, up, down), sems):
            copy.wait()

    moe_in = rows[:, :width]
    gate_act = dot_nt(moe_in, gate[...])
    up_act = dot_nt(moe_in, up[...])
    units = gate_act.shape[1]
    acts[:, :units] = gate_act.astype(BF16)
    acts[:, units:] = up_act.astype(BF16)
    hidden = gate_act / (1.0 + jnp.exp(-gate_act)) * up_act
    hidden = hidden * gate_columns(rows[:, width:], units // 2)
    out[...] = dot_nn(hidden.astype(BF16), down[...]).astype(BF16)


def experts(layer, rows_all, own, other):
    count = RING**3 * rows_all.shape[3]
    width = rows_all.shape[4] - GATED
    units = 2 * own[0].shape[1]
    rows = rows_all.reshape(count, width + GATED)
    out, acts = pl.pallas_call(
        functools.partial(expert_kernel, layer),
        name="experts",
        grid=(count // TILE,),
        out_shape=(
            jax.ShapeDtypeStruct((count, width), BF16),
            jax.ShapeDtypeStruct((count, 2 * units), BF16),
        ),
        in_specs=[pl.BlockSpec((TILE, width + GATED), lambda i: (i, 0))] + [ANYWHERE] * 6,
        out_specs=(
            pl.BlockSpec((TILE, width), lambda i: (i, 0)),
            pl.BlockSpec((TILE, 2 * units), lambda i: (i, 0)),
        ),
        scratch_shapes=[pltpu.VMEM((units, width), BF16)] * 3 + [pltpu.SemaphoreType.DMA((6,))],
        compiler_params=pltpu.CompilerParams(vmem_limit_bytes=VMEM_LIMIT),
    )(rows, *own, *other)
    return out.reshape(*rows_all.shape[:4], width), acts


def expert_back_kernel(
    layer, rows, grads, acts, own0, own1, own2, other0, other1, other2, out, grad_in, grad_down,
    gate, up, down, sum_in, sum_down, sems
):
    width = grads.shape[1]
    units = acts.shape[1] // 2
    step = pl.program_id(0)

    @pl.when(step == 0)
    def _():
        copies = load_weights(layer, (own0, own1, own2), (other0, other1, other2), (gate, up, down), sems)
        sum_in[...] = jnp.zeros_like(sum_in)
        sum_down[...] = jnp.zeros_like(sum_down)
        for copy in copies:
            copy.wait()

    grad = grads[...]
    weights = gate_columns(rows[:, width:], units // 2)
    back = dot_nt(grad, down[...])
    gate_act = acts[:, :units].astype(F32)
    up_act = acts[:, units:].astype(F32)
    sigmoid = 1.0 / (1.0 + jnp.exp(-gate_act))
    silu = gate_act * sigmoid
    hidden = silu * up_act
    products = hidden * back
    first = 2 * lax.axis_index("expert")
    in_one = lax.broadcasted_iota(jnp.int32, products.shape, 1) < units // 2
    one = jnp.sum(jnp.where(in_one, products, 0.0), axis=1, keepdims=True)
    two = jnp.sum(jnp.where(in_one, 0.0, products), axis=1, keepdims=True)
    lanes = lax.broadcasted_iota(jnp.int32, (products.shape[0], GATED), 1)
    d_gates = jnp.where(lanes == first, one, jnp.where(lanes == first + 1, two, 0.0))
    d_hidden = back * weights
    d_gate = (d_hidden * up_act * sigmoid * (1.0 + gate_act * (1.0 - sigmoid))).astype(BF16)
    d_up = (d_hidden * silu).astype(BF16)
    out[:, :width] = (dot_nn(d_gate, gate[...]) + dot_nn(d_up, up[...])).astype(BF16)
    out[:, width:] = d_gates.astype(BF16)
    moe_in = rows[:, :width]
    sum_in[:units] += dot_tn(d_gate, moe_in)
    sum_in[units:] += dot_tn(d_up, moe_in)
    sum_down[...] += dot_tn((hidden * weights).astype(BF16), grad)

    @pl.when(step == pl.num_programs(0) - 1)
    def _():
        grad_in[...] = sum_in[...].astype(BF16)
        grad_down[...] = sum_down[...].astype(BF16)


def experts_back(layer, rows_all, grads_all, acts, own, other):
    count = RING**3 * rows_all.shape[3]
    width = rows_all.shape[4] - GATED
    units = 2 * own[0].shape[1]
    out, grad_in, grad_down = pl.pallas_call(
        functools.partial(expert_back_kernel, layer),
        name="experts_back",
        grid=(count // TILE,),
        out_shape=(
            jax.ShapeDtypeStruct((count, width + GATED), BF16),
            jax.ShapeDtypeStruct((2 * units, width), BF16),
            jax.ShapeDtypeStruct((units, width), BF16),
        ),
        in_specs=[
            pl.BlockSpec((TILE, width + GATED), lambda i: (i, 0)),
            pl.BlockSpec((TILE, width), lambda i: (i, 0)),
            pl.BlockSpec((TILE, 2 * units), lambda i: (i, 0)),
        ]
        + [ANYWHERE] * 6,
        out_specs=(
            pl.BlockSpec((TILE, width + GATED), lambda i: (i, 0)),
            pl.BlockSpec((2 * units, width), lambda i: (0, 0)),
            pl.BlockSpec((units, width), lambda i: (0, 0)),
        ),
        scratch_shapes=[pltpu.VMEM((units, width), BF16)] * 3
        + [pltpu.VMEM((2 * units, width), F32), pltpu.VMEM((units, width), F32), pltpu.SemaphoreType.DMA((6,))],
        compiler_params=pltpu.CompilerParams(vmem_limit_bytes=VMEM_LIMIT),
    )(rows_all.reshape(count, width + GATED), grads_all.reshape(count, width), acts, *own, *other)
    return out.reshape(*rows_all.shape), grad_in, grad_down


def pull(layer, own, other, targets, sems):
    section = lax.axis_index("section")

    @pl.when(section == layer)
    def _():
        for i, (source, target) in enumerate(zip(own, targets)):
            pltpu.make_async_copy(source, target, sems.at[i]).start()

    @pl.when(section != layer)
    def _():
        for i, (source, target) in enumerate(zip(other, targets)):
            pltpu.make_async_copy(source, target, sems.at[i]).start()

    return [pltpu.make_async_copy(source, target, sems.at[i]) for i, (source, target) in enumerate(zip(own, targets))]


def of_layer(layer, own, other):
    return jnp.where(lax.axis_index("section") == layer, own, other)


def tables(seg_column, seg_row, dim):
    rows = seg_column.shape[0]
    at_row = lax.broadcasted_iota(jnp.int32, (rows, rows), 0)
    at_column = lax.broadcasted_iota(jnp.int32, (rows, rows), 1)
    earlier = jnp.sum((seg_row < seg_column).astype(F32), axis=1, keepdims=True)
    position = lax.broadcasted_iota(jnp.int32, (rows, dim), 0).astype(F32) - earlier
    lane = lax.broadcasted_iota(jnp.int32, (rows, dim), 1)
    half = dim // 2
    place = jnp.where(lane < half, lane, lane - half).astype(F32)
    angle = position * jnp.exp(place * (-math.log(THETA) / half))
    sine = jnp.sin(angle)
    return jnp.cos(angle), jnp.where(lane < half, -sine, sine), (seg_row == seg_column) & (at_column <= at_row)


def turn(rows, cosine, sine):
    return rows * cosine + pltpu.roll(rows, rows.shape[1] // 2, 1) * sine


def turn_back(grad, cosine, sine):
    return grad * cosine + pltpu.roll(grad * sine, grad.shape[1] // 2, 1)


PACK_ROUTER = 128
PACK_ROWS = 144
HEADS_STEP = 2


def attention_kernel(
    layer, rows, seg_column, seg_row, pack0, pack1, q0, k0, v0, o0, q1, k1, v1, o1,
    part, attended, query_raw, key_raw, value_low, wq, wk, wv, wo, total, sems
):
    dim = wk.shape[1]
    heads = wq.shape[1] // dim
    step = HEADS_STEP * dim
    steps = heads // HEADS_STEP

    def pieces(q, k, v, o):
        columns = [q.at[:, pl.ds(i * step, step)] for i in range(steps)]
        return [k, v, *columns, *[o.at[pl.ds(i * step, step)] for i in range(steps)]]

    loads = pull(layer, pieces(q0, k0, v0, o0), pieces(q1, k1, v1, o1), pieces(wq, wk, wv, wo), sems)
    resid = rows[...].astype(F32)
    gain = of_layer(layer, pack0[PACK_ROUTER : PACK_ROUTER + 1], pack1[PACK_ROUTER : PACK_ROUTER + 1]).astype(F32)
    gains = of_layer(layer, pack0[PACK_ROUTER + 2 : PACK_ROUTER + 3], pack1[PACK_ROUTER + 2 : PACK_ROUTER + 3]).astype(F32)
    gain_query, gain_key = gains[:, :dim], gains[:, dim : 2 * dim]
    cosine, sine, allowed = tables(seg_column[...], seg_row[...], dim)
    normed = (resid * inverse_rms(resid) * gain).astype(BF16)
    loads[0].wait()
    raw = dot_nn(normed, wk[...])
    key_raw[...] = raw
    key = turn(raw * inverse_rms(raw) * gain_key, cosine, sine).astype(BF16)
    loads[1].wait()
    value = dot_nn(normed, wv[...]).astype(BF16)
    value_low[...] = value
    for i in range(steps):
        loads[2 + i].wait()
        raws = dot_nn(normed, wq[:, i * step : (i + 1) * step])
        query_raw[:, i * step : (i + 1) * step] = raws
        for h in range(HEADS_STEP):
            raw = raws[:, h * dim : (h + 1) * dim]
            query = turn(raw * inverse_rms(raw) * gain_query, cosine, sine).astype(BF16)
            scores = jnp.where(allowed, dot_nt(query, key) * (1.0 / math.sqrt(dim)), MASKED)
            raised = jnp.exp(scores - jnp.max(scores, axis=1, keepdims=True))
            probs = (raised / jnp.sum(raised, axis=1, keepdims=True)).astype(BF16)
            at = i * step + h * dim
            attended[:, at : at + dim] = dot_nn(probs, value).astype(BF16)
        loads[2 + steps + i].wait()
        piece = dot_nn(attended[:, i * step : (i + 1) * step], wo[i * step : (i + 1) * step])
        if i == 0:
            total[...] = piece
        else:
            total[...] += piece
    quarter = part.shape[1]
    for i in range(part.shape[0]):
        part[i] = total[i * quarter : (i + 1) * quarter].astype(BF16)


def weight_scratch(dense):
    return [pltpu.VMEM(w.shape, BF16) for w in dense]


def attention(layer, rows, segs, packs, own, other):
    count, width = rows.shape
    dim, inner = own[1].shape[1], own[0].shape[1]
    return pl.pallas_call(
        functools.partial(attention_kernel, layer),
        name="attention",
        out_shape=(
            jax.ShapeDtypeStruct((RING, count // RING, width), BF16),
            jax.ShapeDtypeStruct((count, inner), BF16),
            jax.ShapeDtypeStruct((count, inner), F32),
            jax.ShapeDtypeStruct((count, dim), F32),
            jax.ShapeDtypeStruct((count, dim), BF16),
        ),
        in_specs=[IN_VMEM] * 5 + [ANYWHERE] * 8,
        out_specs=(IN_VMEM,) * 5,
        scratch_shapes=[
            *weight_scratch(own),
            pltpu.VMEM((count, width), F32),
            pltpu.SemaphoreType.DMA((2 + 2 * (inner // dim // HEADS_STEP),)),
        ],
        compiler_params=pltpu.CompilerParams(vmem_limit_bytes=VMEM_LIMIT),
    )(rows, *segs, *packs, *own, *other)


def attention_back_kernel(
    layer, rows, seg_column, seg_row, pack0, pack1, attended, query_raw, key_raw, value_low, upstream, d_part,
    q0, k0, v0, o0, q1, k1, v1, o1,
    part, d_mid, normed_out, d_proj, d_mid_low, gain_terms, wq, wk, wv, wo, total, d_heads, sems
):
    dim = wk.shape[1]
    heads = wq.shape[1] // dim
    inner = heads * dim
    step = HEADS_STEP * dim
    steps = heads // HEADS_STEP
    quarter = d_part.shape[1]

    def pieces(q, k, v, o):
        return [*[o.at[pl.ds(i * step, step)] for i in range(steps)],
                *[q.at[:, pl.ds(i * step, step)] for i in range(steps)], k, v]

    loads = pull(layer, pieces(q0, k0, v0, o0), pieces(q1, k1, v1, o1), pieces(wq, wk, wv, wo), sems)
    for i in range(RING):
        grad = upstream[i].astype(F32) + d_part[i].astype(F32)
        d_mid[i] = grad
        total[i * quarter : (i + 1) * quarter] = grad
    grad_low = total[...].astype(BF16)
    d_mid_low[...] = grad_low
    resid = rows[...].astype(F32)
    gain = of_layer(layer, pack0[PACK_ROUTER : PACK_ROUTER + 1], pack1[PACK_ROUTER : PACK_ROUTER + 1]).astype(F32)
    gains = of_layer(layer, pack0[PACK_ROUTER + 2 : PACK_ROUTER + 3], pack1[PACK_ROUTER + 2 : PACK_ROUTER + 3]).astype(F32)
    gain_query, gain_key = gains[:, :dim], gains[:, dim : 2 * dim]
    cosine, sine, allowed = tables(seg_column[...], seg_row[...], dim)
    normed_out[...] = (resid * inverse_rms(resid) * gain).astype(BF16)
    raw_key = key_raw[...]
    key = turn(raw_key * inverse_rms(raw_key) * gain_key, cosine, sine).astype(BF16)
    value = value_low[...]
    scale = 1.0 / math.sqrt(dim)
    d_key = jnp.zeros(key.shape, F32)
    d_value = jnp.zeros(key.shape, F32)
    gain_total = jnp.zeros(gain_query.shape, F32)
    for i in range(steps):
        loads[i].wait()
        d_heads[...] = dot_nt(grad_low, wo[i * step : (i + 1) * step]).astype(BF16)
        for h in range(HEADS_STEP):
            at = i * step + h * dim
            raw = query_raw[:, at : at + dim]
            query = turn(raw * inverse_rms(raw) * gain_query, cosine, sine).astype(BF16)
            scores = jnp.where(allowed, dot_nt(query, key) * scale, MASKED)
            raised = jnp.exp(scores - jnp.max(scores, axis=1, keepdims=True))
            probs = raised / jnp.sum(raised, axis=1, keepdims=True)
            d_head = d_heads[:, h * dim : (h + 1) * dim]
            d_probs = dot_nt(d_head, value)
            d_value = d_value + dot_tn(probs.astype(BF16), d_head)
            d_scores = (probs * (d_probs - jnp.sum(d_probs * probs, axis=1, keepdims=True))).astype(BF16)
            d_query = turn_back(dot_nn(d_scores, key) * scale, cosine, sine)
            d_key = d_key + dot_tn(d_scores, query) * scale
            d_raw, terms = rms_back(raw, gain_query, d_query)
            gain_total = gain_total + jnp.sum(terms, axis=0, keepdims=True)
            d_proj[:, at : at + dim] = d_raw.astype(BF16)
        loads[steps + i].wait()
        piece = dot_nt(d_proj[:, i * step : (i + 1) * step], wq[:, i * step : (i + 1) * step])
        if i == 0:
            total[...] = piece
        else:
            total[...] += piece
    d_raw, terms = rms_back(raw_key, gain_key, turn_back(d_key, cosine, sine))
    d_proj[:, inner : inner + dim] = d_raw.astype(BF16)
    d_proj[:, inner + dim :] = d_value.astype(BF16)
    gain_terms[...] = jnp.zeros(gain_terms.shape, F32)
    gain_terms[:, :dim] = gain_total
    gain_terms[:, dim : 2 * dim] = jnp.sum(terms, axis=0, keepdims=True)
    loads[2 * steps].wait()
    loads[2 * steps + 1].wait()
    total[...] += dot_nt(d_proj[:, inner : inner + dim], wk[...]) + dot_nt(d_proj[:, inner + dim :], wv[...])
    for i in range(RING):
        part[i] = total[i * quarter : (i + 1) * quarter].astype(BF16)


def attention_back(layer, rows, segs, packs, saved, upstream, d_part, own, other):
    count, width = rows.shape
    dim, inner = own[1].shape[1], own[0].shape[1]
    return pl.pallas_call(
        functools.partial(attention_back_kernel, layer),
        name="attention_back",
        out_shape=(
            jax.ShapeDtypeStruct(d_part.shape, BF16),
            jax.ShapeDtypeStruct(d_part.shape, F32),
            jax.ShapeDtypeStruct((count, width), BF16),
            jax.ShapeDtypeStruct((count, inner + 2 * dim), BF16),
            jax.ShapeDtypeStruct((count, width), BF16),
            jax.ShapeDtypeStruct((1, width), F32),
        ),
        in_specs=[IN_VMEM] * 11 + [ANYWHERE] * 8,
        out_specs=(IN_VMEM,) * 6,
        scratch_shapes=[
            *weight_scratch(own),
            pltpu.VMEM((count, width), F32),
            pltpu.VMEM((count, HEADS_STEP * dim), BF16),
            pltpu.SemaphoreType.DMA((2 + 2 * (inner // dim // HEADS_STEP),)),
        ],
        compiler_params=pltpu.CompilerParams(vmem_limit_bytes=VMEM_LIMIT),
    )(rows, *segs, *packs, *saved, upstream, d_part, *own, *other)


SMALL = 48


def finish_kernel(
    n0, p0, a0, m0, n1, p1, a1, m1, r0, g0, h0, q0, r1, g1, h1, q1, in0, down0, in1, down1, out0, out1, ig0, ig1,
    first, second, small_out, got_in, got_down, outputs, input_grads,
    first_sums, second_sums, normed, proj, heads, mids, mine, theirs, arrived, passing, small_slots, send, recv, local, *slots
):
    place = Place()
    lower = place.section == 0
    peer = place.peer()
    sender = Sender(send, recv)
    rows = n0.shape[0]

    def keep(index, flag, source, otherwise, target):
        one, two = (pltpu.make_async_copy(origin, target, local.at[index]) for origin in (source, otherwise))
        pl.when(flag)(one.start)
        pl.when(jnp.logical_not(flag))(two.start)
        return one

    pairs = ((n0, n1, normed), (p0, p1, proj), (a0, a1, heads), (m0, m1, mids))
    kept = [keep(i, lower, low, high, target.at[pl.ds(0, rows)]) for i, (low, high, target) in enumerate(pairs)]
    kept.append(keep(4, lower, out0, out1, outputs.at[place.section]))
    kept.append(keep(5, lower, ig0, ig1, input_grads.at[place.section]))
    for at, low, high in ((0, r0, r1), (32, g0, g1), (33, h0, h1), (34, q0, q1)):
        count = low.shape[0]
        mine[at : at + count] = jnp.where(lower, low[...], high[...])
        passing[at : at + count] = jnp.where(lower, high[...], low[...])
    empty = jnp.zeros((SMALL - 35, passing.shape[1]), F32)
    mine[35:] = empty
    passing[35:] = empty
    theirs[...] = passing[...].astype(BF16)
    meet([peer, *neighbours(place)])
    factors = [
        sender.send_either(lower, high, low, target.at[pl.ds(rows, rows)], peer) for low, high, target in pairs
    ]
    small_copy = sender.send(theirs, arrived, peer)
    late = [
        sender.send_either(lower, out1, out0, outputs.at[place.section], peer),
        sender.send_either(lower, ig1, ig0, input_grads.at[place.section], peer),
        sender.send_either(lower, in1, in0, got_in, peer),
        sender.send_either(lower, down1, down0, got_down, peer),
    ]
    for copy in kept:
        copy.wait()
    for copy in factors:
        copy.wait_recv()
    lanes = 128

    def output_blocks(i, _):
        pair = dot_tn(heads[:, pl.ds(pl.multiple_of(i * lanes, lanes), lanes)], mids[...]).astype(BF16)
        half = lanes // 2
        at = 2 * i
        second_sums[lax.div(at, RING), lax.rem(at, RING)] = pair[:half]
        second_sums[lax.div(at, RING), lax.rem(at, RING) + 1] = pair[half:]
        return 0

    def input_blocks(i, _):
        block = dot_tn(normed[:, pl.ds(pl.multiple_of(i * lanes, lanes), lanes)], proj[...])
        first_sums[lax.div(i, RING), lax.rem(i, RING)] = block.astype(BF16)
        return 0

    lax.fori_loop(0, heads.shape[1] // lanes, output_blocks, 0)
    lax.fori_loop(0, normed.shape[1] // lanes, input_blocks, 0)
    sums = [(first_sums, "yz", (0, first.shape[-1])), (second_sums, "zy", (0, second.shape[-1]))]
    plans = [(first, "yz", (0, first.shape[-1])), (second, "zy", (0, second.shape[-1]))]
    state = {}

    def exchange(step, total):
        passing[...] = total
        buffer = small_slots.at[step, 3]
        buffer[...] = total.astype(BF16)
        state["copies"] = [
            sender.send(buffer, small_slots.at[step, i], place.device("xyz"[step], delta))
            for i, delta in enumerate((1, -1, 2))
        ]

    def collect(step):
        for copy in state["copies"]:
            copy.wait_recv()
        total = passing[...]
        for i in range(3):
            total = total + small_slots[step, i].astype(F32)
        return total

    def small_last():
        small_out[...] = collect(2)

    small_copy.wait_recv()
    exchange(0, mine[...] + arrived[...].astype(F32))
    reduce(place, sender, sums, sort_slots(slots, 2, 2), (lambda: exchange(1, collect(0)), lambda: exchange(2, collect(1))))
    first[place.z, place.y] = first_sums[place.z, place.y]
    second[place.z, place.y] = second_sums[place.z, place.y]
    gather(place, sender, plans, None, None, (small_last,))
    for copy in late:
        copy.wait_recv()
    sender.finish()


def finish(factors, smalls, expert_grads, outs, input_grads):
    rows, width = factors[0][0].shape
    proj = factors[0][1].shape[1]
    inner = factors[0][2].shape[1]
    blocks = RING * RING
    first = (RING, RING, width // blocks, proj)
    second = (RING, RING, inner // blocks, width)
    both = (2, *outs[0].shape)
    return pl.pallas_call(
        finish_kernel,
        name="finish",
        out_shape=(
            jax.ShapeDtypeStruct(first, BF16),
            jax.ShapeDtypeStruct(second, BF16),
            jax.ShapeDtypeStruct((SMALL, width), F32),
            jax.ShapeDtypeStruct(expert_grads[0][0].shape, BF16),
            jax.ShapeDtypeStruct(expert_grads[0][1].shape, BF16),
            jax.ShapeDtypeStruct(both, BF16),
            jax.ShapeDtypeStruct(both, BF16),
        ),
        in_specs=[ANYWHERE] * 8 + [IN_VMEM] * 8 + [ANYWHERE] * 8,
        out_specs=(IN_VMEM,) * 3 + (ANYWHERE,) * 4,
        scratch_shapes=[
            pltpu.VMEM(first, BF16),
            pltpu.VMEM(second, BF16),
            pltpu.VMEM((2 * rows, width), BF16),
            pltpu.VMEM((2 * rows, proj), BF16),
            pltpu.VMEM((2 * rows, inner), BF16),
            pltpu.VMEM((2 * rows, width), BF16),
            pltpu.VMEM((SMALL, width), F32),
            pltpu.VMEM((SMALL, width), BF16),
            pltpu.VMEM((SMALL, width), BF16),
            pltpu.VMEM((SMALL, width), F32),
            pltpu.VMEM((3, 4, SMALL, width), BF16),
            *copy_sems(9 + 9 + 36),
            pltpu.SemaphoreType.DMA((6,)),
            *slot_scratch([(first[2], 2, (0, proj)), (second[2], 2, (0, width))]),
        ],
        compiler_params=params(9),
    )(*factors[0], *factors[1], *smalls[0], *smalls[1], *expert_grads[0], *expert_grads[1], *outs, *input_grads)


def swap(vector):
    return lax.ppermute(vector, "section", [(0, 1), (1, 0)])


def body(
    block_input,
    cotangent,
    segments,
    routes,
    norm_attn,
    w_query,
    key_matrix,
    value_matrix,
    norm_query,
    norm_key,
    w_output,
    norm_moe,
    w_router,
    w_gate,
    w_up,
    w_down,
):
    section = lax.axis_index("section")
    lower = section == 0
    _, group_rows, width = block_input.shape
    expert_count = w_router.shape[2]
    quarter = group_rows // RING
    dim = norm_query.shape[1]

    dense_own = (w_query[0], key_matrix[0], value_matrix[0], w_output[0])
    expert_own = (jnp.swapaxes(w_gate[0], 1, 2), jnp.swapaxes(w_up[0], 1, 2), w_down[0])
    pack_own = jnp.concatenate(
        [
            jnp.pad(w_router[0].T, ((0, PACK_ROUTER - expert_count), (0, 0))),
            norm_attn,
            norm_moe,
            jnp.pad(jnp.concatenate([norm_query, norm_key], axis=1), ((0, PACK_ROWS - PACK_ROUTER - 3), (0, width - 2 * dim))),
        ],
        axis=0,
    )
    routes_own = lax.dynamic_index_in_dim(routes[0], section, 0, keepdims=False)
    routes_other = swap(lax.dynamic_index_in_dim(routes[0], 1 - section, 0, keepdims=False))
    packs = (pack_own, swap(pack_own))
    dense_other = tuple(swap(w) for w in dense_own)
    expert_other = tuple(swap(w) for w in expert_own)
    chosen = tuple(r.reshape(RING, quarter, r.shape[-1]) for r in (routes_own, routes_other))

    def pick(array):
        return lax.dynamic_index_in_dim(array, section, 0, keepdims=False)

    def quarters(array):
        return array.reshape(RING, quarter, array.shape[-1])

    segment = pick(segments)
    segs = (segment.reshape(group_rows, 1), segment.reshape(1, group_rows))

    rows_in = pick(block_input)
    upstream = quarters(pick(cotangent))
    grads_all = share_rows(upstream)
    saved, layer_ins, outs = [], [], []
    for layer in range(2):
        layer_ins.append(rows_in)
        part, *attn_saved = attention(layer, rows_in, segs, packs, dense_own, dense_other)
        mid, gates, rows_all = mix(layer, part, quarters(rows_in), packs, chosen)
        partial, acts = experts(layer, rows_all, expert_own, expert_other)
        out = settle_layer(partial, mid)
        saved.append((attn_saved, mid, gates, rows_all, acts))
        rows_in = out.reshape(group_rows, width)
        outs.append(out)

    factors, smalls, expert_grads, input_grads = [None] * 2, [None] * 2, [None] * 2, [None] * 2
    for layer in (1, 0):
        attn_saved, mid, gates, rows_all, acts = saved[layer]
        partial, grad_in, grad_down = experts_back(layer, rows_all, grads_all, acts, expert_own, expert_other)
        expert_grads[layer] = (grad_in, grad_down)
        d_part, moe_gain_term, router_term = moe_back(layer, partial, mid, gates, packs, expert_count)
        attended, query_raw, key_raw, value_low = attn_saved
        part, d_mid, normed, d_proj, d_mid_low, head_gain_terms = attention_back(
            layer, layer_ins[layer], segs, packs, attn_saved, upstream, d_part, dense_own, dense_other
        )
        factors[layer] = (normed, d_proj, attended, d_mid_low)
        d_input, attn_gain_term = attn_back_rows(layer, part, quarters(layer_ins[layer]), packs, d_mid)
        if layer == 1:
            grads_all = d_input
            d_input = lax.dynamic_index_in_dim(
                d_input.reshape(RING * RING, RING, quarter, width), lax.axis_index("expert"), 0, keepdims=False
            )
        upstream = d_input
        input_grads[layer] = upstream
        smalls[layer] = (router_term, moe_gain_term, attn_gain_term, head_gain_terms)

    first, second, small, got_in, got_down, outputs, d_inputs = finish(factors, smalls, expert_grads, outs, input_grads)
    inner = w_query.shape[2]
    projections = first.reshape(width, first.shape[-1]).astype(F32)[None]

    def total(low, high, got):
        return jnp.where(lower, low, high).astype(F32) + got.astype(F32)

    grad_in = total(expert_grads[0][0], expert_grads[1][0], got_in)
    grad_down = total(expert_grads[0][1], expert_grads[1][1], got_down)
    units = w_gate.shape[3]
    grad_in = grad_in.reshape(2, 2, units, width)
    return (
        outputs.reshape(1, 2, group_rows, width),
        d_inputs.astype(F32).reshape(1, 2, group_rows, width),
        small[33:34],
        projections[:, :, :inner],
        projections[:, :, inner : inner + dim],
        projections[:, :, inner + dim :],
        small[34:35, :dim],
        small[34:35, dim : 2 * dim],
        second.reshape(inner, width).astype(F32)[None],
        small[32:33],
        small[:expert_count].T[None],
        jnp.swapaxes(grad_in[0], 1, 2)[None],
        jnp.swapaxes(grad_in[1], 1, 2)[None],
        grad_down.reshape(1, 2, units, width),
    )


def solution(mesh):
    placed = (
        P(None, "expert", None),
        P(None, "expert", None),
        P(None, "expert", None),
        P("section", None, "expert", None),
        P("section", None),
        P("section", None, "tensor"),
        P("section", None, "tensor"),
        P("section", None, "tensor"),
        P("section", None),
        P("section", None),
        P("section", "tensor", None),
        P("section", None),
        P("section", None, None),
        P("section", "expert", None, "tensor"),
        P("section", "expert", None, "tensor"),
        P("section", "expert", "tensor", None),
    )
    return jax.shard_map(
        body,
        mesh=mesh,
        in_specs=placed,
        out_specs=(
            P("section", None, "expert", None),
            P("section", None, "expert", None),
            P("section", None),
            P("section", None, "tensor"),
            P("section", None, "tensor"),
            P("section", None, "tensor"),
            P("section", None),
            P("section", None),
            P("section", "tensor", None),
            P("section", None),
            P("section", None, None),
            P("section", "expert", None, "tensor"),
            P("section", "expert", None, "tensor"),
            P("section", "expert", "tensor", None),
        ),
        check_vma=False,
    )
```

time: 1800 us -> 677 us (0.38)
  Pallas kernels: 0 us -> 615 us
  waiting for transfers between devices: 586 us -> 11.6 us
  blocking collectives: 384 us -> 0 us
  matrix products: 289 us -> 0 us
  local copies, waits for them, and re-layouts: 239 us -> 27.7 us
  other arithmetic: 217 us -> 11.9 us
  starting transfers between devices: 46 us -> 2.05 us
    pallas_call x0 -> x18, Pallas kernels: none -> 615 us  [the longest x1 141 us: finish(): pl.pallas_call(finish_kernel, name='finish', out_shape=(jax.ShapeDtypeStr...]
    dot_general x102 -> x0, matrix products: 289 us -> none  [the longest x3 25.1 us: expert_forward(): jnp.einsum('erf,efd->erd', hidden, down_w, preferred_element_type=jnp.flo...]
    all_gather x6 -> x0, waiting for transfers between devices: 257 us -> none  [spread(): return lax.all_gather(slot_rows, 'tensor', axis=1, tiled=True)]
    all_gather x12 -> x0, blocking collectives: 160 us -> none  [the longest x3 46.2 us: layer_backward(): lax.all_gather(router_term[None].astype(jnp.bfloat16), 'tensor', axis=0,...]
    psum x6 -> x0, waiting for transfers between devices: 151 us -> none  [the longest x3 121 us: body(): lax.psum(jnp.dot(layer_attended_low, output_w, preferred_element_type=jnp...]
    all_to_all x6 -> x0, blocking collectives: 139 us -> none  [send_rows(): lax.all_to_all(buffer, 'expert', split_axis=1, concat_axis=1, tiled=True)]
    reduce_scatter x6 -> x0, waiting for transfers between devices: 130 us -> none  [collect(): lax.psum_scatter(partial_rows.astype(jnp.bfloat16), 'tensor', scatter_dim...]
    psum x2 -> x0, blocking collectives: 84.7 us -> none  [the longest x1 75.5 us: body(): lax.psum(totals[0].astype(jnp.bfloat16), 'expert').astype(jnp.float32)]
  transfers between devices with their start and end apart: 28 -> 9, of which waited for: 21 -> 2; matrix products, arithmetic and copies ran while one was open for 19% -> 1% of each run, Pallas kernels for 0% -> 14%
where the time goes in v1:
time: 677 us; the launch traced here: 670 us
  Pallas kernels  615 us (91%)
  local copies, waits for them, and re-layouts  27.7 us (4%)
  other arithmetic  11.9 us (2%)
  waiting for transfers between devices  11.6 us (2%)
    pallas_call x1, Pallas kernels, finish(): pl.pallas_call(finish_kernel, name='finish', out_shape=(jax.ShapeDtypeStr...  141 us
    pallas_call x2, Pallas kernels, mix(): pl.pallas_call(functools.partial(mix_kernel, layer), name='mix', out_shap...  83.1 us
    pallas_call x2, Pallas kernels, settle_layer(): pl.pallas_call(settle_kernel, name='settle', out_shape=jax.ShapeDtypeStru...  81.6 us
    pallas_call x2, Pallas kernels, moe_back(): pl.pallas_call(functools.partial(moe_back_kernel, layer), name='moe_back'...  78.7 us
    pallas_call x2, Pallas kernels, experts_back(): pl.pallas_call(functools.partial(expert_back_kernel, layer), name='expert...  54.4 us
    pallas_call x2, Pallas kernels, attn_back_rows(): pl.pallas_call(functools.partial(attn_back_kernel, layer), name='attn_bac...  52.8 us
    pallas_call x1, Pallas kernels, share_rows(): pl.pallas_call(share_kernel, name='share', out_shape=jax.ShapeDtypeStruct...  42 us
    pallas_call x2, Pallas kernels, experts(): pl.pallas_call(functools.partial(expert_kernel, layer), name='experts', g...  32.9 us
  transfers between devices with their start and end apart: 9, of which 2 were waited for; matrix products, arithmetic and copies ran while one was open for 1% of the time, Pallas kernels for 14%

profile of v1, /device:TPU:0, one launch (start us, length us, event | category | flops | bytes accessed | tf_op | source)
XLA Modules:
  0.0 670.1 jit_solution(5875783923453386756)
XLA Ops:
  4.3 6.0 collective-permute-done.5
  10.8 5.6 collective-permute-done.3.v1
  22.1 42.0 %share.1 = bf16[4,4,4,24,2048]{4,3,2,1,0:T(8,128)(2,1)} custom-call(bf16[4,24,2048]{2,1,0:T(8,128)(2,1)} %bitcast.114), custom_call_target="tpu_custom_call" | custom-call | tf_op jit(solution)/shard_map/share/pallas_call | solution.py:408
  64.9 10.5 %attention.2 = (bf16[4,24,2048]{2,1,0:T(8,128)(2,1)}, bf16[96,1024]{1,0:T(8,128)(2,1)}, f32[96,1024]{1,0:T(8,128)}, f32[96,128]{1,0:T(8,128)}, bf16[96,128]{1,0:T(8,128)(2,1)}) custom-call(bf16[96,2048]{1,0:T(8,128)(2,1)} %bitcast.93, s32[96,1]{1,0:T(8,128)} %copy.40.seg_column, s32[1,96]{1,0:T(1,128)} %get-tuple-element.134.seg_row, ...), custom_call_target="tpu_custom_call" | custom-call | tf_op jit(solution)/shard_map/attention/pallas_call | solution.py:775
  75.4 41.0 %mix.2 = (f32[24,2048]{1,0:T(8,128)}, f32[24,128]{1,0:T(8,128)}, bf16[4,4,4,24,2176]{4,3,2,1,0:T(8,128)(2,1)}) custom-call(bf16[4,24,2048]{2,1,0:T(8,128)(2,1)} %get-tuple-element.73.part, bf16[4,24,2048]{2,1,0:T(8,128)(2,1)} %bitcast.94, bf16[144,2048]{1,0:T(8,128)(2,1)} %copy-done, bf16[144,2048]{1,0:T(8,128)(2,1)} %copy-done.1, s32[4,24,8]{2,1,0:T(8,128)} %bitcast.121, ...), custom_call_target="tpu_custom_call" | custom-call | tf_op jit(solution)/shard_map/mix/pallas_call | solution.py:343
  117.5 16.7 %experts.2 = (bf16[1536,2048]{1,0:T(8,128)(2,1)}, bf16[1536,768]{1,0:T(8,128)(2,1)}) custom-call(bf16[1536,2176]{1,0:T(8,128)(2,1)} %bitcast.69, bf16[2,192,2048]{2,1,0:T(8,128)(2,1)} %bitcast.75, bf16[2,192,2048]{2,1,0:T(8,128)(2,1)} %bitcast.80, bf16[2,192,2048]{2,1,0:T(8,128)(2,1)} %bitcast.85, bf16[2,192,2048]{2,1,0:T(8,128)(2,1)} %copy-done.2, ...), custom_call_target="tpu_custom_call" | custom-call | tf_op jit(solution)/shard_map/experts/pallas_call | solution.py:574
  134.2 42.6 %settle.2.resid.out0 = bf16[4,24,2048]{2,1,0:T(8,128)(2,1)} custom-call(bf16[4,4,4,24,2048]{4,3,2,1,0:T(8,128)(2,1)} %bitcast.111, f32[24,2048]{1,0:T(8,128)} %get-tuple-element.76.mid), custom_call_target="tpu_custom_call" | custom-call | tf_op jit(solution)/shard_map/settle/pallas_call | solution.py:379
  176.8 10.8 %attention.3 = (bf16[4,24,2048]{2,1,0:T(8,128)(2,1)}, bf16[96,1024]{1,0:T(8,128)(2,1)}, f32[96,1024]{1,0:T(8,128)}, f32[96,128]{1,0:T(8,128)}, bf16[96,128]{1,0:T(8,128)(2,1)}) custom-call(bf16[96,2048]{1,0:T(8,128)(2,1)} %bitcast.91, s32[96,1]{1,0:T(8,128)} %copy.40.seg_column, s32[1,96]{1,0:T(1,128)} %get-tuple-element.134.seg_row, ...), custom_call_target="tpu_custom_call" | custom-call | tf_op jit(solution)/shard_map/attention/pallas_call | solution.py:775
  187.6 42.1 %mix.3 = (f32[24,2048]{1,0:T(8,128)}, f32[24,128]{1,0:T(8,128)}, bf16[4,4,4,24,2176]{4,3,2,1,0:T(8,128)(2,1)}) custom-call(bf16[4,24,2048]{2,1,0:T(8,128)(2,1)} %get-tuple-element.81.part, bf16[4,24,2048]{2,1,0:T(8,128)(2,1)} %settle.2.resid.out0, bf16[144,2048]{1,0:T(8,128)(2,1)} %copy-done, bf16[144,2048]{1,0:T(8,128)(2,1)} %copy-done.1, ...), custom_call_target="tpu_custom_call" | custom-call | tf_op jit(solution)/shard_map/mix/pallas_call | solution.py:343
  229.8 16.2 %experts.3 = (bf16[1536,2048]{1,0:T(8,128)(2,1)}, bf16[1536,768]{1,0:T(8,128)(2,1)}) custom-call(bf16[1536,2176]{1,0:T(8,128)(2,1)} %bitcast.71, bf16[2,192,2048]{2,1,0:T(8,128)(2,1)} %bitcast.76, bf16[2,192,2048]{2,1,0:T(8,128)(2,1)} %bitcast.81, bf16[2,192,2048]{2,1,0:T(8,128)(2,1)} %bitcast.86, bf16[2,192,2048]{2,1,0:T(8,128)(2,1)} %copy-done.2, ...), custom_call_target="tpu_custom_call" | custom-call | tf_op jit(solution)/shard_map/experts/pallas_call | solution.py:574
  246.0 39.0 %settle.3.out1 = bf16[4,24,2048]{2,1,0:T(8,128)(2,1)} custom-call(bf16[4,4,4,24,2048]{4,3,2,1,0:T(8,128)(2,1)} %bitcast.112, f32[24,2048]{1,0:T(8,128)} %get-tuple-element.85.mid), custom_call_target="tpu_custom_call" | custom-call | tf_op jit(solution)/shard_map/settle/pallas_call | solution.py:379
  285.0 27.2 %experts_back.2 = (bf16[1536,2176]{1,0:T(8,128)(2,1)}, bf16[768,2048]{1,0:T(8,128)(2,1)}, bf16[384,2048]{1,0:T(8,128)(2,1)}) custom-call(bf16[1536,2176]{1,0:T(8,128)(2,1)} %bitcast.72, bf16[1536,2048]{1,0:T(8,128)(2,1)} %bitcast.73, bf16[1536,768]{1,0:T(8,128)(2,1)} %get-tuple-element.83.acts, bf16[2,192,2048]{2,1,0:T(8,128)(2,1)} %bitcast.77, ...), custom_call_target="tpu_custom_call" | custom-call | tf_op jit(solution)/shard_map/experts_back/pallas_call | solution.py:644
  312.3 40.3 %moe_back.2 = (bf16[4,24,2048]{2,1,0:T(8,128)(2,1)}, f32[1,2048]{1,0:T(1,128)}, f32[32,2048]{1,0:T(8,128)}) custom-call(bf16[4,4,4,24,2176]{4,3,2,1,0:T(8,128)(2,1)} %bitcast.110, f32[24,2048]{1,0:T(8,128)} %get-tuple-element.85.mid, f32[24,128]{1,0:T(8,128)} %get-tuple-element.86.gates, bf16[144,2048]{1,0:T(8,128)(2,1)} %copy-done, bf16[144,2048]{1,0:T(8,128)(2,1)} %copy-done.1), custom_call_target="tpu_custom_call" | custom-call | tf_op jit(solution)/shard_map/moe_back/pallas_call | solution.py:447
  352.6 13.7 %attention_back.2 = (bf16[4,24,2048]{2,1,0:T(8,128)(2,1)}, f32[4,24,2048]{2,1,0:T(8,128)}, bf16[96,2048]{1,0:T(8,128)(2,1)}, bf16[96,1280]{1,0:T(8,128)(2,1)}, b...) custom-call(bf16[96,2048]{1,0:T(8,128)(2,1)} %bitcast.92, s32[96,1]{1,0:T(8,128)} %copy.40.seg_column, ...), custom_call_target="tpu_custom_call" | custom-call | tf_op jit(solution)/shard_map/attention_back/pallas_call | solution.py:873
  366.2 36.7 %attn_back.1 = (bf16[4,4,4,24,2048]{4,3,2,1,0:T(8,128)(2,1)}, f32[1,2048]{1,0:T(1,128)}) custom-call(bf16[4,24,2048]{2,1,0:T(8,128)(2,1)} %get-tuple-element.88.part, bf16[4,24,2048]{2,1,0:T(8,128)(2,1)} %settle.2.resid.out0, bf16[144,2048]{1,0:T(8,128)(2,1)} %copy-done, bf16[144,2048]{1,0:T(8,128)(2,1)} %copy-done.1, f32[4,24,2048]{2,1,0:T(8,128)} %get-tuple-element.89.d_mid), custom_call_target="tpu_custom_call" | custom-call | tf_op jit(solution)/shard_map/attn_back/pallas_call | solution.py:492
  404.7 27.2 %experts_back.3 = (bf16[1536,2176]{1,0:T(8,128)(2,1)}, bf16[768,2048]{1,0:T(8,128)(2,1)}, bf16[384,2048]{1,0:T(8,128)(2,1)}) custom-call(bf16[1536,2176]{1,0:T(8,128)(2,1)} %bitcast.70, bf16[1536,2048]{1,0:T(8,128)(2,1)} %bitcast.108, bf16[1536,768]{1,0:T(8,128)(2,1)} %get-tuple-element.91.acts, bf16[2,192,2048]{2,1,0:T(8,128)(2,1)} %bitcast.78, ...), custom_call_target="tpu_custom_call" | custom-call | tf_op jit(solution)/shard_map/experts_back/pallas_call | solution.py:644
  431.9 38.4 %moe_back.3 = (bf16[4,24,2048]{2,1,0:T(8,128)(2,1)}, f32[1,2048]{1,0:T(1,128)}, f32[32,2048]{1,0:T(8,128)}) custom-call(bf16[4,4,4,24,2176]{4,3,2,1,0:T(8,128)(2,1)} %bitcast.109, f32[24,2048]{1,0:T(8,128)} %get-tuple-element.76.mid, f32[24,128]{1,0:T(8,128)} %get-tuple-element.93.gates, bf16[144,2048]{1,0:T(8,128)(2,1)} %copy-done, bf16[144,2048]{1,0:T(8,128)(2,1)} %copy-done.1), custom_call_target="tpu_custom_call" | custom-call | tf_op jit(solution)/shard_map/moe_back/pallas_call | solution.py:447
  470.3 13.4 %attention_back.3 = (bf16[4,24,2048]{2,1,0:T(8,128)(2,1)}, f32[4,24,2048]{2,1,0:T(8,128)}, bf16[96,2048]{1,0:T(8,128)(2,1)}, bf16[96,1280]{1,0:T(8,128)(2,1)}, b...) custom-call(bf16[96,2048]{1,0:T(8,128)(2,1)} %bitcast.95, s32[96,1]{1,0:T(8,128)} %copy.40.seg_column, ...), custom_call_target="tpu_custom_call" | custom-call | tf_op jit(solution)/shard_map/attention_back/pallas_call | solution.py:873
  483.7 16.1 %attn_back_last.1 = (bf16[4,24,2048]{2,1,0:T(8,128)(2,1)}, f32[1,2048]{1,0:T(1,128)}) custom-call(bf16[4,24,2048]{2,1,0:T(8,128)(2,1)} %get-tuple-element.103.part, bf16[4,24,2048]{2,1,0:T(8,128)(2,1)} %bitcast.96, bf16[144,2048]{1,0:T(8,128)(2,1)} %copy-done, bf16[144,2048]{1,0:T(8,128)(2,1)} %copy-done.1, f32[4,24,2048]{2,1,0:T(8,128)} %get-tuple-element.104.d_mid), custom_call_target="tpu_custom_call" | custom-call | tf_op jit(solution)/shard_map/attn_back_last/pallas_call | solution.py:492
  499.8 141.4 %finish.1 = (bf16[4,4,128,1280]{3,2,1,0:T(8,128)(2,1)}, bf16[4,4,64,2048]{3,2,1,0:T(8,128)(2,1)}, f32[48,2048]{1,0:T(8,128)}, bf16[768,2048]{1,0:T(8,128)(2,1)},...) custom-call(bf16[96,2048]{1,0:T(8,128)(2,1)} %get-tuple-element.95.n0, ...), custom_call_target="tpu_custom_call" | custom-call | tf_op jit(solution)/shard_map/finish/pallas_call | solution.py:1003
  641.3 6.8 %slice.42 = f32[1,2048,1024]{2,1,0:T(8,128)} slice(bf16[1,2048,1280]{2,1,0:T(8,128)(2,1)} %bitcast.89), slice={[0:1], [0:2048], [0:1024]} | slice | bytes 16777216 | tf_op jit(solution)/shard_map/slice | solution.py:1143
  648.1 2.8 fusion.13
  658.8 3.5 fusion.12
  663.0 4.4 convert.5
  (62 shorter events, 24.2 us)
Async XLA Ops:
  0.6 64.2 %collective-permute-start.1 = (bf16[2048,1024]{1,0:T(8,128)(2,1)}, bf16[2048,1024]{1,0:T(8,128)(2,1)}, u32[]{:S(2)}, u32[]{:S(2)}) collective-permute-start(bf16[2048,1024]{1,0:T(8,128)(2,1)} %bitcast.59), channel_id=1, source_target_pairs={{0,64},{64,0},{1,65},{65,1},{2,66},{66,2},{3,67},{67,3},{4,68},{68... | collective-permute-start | bytes 12582920 | tf_op jit(solution)/shard_map/ppermute | solution.py:1038
  0.7 64.1 %collective-permute-start.4 = (bf16[1024,2048]{1,0:T(8,128)(2,1)}, bf16[1024,2048]{1,0:T(8,128)(2,1)}, u32[]{:S(2)}, u32[]{:S(2)}) collective-permute-start(bf16[1024,2048]{1,0:T(8,128)(2,1)} %bitcast.64), channel_id=1, source_target_pairs={{0,64},{64,0},{1,65},{65,1},{2,66},{66,2},{3,67},{67,3},{4,68},{68... | collective-permute-start | bytes 12582920 | tf_op jit(solution)/shard_map/ppermute | solution.py:1038
  2.9 61.2 %copy-start = (bf16[144,2048]{1,0:T(8,128)(2,1)}, bf16[144,2048]{1,0:T(8,128)(2,1)S(1)}, u32[]{:S(2)}) copy-start(bf16[144,2048]{1,0:T(8,128)(2,1)S(1)} %fusion.3.pack0) | copy-start | bytes 1769476
  2.9 13.7 %collective-permute-start = (bf16[144,2048]{1,0:T(8,128)(2,1)S(1)}, bf16[144,2048]{1,0:T(8,128)(2,1)S(1)}, u32[]{:S(2)}, u32[]{:S(2)}) collective-permute-start(bf16[144,2048]{1,0:T(8,128)(2,1)S(1)} %fusion.3.pack0), channel_id=1, source_target_pairs={{0,64},{64,0},{1,65},{65,1},{2,66},{66,2},{3,67},{67,3},{4,68},{68... | collective-permute-start | bytes 1769480 | tf_op jit(solution)/shard_map/ppermute | solution.py:1038
  3.8 6.5 collective-permute-start.5
  4.2 6.3 collective-permute-start.2
  10.3 6.1 collective-permute-start.3
  10.5 53.7 %copy-start.5 = (bf16[2048,128]{1,0:T(8,128)(2,1)}, bf16[2048,128]{1,0:T(8,128)(2,1)S(1)}, u32[]{:S(2)}) copy-start(bf16[2048,128]{1,0:T(8,128)(2,1)S(1)} %collective-permute-done.2.k1) | copy-start | bytes 1572868
  10.5 105.9 %collective-permute-start.6 = (bf16[2,192,2048]{2,1,0:T(8,128)(2,1)}, bf16[2,192,2048]{2,1,0:T(8,128)(2,1)S(1)}, u32[]{:S(2)}, u32[]{:S(2)}) collective-permute-start(bf16[2,192,2048]{2,1,0:T(8,128)(2,1)} %bitcast.74), channel_id=1, source_target_pairs={{0,64},{64,0},{1,65},{65,1},{2,66},{66,2},{3,67},{67,3},{4,68},{68... | collective-permute-start | bytes 4718600 | tf_op jit(solution)/shard_map/ppermute | solution.py:1038
  16.4 0.8 copy-start.6
  16.4 100.0 %collective-permute-start.7 = (bf16[2,192,2048]{2,1,0:T(8,128)(2,1)}, bf16[2,192,2048]{2,1,0:T(8,128)(2,1)}, u32[]{:S(2)}, u32[]{:S(2)}) collective-permute-start(bf16[2,192,2048]{2,1,0:T(8,128)(2,1)} %bitcast.79), channel_id=1, source_target_pairs={{0,64},{64,0},{1,65},{65,1},{2,66},{66,2},{3,67},{67,3},{4,68},{68... | collective-permute-start | bytes 4718600 | tf_op jit(solution)/shard_map/ppermute | solution.py:1038
  17.2 46.9 %copy-start.1 = (bf16[144,2048]{1,0:T(8,128)(2,1)}, bf16[144,2048]{1,0:T(8,128)(2,1)S(1)}, u32[]{:S(2)}) copy-start(bf16[144,2048]{1,0:T(8,128)(2,1)S(1)} %collective-permute-done.pack1) | copy-start | bytes 1769476
  17.3 99.2 %collective-permute-start.8 = (bf16[2,192,2048]{2,1,0:T(8,128)(2,1)}, bf16[2,192,2048]{2,1,0:T(8,128)(2,1)}, u32[]{:S(2)}, u32[]{:S(2)}) collective-permute-start(bf16[2,192,2048]{2,1,0:T(8,128)(2,1)} %bitcast.84), channel_id=1, source_target_pairs={{0,64},{64,0},{1,65},{65,1},{2,66},{66,2},{3,67},{67,3},{4,68},{68... | collective-permute-start | bytes 4718600 | tf_op jit(solution)/shard_map/ppermute | solution.py:1038
  116.4 1.1 copy-start.2
  641.3 9.6 %copy-start.14 = (f32[48,2048]{1,0:T(8,128)S(1)}, f32[48,2048]{1,0:T(8,128)}, u32[]{:S(2)}) copy-start(f32[48,2048]{1,0:T(8,128)} %get-tuple-element.119) | copy-start | bytes 1179652
  641.3 11.5 %copy-start.11 = (bf16[384,2048]{1,0:T(8,128)(2,1)S(1)}, bf16[384,2048]{1,0:T(8,128)(2,1)}, u32[]{:S(2)}) copy-start(bf16[384,2048]{1,0:T(8,128)(2,1)} %get-tuple-element.123) | copy-start | bytes 4718596
  648.1 4.7 copy-start.7
  648.1 4.7 copy-start.8
  648.1 7.2 %copy-start.10 = (bf16[768,2048]{1,0:T(8,128)(2,1)S(1)}, bf16[768,2048]{1,0:T(8,128)(2,1)}, u32[]{:S(2)}) copy-start(bf16[768,2048]{1,0:T(8,128)(2,1)} %get-tuple-element.122) | copy-start | bytes 9437188
  652.7 2.5 copy-start.3
  652.8 4.0 copy-start.4
  658.8 4.2 copy-start.9
  663.0 4.5 copy-start.13
  663.0 5.8 copy-start.12

commit v2 on v1

v2 whole, which is shorter than its diff:
```python
import functools
import math

import jax
import jax.numpy as jnp
from jax import lax
from jax.experimental import pallas as pl
from jax.experimental.pallas import tpu as pltpu
from jax.sharding import PartitionSpec as P

RING = 4
BF16 = jnp.bfloat16
F32 = jnp.float32


def wrap(value):
    return lax.rem(value + 2 * RING, RING)


class Place:
    def __init__(self):
        self.section = lax.axis_index("section")
        expert = lax.axis_index("expert")
        self.x = lax.axis_index("tensor")
        self.z = lax.div(expert, RING)
        self.y = lax.rem(expert, RING)

    def index(self, axis):
        return getattr(self, axis)

    def device(self, axis, delta):
        at = {"x": self.x, "y": self.y, "z": self.z}
        at[axis] = wrap(at[axis] + delta)
        return (self.section, at["z"] * RING + at["y"], at["x"])

    def peer(self):
        return (1 - self.section, self.z * RING + self.y, self.x)


def greet(devices):
    barrier = pltpu.get_barrier_semaphore()
    for device in devices:
        pl.semaphore_signal(barrier, inc=1, device_id=device, device_id_type=pl.DeviceIdType.MESH)
    return lambda: pl.semaphore_wait(barrier, len(devices))


def meet(devices):
    greet(devices)()


class Copy:
    def __init__(self, sender, copy):
        self.sender, self.copy = sender, copy

    def wait_recv(self):
        self.sender.when(self.copy.wait_recv)


class Sender:
    def __init__(self, send_sems, recv_sems, flag=None):
        self.send_sems, self.recv_sems = send_sems, recv_sems
        self.flag = flag
        self.used = 0
        self.started = []

    def when(self, effect):
        if self.flag is None:
            effect()
        else:
            pl.when(self.flag)(effect)

    def make(self, source, target, device):
        copy = pltpu.make_async_remote_copy(
            src_ref=source,
            dst_ref=target,
            send_sem=self.send_sems.at[self.used],
            recv_sem=self.recv_sems.at[self.used],
            device_id=device,
            device_id_type=pl.DeviceIdType.MESH,
        )
        return copy

    def send(self, source, target, device):
        copy = self.make(source, target, device)
        self.used += 1
        self.when(copy.start)
        self.started.append(copy)
        return Copy(self, copy)

    def send_either(self, flag, source, otherwise, target, device):
        first, second = self.make(source, target, device), self.make(otherwise, target, device)
        self.used += 1
        pl.when(flag)(first.start)
        pl.when(jnp.logical_not(flag))(second.start)
        self.started.append(first)
        return Copy(self, first)

    def hand(self, flag, pairs, device):
        copies = []
        for source, target in pairs:
            copies.append(self.make(source, target, device))
            self.used += 1

        @pl.when(flag)
        def _():
            for copy in copies:
                copy.start()

        def settle():
            @pl.when(flag)
            def _():
                for copy in copies:
                    copy.wait_send()

            @pl.when(jnp.logical_not(flag))
            def _():
                for copy in copies:
                    copy.wait_recv()

        return settle

    def finish(self):
        def effect():
            for copy in self.started:
                copy.wait_send()

        self.when(effect)


def run(job):
    for _ in job:
        pass


def cut(width, count):
    tiles = width // 128
    edges = [tiles * i // count for i in range(count + 1)]
    return [(128 * a, 128 * (b - a)) for a, b in zip(edges[:-1], edges[1:])]


def region(place, order, phase, at, columns):
    spot = {}
    for i, axis in enumerate(order):
        spot[axis] = slice(None) if i < phase else (at if i == phase else place.index(axis))
    return (*[spot[axis] for axis in "zyx" if axis in spot], slice(None), pl.ds(*columns))


SENDS = 3 * (3 + 3 + 6)


def halves(columns):
    left, right = cut(columns[1], 2)
    return (columns[0] + left[0], left[1]), (columns[0] + right[0], right[1])


def thirds(buffer):
    return [(buffer, order, columns) for order, columns in zip(("xyz", "yzx", "zxy"), cut(buffer.shape[-1], 3))]


def gather(place, sender, plans, own=None, settle=None, beside=()):
    last_phase = len(plans[0][1]) - 1
    for phase in range(last_phase + 1):
        waits = []
        for buffer, order, columns in plans:
            axis = order[phase]
            me = place.index(axis)

            def push(delta, piece, buffer=buffer, order=order, axis=axis, me=me):
                here = buffer.at[region(place, order, phase, me, piece)]
                source = own.at[:, pl.ds(*piece)] if own is not None and phase == 0 else here
                return sender.send(source, here, place.device(axis, delta))

            if phase == last_phase:
                left, right = halves(columns)
                onward = (push(1, left), push(-1, right))
                waits += [push(1, right), push(-1, left)]
                waits.append((onward, buffer, order, axis, me, left, right))
            else:
                waits += [push(1, columns), push(-1, columns), push(2, columns)]
        if phase < len(beside):
            beside[phase]()
        yield
        last = []
        for wait in waits:
            if isinstance(wait, tuple):
                (up, down), buffer, order, axis, me, left, right = wait
                up.wait_recv()
                passing = buffer.at[region(place, order, phase, wrap(me - 1), left)]
                last.append(sender.send(passing, passing, place.device(axis, 1)))
                down.wait_recv()
                passing = buffer.at[region(place, order, phase, wrap(me + 1), right)]
                last.append(sender.send(passing, passing, place.device(axis, -1)))
            else:
                last.append(wait)
        if phase == last_phase:
            yield
        for copy in last:
            copy.wait_recv()
        if phase == 0 and settle is not None:
            settle()


def neighbours(place, axes="xyz"):
    return [place.device(axis, delta) for axis in axes for delta in (1, -1, 2)]


def reduce(place, sender, plans, slots, beside=()):
    last_phase = len(plans[0][1]) - 1
    for turn_number, phase in enumerate(range(last_phase, -1, -1)):
        waits = []
        for (buffer, order, columns), slot in zip(plans, slots):
            axis, slot = order[phase], slot[phase]
            me = place.index(axis)

            def push(delta, at, piece, target, buffer=buffer, order=order, axis=axis, me=me):
                source = buffer.at[region(place, order, phase, wrap(me + at), piece)]
                return sender.send(source, target, place.device(axis, delta))

            if phase == last_phase:
                left, right = halves(columns)
                up, down = push(1, 2, left, slot[0]), push(-1, 2, right, slot[1])
                near = push(1, 1, right, slot[2]), push(-1, -1, left, slot[3])
                waits.append((push, up, down, near))
            else:
                waits.append([push(delta, delta, columns, slot[i]) for i, delta in enumerate((1, -1, 2))])
        if turn_number < len(beside):
            beside[turn_number]()
        yield
        if phase == last_phase:
            later = []
            for (buffer, order, columns), slot, (push, up, down, near) in zip(plans, slots, waits):
                slot = slot[phase]
                me = place.index(order[phase])
                left, right = halves(columns)
                up.wait_recv()
                add_into(sender, buffer, region(place, order, phase, wrap(me + 1), left), slot[0])
                on_up = push(1, 1, left, slot[4])
                down.wait_recv()
                add_into(sender, buffer, region(place, order, phase, wrap(me - 1), right), slot[1])
                on_down = push(-1, -1, right, slot[5])
                later.append((*near, on_up, on_down))
            yield
            for (buffer, order, columns), slot, copies in zip(plans, slots, later):
                slot = slot[phase]
                me = place.index(order[phase])
                left, right = halves(columns)
                for copy in copies:
                    copy.wait_recv()
                add_into(sender, buffer, region(place, order, phase, me, left), slot[3], slot[4])
                add_into(sender, buffer, region(place, order, phase, me, right), slot[2], slot[5])
        else:
            for (buffer, order, columns), slot, copies in zip(plans, slots, waits):
                for copy in copies:
                    copy.wait_recv()
                add_into(sender, buffer, region(place, order, phase, place.index(order[phase]), columns), *slot[phase])


def slot_scratch(plans):
    scratch = []
    for rows, axes, columns in plans:
        left, right = halves(columns)
        for phase in range(axes):
            widths = (left, right, right, left, left, right) if phase == axes - 1 else (columns,) * 3
            scratch += [pltpu.VMEM((RING,) * phase + (rows, width), BF16) for _, width in widths]
    return scratch


def third_slots(rows, columns):
    return slot_scratch([(rows, 3, piece) for piece in cut(columns, 3)])


def sort_slots(refs, plans, axes):
    refs = list(refs)
    counts = [6 if phase == axes - 1 else 3 for phase in range(axes)]
    return [[[refs.pop(0) for _ in range(count)] for count in counts] for _ in range(plans)]


def add_into(sender, buffer, at, *terms):
    *spots, rows, columns = at
    free = [i for i, spot in enumerate(spots) if isinstance(spot, slice)]

    def one(n, _):
        spot = list(spots)
        picks = []
        for i in reversed(free):
            spot[i] = lax.rem(n, RING)
            picks.insert(0, spot[i])
            n = lax.div(n, RING)
        here = (*spot, rows, columns)
        total = buffer[here].astype(F32)
        for term in terms:
            total = total + term[(*picks, slice(None), slice(None))].astype(F32)
        buffer[here] = total.astype(BF16)
        return 0

    def all_blocks():
        if free:
            lax.fori_loop(0, RING ** len(free), one, 0)
        else:
            one(0, 0)

    sender.when(all_blocks)


EPS = 1e-06
THETA = 1000000.0
MASKED = -1e30
GATED = 128
VMEM_LIMIT = 56 << 20


def params(number):
    return pltpu.CompilerParams(collective_id=number, has_side_effects=True, vmem_limit_bytes=VMEM_LIMIT)


IN_VMEM = pl.BlockSpec(memory_space=pltpu.VMEM)
ANYWHERE = pl.BlockSpec(memory_space=pl.ANY)


def copy_sems(count):
    return [pltpu.SemaphoreType.DMA((count,)), pltpu.SemaphoreType.DMA((count,))]


def dot_nn(left, right):
    return lax.dot_general(left, right, (((1,), (0,)), ((), ())), preferred_element_type=F32)


def dot_nt(left, right):
    return lax.dot_general(left, right, (((1,), (1,)), ((), ())), preferred_element_type=F32)


def dot_tn(left, right):
    return lax.dot_general(left, right, (((0,), (0,)), ((), ())), preferred_element_type=F32)


def inverse_rms(rows):
    return lax.rsqrt(jnp.mean(rows * rows, axis=-1, keepdims=True) + EPS)


def rms_back(rows, gain, grad):
    scale = inverse_rms(rows)
    unit = rows * scale
    lifted = grad * gain
    return scale * (lifted - unit * jnp.mean(lifted * unit, axis=-1, keepdims=True)), grad * unit


def send_x(place, sender, part, slots):
    return [
        sender.send(part.at[wrap(place.x + delta)], slots.at[i], place.device("x", delta))
        for i, delta in enumerate((1, -1, 2))
    ]


def sum_x(place, copies, part, slots):
    for copy in copies:
        copy.wait_recv()
    total = part[place.x].astype(F32)
    for i in range(3):
        total = total + slots[i].astype(F32)
    return total


def gather_x(place, sender, whole):
    mine = whole.at[place.x]
    copies = [sender.send(mine, mine, place.device("x", delta)) for delta in (1, -1, 2)]
    for copy in copies:
        copy.wait_recv()


def settle_job(place, sender, load, buffer, slots, mid, out):
    load.wait()
    yield from reduce(place, sender, thirds(buffer), sort_slots(slots, 3, 3))
    moe_rows = buffer[place.z, place.y, place.x].astype(F32)
    out[place.x] = (mid[...] + moe_rows).astype(BF16)
    mine = out.at[place.x]
    copies = [sender.send(mine, mine, place.device("x", delta)) for delta in (1, -1, 2)]
    yield
    for copy in copies:
        copy.wait_recv()


def settle_kernel(partial, mid, out, buffer, send, recv, local, *slots):
    place = Place()
    load = pltpu.make_async_copy(partial, buffer, local)
    load.start()
    meet(neighbours(place))
    sender = Sender(send, recv)
    run(settle_job(place, sender, load, buffer, slots, mid, out))
    sender.finish()


def settle_layer(partial, mid):
    rows, width = partial.shape[-2:]
    return pl.pallas_call(
        settle_kernel,
        name="settle",
        out_shape=jax.ShapeDtypeStruct((RING, rows, width), BF16),
        in_specs=[ANYWHERE, IN_VMEM],
        out_specs=IN_VMEM,
        scratch_shapes=[
            pltpu.VMEM(partial.shape, BF16),
            *copy_sems(3 + SENDS),
            pltpu.SemaphoreType.DMA,
            *third_slots(rows, width),
        ],
        compiler_params=params(3),
    )(partial, mid)


def moe_back_kernel(
    layer, partial, mid, gates, pack0, pack1, d_part, gain_term, router_term, buffer, send, recv, local, *slots
):
    place = Place()
    load = pltpu.make_async_copy(partial, buffer, local)
    load.start()
    meet(neighbours(place))
    sender = Sender(send, recv)
    gain = of_layer(layer, pack0[PACK_ROUTER + 1 : PACK_ROUTER + 2], pack1[PACK_ROUTER + 1 : PACK_ROUTER + 2]).astype(F32)
    router = of_layer(layer, pack0[:PACK_ROUTER], pack1[:PACK_ROUTER])
    load.wait()
    run(reduce(place, sender, thirds(buffer), sort_slots(slots, 3, 3)))
    width = mid.shape[1]
    sums = buffer[place.z, place.y, place.x].astype(F32)
    weights = gates[...]
    d_gates = sums[:, width:]
    d_logits = (weights * (d_gates - jnp.sum(d_gates * weights, axis=-1, keepdims=True))).astype(BF16)
    d_moe_in = sums[:, :width] + dot_nn(d_logits, router)
    mid_rows = mid[...]
    d_mid, terms = rms_back(mid_rows, gain, d_moe_in)
    d_part[place.x] = d_mid.astype(BF16)
    gather_x(place, sender, d_part)
    gain_term[...] = jnp.sum(terms, axis=0, keepdims=True)
    moe_in = (mid_rows * inverse_rms(mid_rows) * gain).astype(BF16)
    router_term[...] = dot_tn(d_logits, moe_in)[: router_term.shape[0]]
    sender.finish()


def moe_back(layer, partial, mid, gates, packs, expert_count):
    rows, width = mid.shape
    return pl.pallas_call(
        functools.partial(moe_back_kernel, layer),
        name="moe_back",
        out_shape=(
            jax.ShapeDtypeStruct((RING, rows, width), BF16),
            jax.ShapeDtypeStruct((1, width), F32),
            jax.ShapeDtypeStruct((expert_count, width), F32),
        ),
        in_specs=[ANYWHERE] + [IN_VMEM] * 4,
        out_specs=(IN_VMEM,) * 3,
        scratch_shapes=[
            pltpu.VMEM(partial.shape, BF16),
            *copy_sems(3 + SENDS),
            pltpu.SemaphoreType.DMA,
            *third_slots(rows, width + GATED),
        ],
        compiler_params=params(5 + layer),
    )(partial, mid, gates, *packs)


TILE = 256


def load_weights(layer, own, other, targets, sems):
    gate, up, down = targets
    half = gate.shape[0] // 2
    section = lax.axis_index("section")

    def pairs(source):
        return [
            (source[0].at[0], gate.at[pl.ds(0, half)]),
            (source[0].at[1], gate.at[pl.ds(half, half)]),
            (source[1].at[0], up.at[pl.ds(0, half)]),
            (source[1].at[1], up.at[pl.ds(half, half)]),
            (source[2].at[0], down.at[pl.ds(0, half)]),
            (source[2].at[1], down.at[pl.ds(half, half)]),
        ]

    @pl.when(section == layer)
    def _():
        for i, (source, target) in enumerate(pairs(own)):
            pltpu.make_async_copy(source, target, sems.at[i]).start()

    @pl.when(section != layer)
    def _():
        for i, (source, target) in enumerate(pairs(other)):
            pltpu.make_async_copy(source, target, sems.at[i]).start()

    return [pltpu.make_async_copy(source, target, sems.at[i]) for i, (source, target) in enumerate(pairs(own))]


def gate_columns(table, half):
    first = 2 * lax.axis_index("expert")
    lanes = lax.broadcasted_iota(jnp.int32, table.shape, 1)
    table = table.astype(F32)
    one = jnp.sum(jnp.where(lanes == first, table, 0.0), axis=1, keepdims=True)
    two = jnp.sum(jnp.where(lanes == first + 1, table, 0.0), axis=1, keepdims=True)
    units = lax.broadcasted_iota(jnp.int32, (table.shape[0], 2 * half), 1)
    return jnp.where(units < half, one, two)


class Stream:
    def __init__(self, hbm, slots, sems, pieces=None):
        self.hbm, self.slots, self.sems = hbm, slots, sems
        self.pieces = pieces

    def copies(self, i, out):
        rows = pl.ds(i * TILE, TILE)
        made = []
        at = 0
        for n, ref in enumerate(self.hbm):
            far, near = ref.at[rows], self.slots.at[i % 2, :, pl.ds(at, ref.shape[1])]
            at += ref.shape[1]
            pair = (near, far) if out else (far, near)
            made.append(pltpu.make_async_copy(*pair, self.sems.at[i % 2, n]))
        return made

    def fetch(self, i):
        for copy in self.copies(i, False):
            copy.start()

    def fetched(self, i):
        for copy in self.copies(i, False):
            copy.wait()
        return self.slots.at[i % 2]

    def store(self, i):
        for copy in self.copies(i, True):
            copy.start()

    def stored(self, i):
        for copy in self.copies(i, True):
            copy.wait()


def stream_scratch(widths, pieces=1):
    scratch = []
    for width in widths:
        scratch += [pltpu.VMEM((2, TILE, width), BF16), pltpu.SemaphoreType.DMA((2, pieces))]
    return scratch


def expert_kernel(
    layer, rows, shared, own0, own1, own2, other0, other1, other2, out, acts, spread,
    gate, up, down, sems, row_slots, row_sems, out_slots, out_sems, act_slots, act_sems, send, recv, local
):
    place = Place()
    met = greet(neighbours(place))
    sender = Sender(send, recv)
    width = out.shape[1]
    units = gate.shape[0]
    tiles = rows.shape[0] // TILE
    weights = load_weights(layer, (own0, own1, own2), (other0, other1, other2), (gate, up, down), sems)
    keep = pltpu.make_async_copy(shared.at[place.x], spread.at[place.z, place.y, place.x], local)
    keep.start()

    def share():
        met()
        columns = shared.shape[2]
        orders = ("xyz", "yzx", "zxy")
        plans = [(spread, order, piece) for order, piece in zip(orders, cut(columns, 2 if layer == 0 else 1))]
        if layer:
            plans = [(spread, "zxy", (0, columns))]
        yield from gather(place, sender, plans, shared.at[place.x], keep.wait)

    job = share()
    ins, outs, kept = Stream([rows], row_slots, row_sems), Stream([out], out_slots, out_sems), Stream([acts], act_slots, act_sems)
    ins.fetch(0)
    for i in range(tiles):
        if i + 1 < tiles:
            ins.fetch(i + 1)
        tile = ins.fetched(i)
        if i == 0:
            for copy in weights:
                copy.wait()
        moe_in = tile[:, :width]
        gate_act = dot_nt(moe_in, gate[...])
        up_act = dot_nt(moe_in, up[...])
        hidden = gate_act / (1.0 + jnp.exp(-gate_act)) * up_act
        hidden = hidden * gate_columns(tile[:, width:], units // 2)
        if i >= 2:
            kept.stored(i - 2)
            outs.stored(i - 2)
        act_slots[i % 2, :, :units] = gate_act.astype(BF16)
        act_slots[i % 2, :, units:] = up_act.astype(BF16)
        out_slots[i % 2] = dot_nn(hidden.astype(BF16), down[...]).astype(BF16)
        kept.store(i)
        outs.store(i)
        next(job, None)
    run(job)
    for i in (tiles - 2, tiles - 1):
        kept.stored(i)
        outs.stored(i)
    sender.finish()


def experts(layer, rows_all, shared, own, other):
    quarter = rows_all.shape[3]
    count = RING**3 * quarter
    width = rows_all.shape[4] - GATED
    units = 2 * own[0].shape[1]
    rows = rows_all.reshape(count, width + GATED)
    out, acts, spread = pl.pallas_call(
        functools.partial(expert_kernel, layer),
        name="experts",
        out_shape=(
            jax.ShapeDtypeStruct((count, width), BF16),
            jax.ShapeDtypeStruct((count, 2 * units), BF16),
            jax.ShapeDtypeStruct((RING, RING, RING, quarter, shared.shape[2]), BF16),
        ),
        in_specs=[ANYWHERE, IN_VMEM] + [ANYWHERE] * 6,
        out_specs=(ANYWHERE,) * 3,
        scratch_shapes=[pltpu.VMEM((units, width), BF16)] * 3
        + [pltpu.SemaphoreType.DMA((6,))]
        + stream_scratch((width + GATED, width, 2 * units))
        + [*copy_sems(SENDS), pltpu.SemaphoreType.DMA],
        compiler_params=params(10 + layer),
    )(rows, shared, *own, *other)
    return out.reshape(*rows_all.shape[:4], width), acts, spread


def expert_back_kernel(layer, pieces, rows, *refs):
    refs = list(refs)

    def take(count):
        taken = refs[:count]
        del refs[:count]
        return taken

    grads, (acts,), own, other = take(pieces), take(1), take(3), take(3)
    extra = take(2 if layer else 6)
    out, grad_in, grad_down = take(3)
    made = take(1 if layer else 4)
    gate, up, down, sum_in, sum_down, sems = take(6)
    row_slots, row_sems, grad_slots, grad_sems, act_slots, act_sems, out_slots, out_sems, send, recv, local = take(11)
    place = Place()
    peer = place.peer()
    width = grad_in.shape[1]
    units = gate.shape[0]
    tiles = rows.shape[0] // TILE
    handed = None
    if layer:
        met = greet(neighbours(place))
        sender = Sender(send, recv)
        partial, mid = extra
        (settled,) = made
        buffer, *slots = refs
        load = pltpu.make_async_copy(partial, buffer, local.at[0])
        load.start()

        def side():
            met()
            yield from settle_job(place, sender, load, buffer, slots, mid, settled)

        job = side()
    else:
        met = greet([peer, *neighbours(place, "yz")])
        upper = place.section == 1
        sender = Sender(send, recv, upper)
        first_own, second_own, got_in, got_down = made
        stacks, (first, second), slots = refs[:4], refs[4:6], refs[6:]
        loads = [pltpu.make_async_copy(*pair, local.at[i]) for i, pair in enumerate(zip(extra[:4], stacks))]
        for copy in loads:
            copy.start()
        handing = Sender(refs[-2], refs[-1])
        slots = refs[6:-2]

        def side():
            for copy in loads:
                copy.wait()
            pl.when(upper)(lambda: gradient_products(*stacks, first, second))
            met()
            state["handed"] = handing.hand(place.section == 0, [(extra[4], got_in), (extra[5], got_down)], peer)
            yield from reduce(place, sender, gradient_plans(first, second), sort_slots(slots, 2, 2))
            first_own[...] = first[place.z, place.y]
            second_own[...] = second[place.z, place.y]

        state = {}
        job = side()

    weights = load_weights(layer, own, other, (gate, up, down), sems)
    ins, ups = Stream([rows], row_slots, row_sems), Stream(grads, grad_slots, grad_sems)
    kept, outs = Stream([acts], act_slots, act_sems), Stream([out], out_slots, out_sems)
    for stream in (ins, ups, kept):
        stream.fetch(0)
    first_expert = 2 * lax.axis_index("expert")
    for i in range(tiles):
        for stream in (ins, ups, kept):
            if i + 1 < tiles:
                stream.fetch(i + 1)
        tile, grad, act = ins.fetched(i), ups.fetched(i)[...], kept.fetched(i)
        if i == 0:
            for copy in weights:
                copy.wait()
        gates = gate_columns(tile[:, width:], units // 2)
        back = dot_nt(grad, down[...])
        gate_act = act[:, :units].astype(F32)
        up_act = act[:, units:].astype(F32)
        sigmoid = 1.0 / (1.0 + jnp.exp(-gate_act))
        silu = gate_act * sigmoid
        hidden = silu * up_act
        products = hidden * back
        in_one = lax.broadcasted_iota(jnp.int32, products.shape, 1) < units // 2
        one = jnp.sum(jnp.where(in_one, products, 0.0), axis=1, keepdims=True)
        two = jnp.sum(jnp.where(in_one, 0.0, products), axis=1, keepdims=True)
        lanes = lax.broadcasted_iota(jnp.int32, (products.shape[0], GATED), 1)
        d_gates = jnp.where(lanes == first_expert, one, jnp.where(lanes == first_expert + 1, two, 0.0))
        d_hidden = back * gates
        d_gate = (d_hidden * up_act * sigmoid * (1.0 + gate_act * (1.0 - sigmoid))).astype(BF16)
        d_up = (d_hidden * silu).astype(BF16)
        if i >= 2:
            outs.stored(i - 2)
        out_slots[i % 2, :, :width] = (dot_nn(d_gate, gate[...]) + dot_nn(d_up, up[...])).astype(BF16)
        out_slots[i % 2, :, width:] = d_gates.astype(BF16)
        outs.store(i)
        moe_in = tile[:, :width]
        terms = (
            (sum_in, slice(0, units), dot_tn(d_gate, moe_in)),
            (sum_in, slice(units, 2 * units), dot_tn(d_up, moe_in)),
            (sum_down, slice(0, units), dot_tn((hidden * gates).astype(BF16), grad)),
        )
        for total, at, term in terms:
            if i == 0:
                total[at] = term
            elif i < tiles - 1:
                total[at] += term
            else:
                low = grad_in if total is sum_in else grad_down
                low[at] = (total[at] + term).astype(BF16)
        next(job, None)
    run(job)
    for i in (tiles - 2, tiles - 1):
        outs.stored(i)
    sender.finish()
    if not layer:
        state["handed"]()


def experts_back(layer, rows_all, grads_all, acts, own, other, extra):
    quarter = rows_all.shape[3]
    count = RING**3 * quarter
    width = rows_all.shape[4] - GATED
    units = 2 * own[0].shape[1]
    grads = [g.reshape(count, g.shape[-1]) for g in grads_all]
    if layer:
        partial, mid = extra
        extra = (partial, mid)
        extra_specs, made_specs = [ANYWHERE, IN_VMEM], (IN_VMEM,)
        made = (jax.ShapeDtypeStruct((RING, quarter, width), BF16),)
        scratch = [
            *copy_sems(3 + SENDS),
            pltpu.SemaphoreType.DMA((1,)),
            pltpu.VMEM(partial.shape, BF16),
            *third_slots(quarter, width),
        ]
    else:
        factors, grads_one, dense = extra
        first, second = gradient_shapes(dense)
        normed, proj, heads, mids = factors
        extra = (normed, proj, heads, mids, *grads_one)
        extra_specs, made_specs = [ANYWHERE] * 6, (IN_VMEM, IN_VMEM, ANYWHERE, ANYWHERE)
        made = (
            jax.ShapeDtypeStruct(first[2:], BF16),
            jax.ShapeDtypeStruct(second[2:], BF16),
            jax.ShapeDtypeStruct(grads_one[0].shape, BF16),
            jax.ShapeDtypeStruct(grads_one[1].shape, BF16),
        )
        scratch = [
            *copy_sems(18),
            pltpu.SemaphoreType.DMA((4,)),
            *[pltpu.VMEM(f.shape, BF16) for f in factors],
            pltpu.VMEM(first, BF16),
            pltpu.VMEM(second, BF16),
            *gradient_slots(first, second),
            *copy_sems(2),
        ]
    out, *rest = pl.pallas_call(
        functools.partial(expert_back_kernel, layer, len(grads)),
        name="experts_back",
        out_shape=(
            jax.ShapeDtypeStruct((count, width + GATED), BF16),
            jax.ShapeDtypeStruct((2 * units, width), BF16),
            jax.ShapeDtypeStruct((units, width), BF16),
            *made,
        ),
        in_specs=[ANYWHERE] * (1 + len(grads) + 1 + 6) + extra_specs,
        out_specs=(ANYWHERE, IN_VMEM, IN_VMEM, *made_specs),
        scratch_shapes=[pltpu.VMEM((units, width), BF16)] * 3
        + [pltpu.VMEM((2 * units, width), F32), pltpu.VMEM((units, width), F32), pltpu.SemaphoreType.DMA((6,))]
        + stream_scratch((width + GATED,))
        + stream_scratch((width,), len(grads))
        + stream_scratch((2 * units, width + GATED))
        + scratch,
        compiler_params=params(12 + layer),
    )(rows_all.reshape(count, width + GATED), *grads, acts, *own, *other, *extra)
    return (out.reshape(*rows_all.shape), *rest)


def pull(layer, own, other, targets, sems):
    section = lax.axis_index("section")

    @pl.when(section == layer)
    def _():
        for i, (source, target) in enumerate(zip(own, targets)):
            pltpu.make_async_copy(source, target, sems.at[i]).start()

    @pl.when(section != layer)
    def _():
        for i, (source, target) in enumerate(zip(other, targets)):
            pltpu.make_async_copy(source, target, sems.at[i]).start()

    return [pltpu.make_async_copy(source, target, sems.at[i]) for i, (source, target) in enumerate(zip(own, targets))]


def of_layer(layer, own, other):
    return jnp.where(lax.axis_index("section") == layer, own, other)


def tables(seg_column, seg_row, dim):
    rows = seg_column.shape[0]
    at_row = lax.broadcasted_iota(jnp.int32, (rows, rows), 0)
    at_column = lax.broadcasted_iota(jnp.int32, (rows, rows), 1)
    earlier = jnp.sum((seg_row < seg_column).astype(F32), axis=1, keepdims=True)
    position = lax.broadcasted_iota(jnp.int32, (rows, dim), 0).astype(F32) - earlier
    lane = lax.broadcasted_iota(jnp.int32, (rows, dim), 1)
    half = dim // 2
    place = jnp.where(lane < half, lane, lane - half).astype(F32)
    angle = position * jnp.exp(place * (-math.log(THETA) / half))
    sine = jnp.sin(angle)
    return jnp.cos(angle), jnp.where(lane < half, -sine, sine), (seg_row == seg_column) & (at_column <= at_row)


def turn(rows, cosine, sine):
    return rows * cosine + pltpu.roll(rows, rows.shape[1] // 2, 1) * sine


def turn_back(grad, cosine, sine):
    return grad * cosine + pltpu.roll(grad * sine, grad.shape[1] // 2, 1)


PACK_ROUTER = 128
PACK_ROWS = 144
HEADS_STEP = 2


def attend_mix_kernel(
    layer, rows, seg_column, seg_row, pack0, pack1, routes0, routes1, q0, k0, v0, o0, q1, k1, v1, o1,
    attended, query_raw, key_raw, value_low, mid, gates, rows_all,
    wq, wk, wv, wo, total, part, own, slots, sems, send, recv, local
):
    place = Place()
    met = greet(neighbours(place))
    dim = wk.shape[1]
    heads = wq.shape[1] // dim
    step = HEADS_STEP * dim
    steps = heads // HEADS_STEP

    def pieces(q, k, v, o):
        columns = [q.at[:, pl.ds(i * step, step)] for i in range(steps)]
        return [k, v, *columns, *[o.at[pl.ds(i * step, step)] for i in range(steps)]]

    loads = pull(layer, pieces(q0, k0, v0, o0), pieces(q1, k1, v1, o1), pieces(wq, wk, wv, wo), sems)
    resid = rows[...].astype(F32)
    gain = of_layer(layer, pack0[PACK_ROUTER : PACK_ROUTER + 1], pack1[PACK_ROUTER : PACK_ROUTER + 1]).astype(F32)
    gains = of_layer(layer, pack0[PACK_ROUTER + 2 : PACK_ROUTER + 3], pack1[PACK_ROUTER + 2 : PACK_ROUTER + 3]).astype(F32)
    gain_query, gain_key = gains[:, :dim], gains[:, dim : 2 * dim]
    cosine, sine, allowed = tables(seg_column[...], seg_row[...], dim)
    normed = (resid * inverse_rms(resid) * gain).astype(BF16)
    loads[0].wait()
    raw = dot_nn(normed, wk[...])
    key_raw[...] = raw
    key = turn(raw * inverse_rms(raw) * gain_key, cosine, sine).astype(BF16)
    loads[1].wait()
    value = dot_nn(normed, wv[...]).astype(BF16)
    value_low[...] = value
    for i in range(steps):
        loads[2 + i].wait()
        raws = dot_nn(normed, wq[:, i * step : (i + 1) * step])
        query_raw[:, i * step : (i + 1) * step] = raws
        for h in range(HEADS_STEP):
            raw = raws[:, h * dim : (h + 1) * dim]
            query = turn(raw * inverse_rms(raw) * gain_query, cosine, sine).astype(BF16)
            scores = jnp.where(allowed, dot_nt(query, key) * (1.0 / math.sqrt(dim)), MASKED)
            raised = jnp.exp(scores - jnp.max(scores, axis=1, keepdims=True))
            probs = (raised / jnp.sum(raised, axis=1, keepdims=True)).astype(BF16)
            at = i * step + h * dim
            attended[:, at : at + dim] = dot_nn(probs, value).astype(BF16)
        loads[2 + steps + i].wait()
        piece = dot_nn(attended[:, i * step : (i + 1) * step], wo[i * step : (i + 1) * step])
        if i == 0:
            total[...] = piece
        else:
            total[...] += piece
    quarter = part.shape[1]
    for i in range(part.shape[0]):
        part[i] = total[i * quarter : (i + 1) * quarter].astype(BF16)
        total[i * quarter : (i + 1) * quarter] = resid[i * quarter : (i + 1) * quarter]
    sender = Sender(send, recv)
    met()
    copies = send_x(place, sender, part, slots)
    chosen = of_layer(layer, routes0[place.x], routes1[place.x])
    lanes = lax.broadcasted_iota(jnp.int32, gates.shape, 1)
    named = chosen[:, 0:1] == lanes
    for i in range(1, chosen.shape[1]):
        named = named | (chosen[:, i : i + 1] == lanes)
    gain = of_layer(layer, pack0[PACK_ROUTER + 1 : PACK_ROUTER + 2], pack1[PACK_ROUTER + 1 : PACK_ROUTER + 2])
    router = of_layer(layer, pack0[:PACK_ROUTER], pack1[:PACK_ROUTER])
    mine = total[pl.ds(pl.multiple_of(place.x * quarter, 8), quarter)]
    mid_rows = mine + sum_x(place, copies, part, slots)
    mid[...] = mid_rows
    moe_in = (mid_rows * inverse_rms(mid_rows) * gain.astype(F32)).astype(BF16)
    logits = jnp.where(named, dot_nt(moe_in, router), MASKED)
    raised = jnp.where(named, jnp.exp(logits - jnp.max(logits, axis=-1, keepdims=True)), 0.0)
    weights = raised / jnp.sum(raised, axis=-1, keepdims=True)
    gates[...] = weights
    own[:, : moe_in.shape[1]] = moe_in
    own[:, moe_in.shape[1] :] = weights.astype(BF16)
    keep = pltpu.make_async_copy(own, rows_all.at[place.z, place.y, place.x], local)
    keep.start()
    run(gather(place, sender, thirds(rows_all), own, keep.wait))
    sender.finish()


def weight_scratch(dense):
    return [pltpu.VMEM(w.shape, BF16) for w in dense]


def attend_mix(layer, rows, segs, packs, routes, own, other):
    count, width = rows.shape
    quarter = count // RING
    dim, inner = own[1].shape[1], own[0].shape[1]
    return pl.pallas_call(
        functools.partial(attend_mix_kernel, layer),
        name="attend_mix",
        out_shape=(
            jax.ShapeDtypeStruct((count, inner), BF16),
            jax.ShapeDtypeStruct((count, inner), F32),
            jax.ShapeDtypeStruct((count, dim), F32),
            jax.ShapeDtypeStruct((count, dim), BF16),
            jax.ShapeDtypeStruct((quarter, width), F32),
            jax.ShapeDtypeStruct((quarter, GATED), F32),
            jax.ShapeDtypeStruct((RING, RING, RING, quarter, width + GATED), BF16),
        ),
        in_specs=[IN_VMEM] * 7 + [ANYWHERE] * 8,
        out_specs=(IN_VMEM,) * 6 + (ANYWHERE,),
        scratch_shapes=[
            *weight_scratch(own),
            pltpu.VMEM((count, width), F32),
            pltpu.VMEM((RING, quarter, width), BF16),
            pltpu.VMEM((quarter, width + GATED), BF16),
            pltpu.VMEM((3, quarter, width), BF16),
            pltpu.SemaphoreType.DMA((2 + 2 * (inner // dim // HEADS_STEP),)),
            *copy_sems(3 + SENDS),
            pltpu.SemaphoreType.DMA,
        ],
        compiler_params=params(1 + layer),
    )(rows, *segs, *packs, *routes, *own, *other)


SMALL = 48


def gradient_shapes(dense):
    width, inner = dense[0].shape
    proj = inner + 2 * dense[1].shape[1]
    blocks = RING * RING
    return (RING, RING, width // blocks, proj), (RING, RING, inner // blocks, width)


def gradient_plans(first, second):
    return [(first, "yz", (0, first.shape[-1])), (second, "zy", (0, second.shape[-1]))]


def gradient_slots(first, second):
    return slot_scratch([(first[2], 2, (0, first[3])), (second[2], 2, (0, second[3]))])


def gradient_products(normed, proj, heads, mids, first, second):
    lanes = 128

    def output_blocks(i, _):
        pair = dot_tn(heads[:, pl.ds(pl.multiple_of(i * lanes, lanes), lanes)], mids[...]).astype(BF16)
        half = lanes // 2
        at = 2 * i
        second[lax.div(at, RING), lax.rem(at, RING)] = pair[:half]
        second[lax.div(at, RING), lax.rem(at, RING) + 1] = pair[half:]
        return 0

    def input_blocks(i, _):
        block = dot_tn(normed[:, pl.ds(pl.multiple_of(i * lanes, lanes), lanes)], proj[...])
        first[lax.div(i, RING), lax.rem(i, RING)] = block.astype(BF16)
        return 0

    lax.fori_loop(0, heads.shape[1] // lanes, output_blocks, 0)
    lax.fori_loop(0, normed.shape[1] // lanes, input_blocks, 0)


def attend_back_kernel(
    layer, rows, seg_column, seg_row, pack0, pack1, attended, query_raw, key_raw, value_low, upstream, d_part,
    router_term, moe_gain_term, *refs
):
    last = layer == 0
    refs = list(refs)
    extra = [refs.pop(0) for _ in range(4 if last else 0)]
    q0, k0, v0, o0, q1, k1, v1, o1, d_input, normed_both, d_proj, heads_both, d_mid_low, smalls = refs[:14]
    refs = refs[14:]
    wide = [refs.pop(0) for _ in range(4 if last else 0)]
    wq, wk, wv, wo, total, d_mid, d_heads, part, own, slots, sems, send, recv, local, *side = refs
    place = Place()
    peer = place.peer()
    met = greet([peer, *neighbours(place)])
    count = rows.shape[0]
    job = iter(())
    if last:
        upper = place.section == 1
        first_own, second_own, grad_in, grad_down = extra
        first, second, got_in, got_down = wide
        side_sender = Sender(side[0], side[1], upper)
        handing = Sender(side[2], side[3])

        def widen():
            first[place.z, place.y] = first_own[...]
            second[place.z, place.y] = second_own[...]
            yield
            met()
            yield from gather(place, side_sender, gradient_plans(first, second))

        job = widen()
    dim = wk.shape[1]
    heads = wq.shape[1] // dim
    inner = heads * dim
    step = HEADS_STEP * dim
    steps = heads // HEADS_STEP
    quarter = d_part.shape[1]

    def pieces(q, k, v, o):
        return [*[o.at[pl.ds(i * step, step)] for i in range(steps)],
                *[q.at[:, pl.ds(i * step, step)] for i in range(steps)], k, v]

    loads = pull(layer, pieces(q0, k0, v0, o0), pieces(q1, k1, v1, o1), pieces(wq, wk, wv, wo), sems)
    for i in range(RING):
        grad = upstream[i].astype(F32) + d_part[i].astype(F32)
        d_mid[i] = grad
        total[i * quarter : (i + 1) * quarter] = grad
    grad_low = total[...].astype(BF16)
    d_mid_low[:count] = grad_low
    heads_both[:count] = attended[...]
    resid = rows[...].astype(F32)
    gain = of_layer(layer, pack0[PACK_ROUTER : PACK_ROUTER + 1], pack1[PACK_ROUTER : PACK_ROUTER + 1]).astype(F32)
    gains = of_layer(layer, pack0[PACK_ROUTER + 2 : PACK_ROUTER + 3], pack1[PACK_ROUTER + 2 : PACK_ROUTER + 3]).astype(F32)
    gain_query, gain_key = gains[:, :dim], gains[:, dim : 2 * dim]
    cosine, sine, allowed = tables(seg_column[...], seg_row[...], dim)
    normed_both[:count] = (resid * inverse_rms(resid) * gain).astype(BF16)
    raw_key = key_raw[...]
    key = turn(raw_key * inverse_rms(raw_key) * gain_key, cosine, sine).astype(BF16)
    value = value_low[...]
    scale = 1.0 / math.sqrt(dim)
    d_key = jnp.zeros(key.shape, F32)
    d_value = jnp.zeros(key.shape, F32)
    gain_total = jnp.zeros(gain_query.shape, F32)
    handed_grads = None
    for i in range(steps):
        next(job, None)
        if last and i == 1:
            handed_grads = handing.hand(upper, [(grad_in, got_in), (grad_down, got_down)], peer)
        loads[i].wait()
        d_heads[...] = dot_nt(grad_low, wo[i * step : (i + 1) * step]).astype(BF16)
        for h in range(HEADS_STEP):
            at = i * step + h * dim
            raw = query_raw[:, at : at + dim]
            query = turn(raw * inverse_rms(raw) * gain_query, cosine, sine).astype(BF16)
            scores = jnp.where(allowed, dot_nt(query, key) * scale, MASKED)
            raised = jnp.exp(scores - jnp.max(scores, axis=1, keepdims=True))
            probs = raised / jnp.sum(raised, axis=1, keepdims=True)
            d_head = d_heads[:, h * dim : (h + 1) * dim]
            d_probs = dot_nt(d_head, value)
            d_value = d_value + dot_tn(probs.astype(BF16), d_head)
            d_scores = (probs * (d_probs - jnp.sum(d_probs * probs, axis=1, keepdims=True))).astype(BF16)
            d_query = turn_back(dot_nn(d_scores, key) * scale, cosine, sine)
            d_key = d_key + dot_tn(d_scores, query) * scale
            d_raw, terms = rms_back(raw, gain_query, d_query)
            gain_total = gain_total + jnp.sum(terms, axis=0, keepdims=True)
            d_proj[:count, at : at + dim] = d_raw.astype(BF16)
        loads[steps + i].wait()
        piece = dot_nt(d_proj[:count, i * step : (i + 1) * step], wq[:, i * step : (i + 1) * step])
        if i == 0:
            total[...] = piece
        else:
            total[...] += piece
    d_raw, terms = rms_back(raw_key, gain_key, turn_back(d_key, cosine, sine))
    d_proj[:count, inner : inner + dim] = d_raw.astype(BF16)
    d_proj[:count, inner + dim :] = d_value.astype(BF16)
    smalls[0, 32:] = jnp.zeros((SMALL - 32, smalls.shape[2]), F32)
    smalls[0, :32] = router_term[...]
    smalls[0, 32:33] = moe_gain_term[...]
    smalls[0, 34:35, :dim] = gain_total
    smalls[0, 34:35, dim : 2 * dim] = jnp.sum(terms, axis=0, keepdims=True)
    loads[2 * steps].wait()
    loads[2 * steps + 1].wait()
    total[...] += dot_nt(d_proj[:count, inner : inner + dim], wk[...]) + dot_nt(d_proj[:count, inner + dim :], wv[...])
    for i in range(RING):
        part[i] = total[i * quarter : (i + 1) * quarter].astype(BF16)
    sender = Sender(send, recv)
    if not last:
        met()
    copies = send_x(place, sender, part, slots)
    theirs = pl.ds(count, count)
    ours = pl.ds(0, count)
    handed = sender.hand(
        place.section != layer,
        [(ref.at[ours], ref.at[theirs]) for ref in (normed_both, d_proj, heads_both, d_mid_low)],
        peer,
    )
    mine = resid[:quarter]
    for i in range(1, RING):
        mine = jnp.where(place.x == i, resid[i * quarter : (i + 1) * quarter], mine)
    d_resid, terms = rms_back(mine, gain, sum_x(place, copies, part, slots))
    smalls[0, 33:34] = jnp.sum(terms, axis=0, keepdims=True)
    handed_small = sender.hand(place.section != layer, [(smalls.at[0], smalls.at[1])], peer)
    d_rows = (d_mid[place.x] + d_resid).astype(BF16)
    if last:
        d_input[place.x] = d_rows
        gather_x(place, sender, d_input)
    else:
        own[...] = d_rows
        keep = pltpu.make_async_copy(own, d_input.at[place.z, place.y, place.x], local)
        keep.start()
        run(gather(place, sender, thirds(d_input), own, keep.wait))
    handed()
    handed_small()
    sender.finish()
    if last:
        run(job)
        handed_grads()
        side_sender.finish()


def attend_back(layer, rows, segs, packs, saved, upstream, d_part, terms, extra, own, other):
    last = layer == 0
    wide, side = (), ()
    if last:
        first, second = gradient_shapes(own)
        wide = tuple(jax.ShapeDtypeStruct(shape, BF16) for shape in (first, second, extra[2].shape, extra[3].shape))
        side = (*copy_sems(18), *copy_sems(2))
    count, width = rows.shape
    quarter = count // RING
    dim, inner = own[1].shape[1], own[0].shape[1]
    out = (RING, quarter, width) if layer == 0 else (RING, RING, RING, quarter, width)
    return pl.pallas_call(
        functools.partial(attend_back_kernel, layer),
        name="attend_back_last" if layer == 0 else "attend_back",
        out_shape=(
            jax.ShapeDtypeStruct(out, BF16),
            jax.ShapeDtypeStruct((2 * count, width), BF16),
            jax.ShapeDtypeStruct((2 * count, inner + 2 * dim), BF16),
            jax.ShapeDtypeStruct((2 * count, inner), BF16),
            jax.ShapeDtypeStruct((2 * count, width), BF16),
            jax.ShapeDtypeStruct((2, SMALL, width), F32),
            *wide,
        ),
        in_specs=[IN_VMEM] * 13 + ([IN_VMEM] * 2 + [ANYWHERE] * 2 if last else []) + [ANYWHERE] * 8,
        out_specs=(IN_VMEM if last else ANYWHERE,) + (IN_VMEM,) * (7 if last else 5) + (ANYWHERE,) * (2 if last else 0),
        scratch_shapes=[
            *weight_scratch(own),
            pltpu.VMEM((count, width), F32),
            pltpu.VMEM((RING, quarter, width), F32),
            pltpu.VMEM((count, HEADS_STEP * dim), BF16),
            pltpu.VMEM((RING, quarter, width), BF16),
            pltpu.VMEM((quarter, width), BF16),
            pltpu.VMEM((3, quarter, width), BF16),
            pltpu.SemaphoreType.DMA((2 + 2 * (inner // dim // HEADS_STEP),)),
            *copy_sems(3 + 5 + (3 if layer == 0 else SENDS)),
            pltpu.SemaphoreType.DMA,
            *side,
        ],
        compiler_params=params(7 + layer),
    )(rows, *segs, *packs, *saved, upstream, d_part, *terms, *extra, *own, *other)


def finish_kernel(
    normed0, proj0, heads0, mids0, small0, small1, first_one, second_one, out0, out1, ig0, ig1,
    first, second, small_out, outputs, input_grads,
    first_sums, second_sums, normed, proj, heads, mids, terms, passing, small_slots, send, recv, flagged_send,
    flagged_recv, local, *slots
):
    place = Place()
    lower = place.section == 0
    upper = place.section == 1
    peer = place.peer()
    met = greet([peer, *neighbours(place)])
    sender = Sender(send, recv)
    reducer = Sender(flagged_send, flagged_recv, lower)

    def keep(index, source, otherwise, target):
        one, two = (pltpu.make_async_copy(origin, target, local.at[index]) for origin in (source, otherwise))
        pl.when(lower)(one.start)
        pl.when(upper)(two.start)
        return one

    pairs = ((small0, small1, terms), (out0, out1, outputs.at[place.section]), (ig0, ig1, input_grads.at[place.section]))
    kept = [keep(i, *pair) for i, pair in enumerate(pairs)]
    loads = ((normed0, normed), (proj0, proj), (heads0, heads), (mids0, mids))
    loads = [pltpu.make_async_copy(*pair, local.at[3 + i]) for i, pair in enumerate(loads)]
    ready = [
        pltpu.make_async_copy(*pair, local.at[7 + i]) for i, pair in enumerate(((first_one, first), (second_one, second)))
    ]

    @pl.when(upper)
    def _():
        for copy in ready:
            copy.start()

    @pl.when(lower)
    def _():
        for copy in loads:
            copy.start()
        for copy in loads:
            copy.wait()
        gradient_products(normed, proj, heads, mids, first_sums, second_sums)

    for copy in kept:
        copy.wait()
    met()
    state = {}

    def exchange(step, total):
        passing[...] = total
        buffer = small_slots.at[step, 3]
        buffer[...] = total.astype(BF16)
        state["copies"] = [
            sender.send(buffer, small_slots.at[step, i], place.device("xyz"[step], delta))
            for i, delta in enumerate((1, -1, 2))
        ]

    def collect(step):
        for copy in state["copies"]:
            copy.wait_recv()
        total = passing[...]
        for i in range(3):
            total = total + small_slots[step, i].astype(F32)
        return total

    def small_last():
        small_out[...] = collect(2)

    def swap_rows():
        state["late"] = [
            sender.send_either(lower, out1, out0, outputs.at[place.section], peer),
            sender.send_either(lower, ig1, ig0, input_grads.at[place.section], peer),
        ]
        exchange(0, terms[0] + terms[1])

    def second_step():
        exchange(1, collect(0))

    plans = gradient_plans(first_sums, second_sums)
    run(reduce(place, reducer, plans, sort_slots(slots, 2, 2), (swap_rows, second_step)))

    @pl.when(lower)
    def _():
        first[place.z, place.y] = first_sums[place.z, place.y]
        second[place.z, place.y] = second_sums[place.z, place.y]

    beside = (lambda: exchange(2, collect(1)), small_last)
    run(gather(place, reducer, gradient_plans(first, second), None, None, beside))
    for copy in state["late"]:
        copy.wait_recv()

    @pl.when(upper)
    def _():
        for copy in ready:
            copy.wait()

    sender.finish()
    reducer.finish()


def finish(factors, smalls, ready, outs, input_grads):
    rows, width = factors[0].shape
    first, second = ready[0].shape, ready[1].shape
    both = (2, *outs[0].shape)
    return pl.pallas_call(
        finish_kernel,
        name="finish",
        out_shape=(
            jax.ShapeDtypeStruct(first, BF16),
            jax.ShapeDtypeStruct(second, BF16),
            jax.ShapeDtypeStruct(smalls[0].shape[1:], F32),
            jax.ShapeDtypeStruct(both, BF16),
            jax.ShapeDtypeStruct(both, BF16),
        ),
        in_specs=[ANYWHERE] * 12,
        out_specs=(IN_VMEM,) * 3 + (ANYWHERE,) * 2,
        scratch_shapes=[
            pltpu.VMEM(first, BF16),
            pltpu.VMEM(second, BF16),
            *[pltpu.VMEM(f.shape, BF16) for f in factors],
            pltpu.VMEM(smalls[0].shape, F32),
            pltpu.VMEM(smalls[0].shape[1:], F32),
            pltpu.VMEM((3, 4, *smalls[0].shape[1:]), BF16),
            *copy_sems(2 + 9),
            *copy_sems(36),
            pltpu.SemaphoreType.DMA((9,)),
            *gradient_slots(first, second),
        ],
        compiler_params=params(9),
    )(*factors, *smalls, *ready, *outs, *input_grads)


def swap(vector):
    return lax.ppermute(vector, "section", [(0, 1), (1, 0)])


def body(
    block_input,
    cotangent,
    segments,
    routes,
    norm_attn,
    w_query,
    key_matrix,
    value_matrix,
    norm_query,
    norm_key,
    w_output,
    norm_moe,
    w_router,
    w_gate,
    w_up,
    w_down,
):
    section = lax.axis_index("section")
    lower = section == 0
    _, group_rows, width = block_input.shape
    expert_count = w_router.shape[2]
    quarter = group_rows // RING
    dim = norm_query.shape[1]

    dense_own = (w_query[0], key_matrix[0], value_matrix[0], w_output[0])
    expert_own = (jnp.swapaxes(w_gate[0], 1, 2), jnp.swapaxes(w_up[0], 1, 2), w_down[0])
    pack_own = jnp.concatenate(
        [
            jnp.pad(w_router[0].T, ((0, PACK_ROUTER - expert_count), (0, 0))),
            norm_attn,
            norm_moe,
            jnp.pad(jnp.concatenate([norm_query, norm_key], axis=1), ((0, PACK_ROWS - PACK_ROUTER - 3), (0, width - 2 * dim))),
        ],
        axis=0,
    )
    routes_own = lax.dynamic_index_in_dim(routes[0], section, 0, keepdims=False)
    routes_other = swap(lax.dynamic_index_in_dim(routes[0], 1 - section, 0, keepdims=False))
    packs = (pack_own, swap(pack_own))
    dense_other = tuple(swap(w) for w in dense_own)
    expert_other = tuple(swap(w) for w in expert_own)
    chosen = tuple(r.reshape(RING, quarter, r.shape[-1]) for r in (routes_own, routes_other))

    def pick(array):
        return lax.dynamic_index_in_dim(array, section, 0, keepdims=False)

    def quarters(array):
        return array.reshape(RING, quarter, array.shape[-1])

    segment = pick(segments)
    segs = (segment.reshape(group_rows, 1), segment.reshape(1, group_rows))

    rows_in = pick(block_input)
    upstream = quarters(pick(cotangent))
    edge = 2 * GATED * ((width // GATED) // 3)
    shared = (upstream[:, :, :edge], upstream[:, :, edge:])
    saved, layer_ins, outs, grads_all = [], [], [], []
    for layer in range(2):
        layer_ins.append(rows_in)
        *attn_saved, mid, gates, rows_all = attend_mix(layer, rows_in, segs, packs, chosen, dense_own, dense_other)
        partial, acts, spread = experts(layer, rows_all, shared[layer], expert_own, expert_other)
        grads_all.append(spread)
        saved.append((attn_saved, mid, gates, rows_all, acts))
        if layer == 0:
            out = settle_layer(partial, mid)
            rows_in = out.reshape(group_rows, width)
            outs.append(out)

    attn_saved, mid, gates, rows_all, acts = saved[1]
    partial, *grads_one, out = experts_back(1, rows_all, grads_all, acts, expert_own, expert_other, (partial, mid))
    outs.append(out)
    d_part, *terms = moe_back(1, partial, mid, gates, packs, expert_count)
    d_all, *factors_one, smalls_one = attend_back(
        1, layer_ins[1], segs, packs, attn_saved, upstream, d_part, terms[::-1], (), dense_own, dense_other
    )
    upstream = lax.dynamic_index_in_dim(
        d_all.reshape(RING * RING, RING, quarter, width), lax.axis_index("expert"), 0, keepdims=False
    )
    input_grads = [None, upstream]
    attn_saved, mid, gates, rows_all, acts = saved[0]
    partial, *grads_zero, first_own, second_own, got_in_one, got_down_one = experts_back(
        0, rows_all, [d_all], acts, expert_own, expert_other, (factors_one, grads_one, dense_own)
    )
    d_part, *terms = moe_back(0, partial, mid, gates, packs, expert_count)
    input_grads[0], *factors_zero, smalls_zero, first_one, second_one, got_in_zero, got_down_zero = attend_back(
        0, layer_ins[0], segs, packs, attn_saved, upstream, d_part, terms[::-1],
        (first_own, second_own, *grads_zero), dense_own, dense_other,
    )
    expert_grads = ((*grads_zero, got_in_zero, got_down_zero), (*grads_one, got_in_one, got_down_one))
    first, second, small, outputs, d_inputs = finish(
        factors_zero, (smalls_zero, smalls_one), (first_one, second_one), outs, input_grads
    )
    inner = w_query.shape[2]
    projections = first.reshape(width, first.shape[-1]).astype(F32)[None]

    def total(index):
        mine, theirs = [
            jnp.where(lower, expert_grads[0][i], expert_grads[1][i]).astype(F32) for i in (index, index + 2)
        ]
        return mine + theirs

    grad_in, grad_down = total(0), total(1)
    units = w_gate.shape[3]
    grad_in = grad_in.reshape(2, 2, units, width)
    return (
        outputs.reshape(1, 2, group_rows, width),
        d_inputs.astype(F32).reshape(1, 2, group_rows, width),
        small[33:34],
        projections[:, :, :inner],
        projections[:, :, inner : inner + dim],
        projections[:, :, inner + dim :],
        small[34:35, :dim],
        small[34:35, dim : 2 * dim],
        second.reshape(inner, width).astype(F32)[None],
        small[32:33],
        small[:expert_count].T[None],
        jnp.swapaxes(grad_in[0], 1, 2)[None],
        jnp.swapaxes(grad_in[1], 1, 2)[None],
        grad_down.reshape(1, 2, units, width),
    )


def solution(mesh):
    placed = (
        P(None, "expert", None),
        P(None, "expert", None),
        P(None, "expert", None),
        P("section", None, "expert", None),
        P("section", None),
        P("section", None, "tensor"),
        P("section", None, "tensor"),
        P("section", None, "tensor"),
        P("section", None),
        P("section", None),
        P("section", "tensor", None),
        P("section", None),
        P("section", None, None),
        P("section", "expert", None, "tensor"),
        P("section", "expert", None, "tensor"),
        P("section", "expert", "tensor", None),
    )
    return jax.shard_map(
        body,
        mesh=mesh,
        in_specs=placed,
        out_specs=(
            P("section", None, "expert", None),
            P("section", None, "expert", None),
            P("section", None),
            P("section", None, "tensor"),
            P("section", None, "tensor"),
            P("section", None, "tensor"),
            P("section", None),
            P("section", None),
            P("section", "tensor", None),
            P("section", None),
            P("section", None, None),
            P("section", "expert", None, "tensor"),
            P("section", "expert", None, "tensor"),
            P("section", "expert", "tensor", None),
        ),
        check_vma=False,
    )
```

time: 677 us -> 639 us (0.944)
  Pallas kernels: 615 us -> 576 us
    pallas_call x1, Pallas kernels: 141 us -> 101 us  [finish(): pl.pallas_call(finish_kernel, name='finish', out_shape=(jax.ShapeDtypeStr...]
    pallas_call x2 -> x1, Pallas kernels: 81.6 us -> 42.5 us  [settle_layer(): pl.pallas_call(settle_kernel, name='settle', out_shape=jax.ShapeDtypeStru...]
    pallas_call x13 -> x8, Pallas kernels: 314 us -> 353 us  [the longest x2 106 us: attend_mix(): pl.pallas_call(functools.partial(attend_mix_kernel, layer), name='attend_...]
  transfers between devices with their start and end apart: 9 -> 9, of which waited for: 2 -> 2; matrix products, arithmetic and copies ran while one was open for 1% -> 1% of each run, Pallas kernels for 14% -> 9%
where the time goes in v2:
time: 639 us; the launch traced here: 636 us
  Pallas kernels  576 us (90%)
  local copies, waits for them, and re-layouts  32.2 us (5%)
  other arithmetic  13.4 us (2%)
  waiting for transfers between devices  10.8 us (2%)
    pallas_call x2, Pallas kernels, attend_mix(): pl.pallas_call(functools.partial(attend_mix_kernel, layer), name='attend_...  106 us
    pallas_call x2, Pallas kernels, attend_back(): pl.pallas_call(functools.partial(attend_back_kernel, layer), name='attend...  101 us
    pallas_call x1, Pallas kernels, finish(): pl.pallas_call(finish_kernel, name='finish', out_shape=(jax.ShapeDtypeStr...  101 us
    pallas_call x2, Pallas kernels, moe_back(): pl.pallas_call(functools.partial(moe_back_kernel, layer), name='moe_back'...  79.6 us
    pallas_call x2, Pallas kernels, experts_back(): pl.pallas_call(functools.partial(expert_back_kernel, layer, len(grads)),...  74.5 us
    pallas_call x2, Pallas kernels, experts(): pl.pallas_call(functools.partial(expert_kernel, layer), name='experts', o...  71.1 us
    pallas_call x1, Pallas kernels, settle_layer(): pl.pallas_call(settle_kernel, name='settle', out_shape=jax.ShapeDtypeStru...  42.5 us
  transfers between devices with their start and end apart: 9, of which 2 were waited for; matrix products, arithmetic and copies ran while one was open for 1% of the time, Pallas kernels for 9%

profile of v2, /device:TPU:0, one launch (start us, length us, event | category | flops | bytes accessed | tf_op | source)
XLA Modules:
  0.0 635.7 jit_solution(15875689882008877544)
XLA Ops:
  4.4 6.0 collective-permute-done.1
  11.7 4.8 collective-permute-done.4.v1.refs_6_.refs_10_
  21.7 1.8 dynamic-slice_bitcast_fusion.1.rows
  24.2 57.5 %attend_mix.2 = (bf16[96,1024]{1,0:T(8,128)(2,1)}, f32[96,1024]{1,0:T(8,128)}, f32[96,128]{1,0:T(8,128)}, bf16[96,128]{1,0:T(8,128)(2,1)}, f32[24,2048]{1,0:T(8,...) custom-call(bf16[96,2048]{1,0:T(8,128)(2,1)} %dynamic-slice_bitcast_fusion.1.rows, ...), custom_call_target="tpu_custom_call" | custom-call | tf_op jit(solution)/shard_map/attend_mix/pallas_call | solution.py:931
  82.9 36.7 %experts.2 = (bf16[1536,2048]{1,0:T(8,128)(2,1)}, bf16[1536,768]{1,0:T(8,128)(2,1)}, bf16[4,4,4,24,1280]{4,3,2,1,0:T(8,128)(2,1)}) custom-call(bf16[1536,2176]{1,0:T(8,128)(2,1)} %bitcast.70, bf16[4,24,1280]{2,1,0:T(8,128)(2,1)} %slice.50.shared, bf16[2,192,2048]{2,1,0:T(8,128)(2,1)} %bitcast.75, bf16[2,192,2048]{2,1,0:T(8,128)(2,1)} %bitcast.80, ...), custom_call_target="tpu_custom_call" | custom-call | tf_op jit(solution)/shard_map/experts/pallas_call | solution.py:602
  119.6 42.5 %settle.1.out0 = bf16[4,24,2048]{2,1,0:T(8,128)(2,1)} custom-call(bf16[4,4,4,24,2048]{4,3,2,1,0:T(8,128)(2,1)} %bitcast.105, f32[24,2048]{1,0:T(8,128)} %get-tuple-element.78.mid), custom_call_target="tpu_custom_call" | custom-call | tf_op jit(solution)/shard_map/settle/pallas_call | solution.py:394
  162.1 48.4 %attend_mix.3 = (bf16[96,1024]{1,0:T(8,128)(2,1)}, f32[96,1024]{1,0:T(8,128)}, f32[96,128]{1,0:T(8,128)}, bf16[96,128]{1,0:T(8,128)(2,1)}, f32[24,2048]{1,0:T(8,...) custom-call(bf16[96,2048]{1,0:T(8,128)(2,1)} %bitcast.107, s32[96,1]{1,0:T(8,128)} %copy.40.seg_column, ...), custom_call_target="tpu_custom_call" | custom-call | tf_op jit(solution)/shard_map/attend_mix/pallas_call | solution.py:931
  210.5 34.4 %experts.3 = (bf16[1536,2048]{1,0:T(8,128)(2,1)}, bf16[1536,768]{1,0:T(8,128)(2,1)}, bf16[4,4,4,24,768]{4,3,2,1,0:T(8,128)(2,1)}) custom-call(bf16[1536,2176]{1,0:T(8,128)(2,1)} %bitcast.72, bf16[4,24,768]{2,1,0:T(8,128)(2,1)} %slice.51.shared, bf16[2,192,2048]{2,1,0:T(8,128)(2,1)} %bitcast.76, bf16[2,192,2048]{2,1,0:T(8,128)(2,1)} %bitcast.81, ...), custom_call_target="tpu_custom_call" | custom-call | tf_op jit(solution)/shard_map/experts/pallas_call | solution.py:602
  245.0 46.1 %experts_back.2 = (bf16[1536,2176]{1,0:T(8,128)(2,1)}, bf16[768,2048]{1,0:T(8,128)(2,1)}, bf16[384,2048]{1,0:T(8,128)(2,1)}, bf16[4,24,2048]{2,1,0:T(8,128)(2,1)}) custom-call(bf16[1536,2176]{1,0:T(8,128)(2,1)} %bitcast.73, bf16[1536,1280]{1,0:T(8,128)(2,1)} %bitcast.110, bf16[1536,768]{1,0:T(8,128)(2,1)} %bitcast.117, ...), custom_call_target="tpu_custom_call" | custom-call | tf_op jit(solution)/shard_map/experts_back/pallas_call | solution.py:776
  291.0 40.1 %moe_back.2 = (bf16[4,24,2048]{2,1,0:T(8,128)(2,1)}, f32[1,2048]{1,0:T(1,128)}, f32[32,2048]{1,0:T(8,128)}) custom-call(bf16[4,4,4,24,2176]{4,3,2,1,0:T(8,128)(2,1)} %bitcast.104, f32[24,2048]{1,0:T(8,128)} %get-tuple-element.88.refs_10_.mid, f32[24,128]{1,0:T(8,128)} %get-tuple-element.90.gates, bf16[144,2048]{1,0:T(8,128)(2,1)} %copy-done.2, ...), custom_call_target="tpu_custom_call" | custom-call | tf_op jit(solution)/shard_map/moe_back/pallas_call | solution.py:440
  331.1 48.6 %attend_back.1 = (bf16[4,4,4,24,2048]{4,3,2,1,0:T(8,128)(2,1)}, bf16[192,2048]{1,0:T(8,128)(2,1)}, bf16[192,1280]{1,0:T(8,128)(2,1)}, bf16[192,1024]{1,0:T(8,128...) custom-call(bf16[96,2048]{1,0:T(8,128)(2,1)} %bitcast.108, s32[96,1]{1,0:T(8,128)} %copy.40.seg_column, ...), custom_call_target="tpu_custom_call" | custom-call | tf_op jit(solution)/shard_map/attend_back/pallas_call | solution.py:1148
  379.7 1.8 dynamic-slice_bitcast_fusion.upstream.ig1
  381.5 28.4 %experts_back.3 = (bf16[1536,2176]{1,0:T(8,128)(2,1)}, bf16[768,2048]{1,0:T(8,128)(2,1)}, bf16[384,2048]{1,0:T(8,128)(2,1)}, bf16[128,1280]{1,0:T(8,128)(2,1)}, ...) custom-call(bf16[1536,2176]{1,0:T(8,128)(2,1)} %bitcast.71, ...), custom_call_target="tpu_custom_call" | custom-call | tf_op jit(solution)/shard_map/experts_back/pallas_call | solution.py:776
  409.9 39.5 %moe_back.3 = (bf16[4,24,2048]{2,1,0:T(8,128)(2,1)}, f32[1,2048]{1,0:T(1,128)}, f32[32,2048]{1,0:T(8,128)}) custom-call(bf16[4,4,4,24,2176]{4,3,2,1,0:T(8,128)(2,1)} %bitcast.103, f32[24,2048]{1,0:T(8,128)} %get-tuple-element.78.mid, f32[24,128]{1,0:T(8,128)} %get-tuple-element.103.gates, bf16[144,2048]{1,0:T(8,128)(2,1)} %copy-done.2, ...), custom_call_target="tpu_custom_call" | custom-call | tf_op jit(solution)/shard_map/moe_back/pallas_call | solution.py:440
  449.4 52.6 %attend_back_last.1 = (bf16[4,24,2048]{2,1,0:T(8,128)(2,1)}, bf16[192,2048]{1,0:T(8,128)(2,1)}, bf16[192,1280]{1,0:T(8,128)(2,1)}, bf16[192,1024]{1,0:T(8,128)(2...) custom-call(bf16[96,2048]{1,0:T(8,128)(2,1)} %dynamic-slice_bitcast_, ...), custom_call_target="tpu_custom_call" | custom-call | tf_op jit(solution)/shard_map/attend_back_last/pallas_call | solution.py:1148
  502.0 101.1 %finish.1 = (bf16[4,4,128,1280]{3,2,1,0:T(8,128)(2,1)}, bf16[4,4,64,2048]{3,2,1,0:T(8,128)(2,1)}, f32[48,2048]{1,0:T(8,128)}, bf16[2,4,24,2048]{3,2,1,0:T(8,128)(2,1)}, bf16[2,4,24,2048]{3,2,1,0:T(8,128)(2,1)}) custom-call(bf16[192,2048]{1,0:T(8,128)(2,1)} %get-tuple-element.111.normed0, bf16[192,1280]{1,0:T(8,128)(2,1)} %get-tuple-element.112.proj0, ...), custom_call_target="tpu_custom_call" | custom-call | tf_op jit(solution)/shard_map/finish/pallas_call | solution.py:1281
  604.3 1.5 fusion.14
  605.8 1.7 slice_bitcast_fusion
  607.5 2.7 fusion.13
  610.2 7.7 %slice.52 = f32[1,2048,1024]{2,1,0:T(8,128)} slice(bf16[1,2048,1280]{2,1,0:T(8,128)(2,1)} %bitcast.90), slice={[0:1], [0:2048], [0:1024]} | slice | bytes 16777216 | tf_op jit(solution)/shard_map/slice | solution.py:1421
  619.1 2.8 convert_add_fusion
  621.9 3.6 fusion.12
  626.9 4.8 convert.5
  631.7 2.8 convert_add_fusion.1
  (67 shorter events, 16.7 us)
Async XLA Ops:
  0.6 16.9 %copy-start = (bf16[2,96,2048]{2,1,0:T(8,128)(2,1)S(1)}, bf16[2,96,2048]{2,1,0:T(8,128)(2,1)}, u32[]{:S(2)}) copy-start(bf16[2,96,2048]{2,1,0:T(8,128)(2,1)} %param.17) | copy-start | bytes 2359300
  0.7 23.5 %collective-permute-start.2 = (bf16[2048,1024]{1,0:T(8,128)(2,1)}, bf16[2048,1024]{1,0:T(8,128)(2,1)}, u32[]{:S(2)}, u32[]{:S(2)}) collective-permute-start(bf16[2048,1024]{1,0:T(8,128)(2,1)} %bitcast.60), channel_id=1, source_target_pairs={{0,64},{64,0},{1,65},{65,1},{2,66},{66,2},{3,67},{67,3},{4,68},{68... | collective-permute-start | bytes 12582920 | tf_op jit(solution)/shard_map/ppermute | solution.py:1310
  0.8 23.4 %collective-permute-start.5 = (bf16[1024,2048]{1,0:T(8,128)(2,1)}, bf16[1024,2048]{1,0:T(8,128)(2,1)}, u32[]{:S(2)}, u32[]{:S(2)}) collective-permute-start(bf16[1024,2048]{1,0:T(8,128)(2,1)} %bitcast.65), channel_id=1, source_target_pairs={{0,64},{64,0},{1,65},{65,1},{2,66},{66,2},{3,67},{67,3},{4,68},{68... | collective-permute-start | bytes 12582920 | tf_op jit(solution)/shard_map/ppermute | solution.py:1310
  2.9 21.2 %copy-start.2 = (bf16[144,2048]{1,0:T(8,128)(2,1)}, bf16[144,2048]{1,0:T(8,128)(2,1)S(1)}, u32[]{:S(2)}) copy-start(bf16[144,2048]{1,0:T(8,128)(2,1)S(1)} %fusion.3.pack0) | copy-start | bytes 1769476
  2.9 13.7 %collective-permute-start = (bf16[144,2048]{1,0:T(8,128)(2,1)S(1)}, bf16[144,2048]{1,0:T(8,128)(2,1)S(1)}, u32[]{:S(2)}, u32[]{:S(2)}) collective-permute-start(bf16[144,2048]{1,0:T(8,128)(2,1)S(1)} %fusion.3.pack0), channel_id=1, source_target_pairs={{0,64},{64,0},{1,65},{65,1},{2,66},{66,2},{3,67},{67,3},{4,68},{68... | collective-permute-start | bytes 1769480 | tf_op jit(solution)/shard_map/ppermute | solution.py:1310
  3.9 6.5 %collective-permute-start.1 = (s32[96,8]{0,1:T(8,128)S(1)}, s32[96,8]{0,1:T(8,128)S(1)}, u32[]{:S(2)}, u32[]{:S(2)}) collective-permute-start(s32[96,8]{0,1:T(8,128)S(1)} %get-tuple-element.138), channel_id=1, source_target_pairs={{0,64},{64,0},{1,65},{65,1},{2,66},{66,2},{3,67},{67,3},{4,68},{68... | collective-permute-start | bytes 9224 | tf_op jit(solution)/shard_map/ppermute | solution.py:1310
  4.2 6.3 collective-permute-start.3
  10.3 6.1 collective-permute-start.4
  11.3 70.4 %collective-permute-start.6 = (bf16[2,192,2048]{2,1,0:T(8,128)(2,1)}, bf16[2,192,2048]{2,1,0:T(8,128)(2,1)S(1)}, u32[]{:S(2)}, u32[]{:S(2)}) collective-permute-start(bf16[2,192,2048]{2,1,0:T(8,128)(2,1)} %bitcast.74), channel_id=1, source_target_pairs={{0,64},{64,0},{1,65},{65,1},{2,66},{66,2},{3,67},{67,3},{4,68},{68... | collective-permute-start | bytes 4718600 | tf_op jit(solution)/shard_map/ppermute | solution.py:1310
  16.5 65.3 %collective-permute-start.7 = (bf16[2,192,2048]{2,1,0:T(8,128)(2,1)}, bf16[2,192,2048]{2,1,0:T(8,128)(2,1)}, u32[]{:S(2)}, u32[]{:S(2)}) collective-permute-start(bf16[2,192,2048]{2,1,0:T(8,128)(2,1)} %bitcast.79), channel_id=1, source_target_pairs={{0,64},{64,0},{1,65},{65,1},{2,66},{66,2},{3,67},{67,3},{4,68},{68... | collective-permute-start | bytes 4718600 | tf_op jit(solution)/shard_map/ppermute | solution.py:1310
  17.3 6.9 %copy-start.4 = (bf16[144,2048]{1,0:T(8,128)(2,1)}, bf16[144,2048]{1,0:T(8,128)(2,1)S(1)}, u32[]{:S(2)}) copy-start(bf16[144,2048]{1,0:T(8,128)(2,1)S(1)} %collective-permute-done.pack1) | copy-start | bytes 1769476
  17.3 64.5 %collective-permute-start.8 = (bf16[2,192,2048]{2,1,0:T(8,128)(2,1)}, bf16[2,192,2048]{2,1,0:T(8,128)(2,1)}, u32[]{:S(2)}, u32[]{:S(2)}) collective-permute-start(bf16[2,192,2048]{2,1,0:T(8,128)(2,1)} %bitcast.84), channel_id=1, source_target_pairs={{0,64},{64,0},{1,65},{65,1},{2,66},{66,2},{3,67},{67,3},{4,68},{68... | collective-permute-start | bytes 4718600 | tf_op jit(solution)/shard_map/ppermute | solution.py:1310
  610.2 7.7 %copy-start.5 = (bf16[768,2048]{1,0:T(8,128)(2,1)S(1)}, bf16[768,2048]{1,0:T(8,128)(2,1)}, u32[]{:S(2)}) copy-start(bf16[768,2048]{1,0:T(8,128)(2,1)} %get-tuple-element.100.refs_12_) | copy-start | bytes 9437188
  610.2 7.7 %copy-start.6 = (bf16[768,2048]{1,0:T(8,128)(2,1)S(1)}, bf16[768,2048]{1,0:T(8,128)(2,1)}, u32[]{:S(2)}) copy-start(bf16[768,2048]{1,0:T(8,128)(2,1)} %get-tuple-element.109.refs_2_) | copy-start | bytes 9437188
  610.2 7.7 %copy-start.13 = (bf16[768,2048]{1,0:T(8,128)(2,1)S(1)}, bf16[768,2048]{1,0:T(8,128)(2,1)}, u32[]{:S(2)}) copy-start(bf16[768,2048]{1,0:T(8,128)(2,1)} %get-tuple-element.127) | copy-start | bytes 9437188
  610.2 8.9 %copy-start.14 = (bf16[768,2048]{1,0:T(8,128)(2,1)S(1)}, bf16[768,2048]{1,0:T(8,128)(2,1)}, u32[]{:S(2)}) copy-start(bf16[768,2048]{1,0:T(8,128)(2,1)} %get-tuple-element.126) | copy-start | bytes 9437188
  621.9 3.6 copy-start.18
  621.9 4.9 copy-start.11
  626.9 4.8 copy-start.9
  626.9 4.8 copy-start.10
  626.9 4.8 copy-start.15
  626.9 4.8 copy-start.16
  631.7 2.9 copy-start.17
  631.7 3.7 copy-start.1
  (4 other events, 3.5 us)

commit v3 on v2

--- a/solution.py
+++ b/solution.py
@@ -125,6 +125,16 @@
                 copy.wait_send()
 
         self.when(effect)
+
+
+def paced(job, points):
+    count = iter(range(1000))
+
+    def step():
+        if next(count) in points:
+            next(job, None)
+
+    return step
 
 
 def run(job):
@@ -198,6 +208,18 @@
             copy.wait_recv()
         if phase == 0 and settle is not None:
             settle()
+
+
+def in_turn(jobs):
+    jobs = list(jobs)
+    while jobs:
+        for job in list(jobs):
+            try:
+                next(job)
+            except StopIteration:
+                jobs.remove(job)
+        if jobs:
+            yield
 
 
 def neighbours(place, axes="xyz"):
@@ -279,25 +301,24 @@
     *spots, rows, columns = at
     free = [i for i, spot in enumerate(spots) if isinstance(spot, slice)]
 
-    def one(n, _):
+    def some(first):
         spot = list(spots)
-        picks = []
-        for i in reversed(free):
-            spot[i] = lax.rem(n, RING)
-            picks.insert(0, spot[i])
-            n = lax.div(n, RING)
+        picks = [slice(None)] * len(free)
+        if first is not None:
+            spot[free[0]] = first
+            picks[0] = first
         here = (*spot, rows, columns)
         total = buffer[here].astype(F32)
         for term in terms:
             total = total + term[(*picks, slice(None), slice(None))].astype(F32)
         buffer[here] = total.astype(BF16)
-        return 0
 
     def all_blocks():
         if free:
-            lax.fori_loop(0, RING ** len(free), one, 0)
+            for i in range(RING):
+                some(i)
         else:
-            one(0, 0)
+            some(None)
 
     sender.when(all_blocks)
 
@@ -309,8 +330,8 @@
 VMEM_LIMIT = 56 << 20
 
 
-def params(number):
-    return pltpu.CompilerParams(collective_id=number, has_side_effects=True, vmem_limit_bytes=VMEM_LIMIT)
+def params(number, vmem=VMEM_LIMIT):
+    return pltpu.CompilerParams(collective_id=number, has_side_effects=True, vmem_limit_bytes=vmem)
 
 
 IN_VMEM = pl.BlockSpec(memory_space=pltpu.VMEM)
@@ -368,7 +389,8 @@
 
 
 def settle_job(place, sender, load, buffer, slots, mid, out):
-    load.wait()
+    if load is not None:
+        load.wait()
     yield from reduce(place, sender, thirds(buffer), sort_slots(slots, 3, 3))
     moe_rows = buffer[place.z, place.y, place.x].astype(F32)
     out[place.x] = (mid[...] + moe_rows).astype(BF16)
@@ -379,46 +401,37 @@
         copy.wait_recv()
 
 
-def settle_kernel(partial, mid, out, buffer, send, recv, local, *slots):
-    place = Place()
-    load = pltpu.make_async_copy(partial, buffer, local)
+def part_columns(part, width):
+    half = width // 2
+    return pl.ds(part * half, half)
+
+
+def settle_part(part, place, sems, partial, mid, out, scratch):
+    sender = Sender(*sems)
+    buffer, sem, *slots = scratch
+    columns = part_columns(part, mid.shape[1])
+    load = pltpu.make_async_copy(partial.at[:, :, :, :, columns], buffer, sem)
     load.start()
-    meet(neighbours(place))
-    sender = Sender(send, recv)
-    run(settle_job(place, sender, load, buffer, slots, mid, out))
-    sender.finish()
-
-
-def settle_layer(partial, mid):
-    rows, width = partial.shape[-2:]
-    return pl.pallas_call(
-        settle_kernel,
-        name="settle",
-        out_shape=jax.ShapeDtypeStruct((RING, rows, width), BF16),
-        in_specs=[ANYWHERE, IN_VMEM],
-        out_specs=IN_VMEM,
-        scratch_shapes=[
-            pltpu.VMEM(partial.shape, BF16),
-            *copy_sems(3 + SENDS),
-            pltpu.SemaphoreType.DMA,
-            *third_slots(rows, width),
-        ],
-        compiler_params=params(3),
-    )(partial, mid)
-
-
-def moe_back_kernel(
-    layer, partial, mid, gates, pack0, pack1, d_part, gain_term, router_term, buffer, send, recv, local, *slots
-):
-    place = Place()
-    load = pltpu.make_async_copy(partial, buffer, local)
-    load.start()
-    meet(neighbours(place))
-    sender = Sender(send, recv)
+    return settle_job(place, sender, load, buffer, slots, mid.at[:, columns], out), sender
+
+
+def settle_scratch(partial):
+    *blocks, rows, width = partial.shape
+    half = width // 2
+    return [
+        *copy_sems(3 + SENDS),
+        pltpu.VMEM((*blocks, rows, half), BF16),
+        pltpu.SemaphoreType.DMA,
+        *third_slots(rows, half),
+    ]
+
+
+SETTLE_SCRATCH = 2 + 2 + 36
+
+
+def moe_back_rows(layer, place, sender, buffer, mid, gates, pack0, pack1, d_part, gain_term, router_term):
     gain = of_layer(layer, pack0[PACK_ROUTER + 1 : PACK_ROUTER + 2], pack1[PACK_ROUTER + 1 : PACK_ROUTER + 2]).astype(F32)
     router = of_layer(layer, pack0[:PACK_ROUTER], pack1[:PACK_ROUTER])
-    load.wait()
-    run(reduce(place, sender, thirds(buffer), sort_slots(slots, 3, 3)))
     width = mid.shape[1]
     sums = buffer[place.z, place.y, place.x].astype(F32)
     weights = gates[...]
@@ -432,6 +445,19 @@
     gain_term[...] = jnp.sum(terms, axis=0, keepdims=True)
     moe_in = (mid_rows * inverse_rms(mid_rows) * gain).astype(BF16)
     router_term[...] = dot_tn(d_logits, moe_in)[: router_term.shape[0]]
+
+
+def moe_back_kernel(
+    layer, partial, mid, gates, pack0, pack1, d_part, gain_term, router_term, buffer, send, recv, local, *slots
+):
+    place = Place()
+    load = pltpu.make_async_copy(partial, buffer, local)
+    load.start()
+    meet(neighbours(place))
+    sender = Sender(send, recv)
+    load.wait()
+    run(reduce(place, sender, thirds(buffer), sort_slots(slots, 3, 3)))
+    moe_back_rows(layer, place, sender, buffer, mid, gates, pack0, pack1, d_part, gain_term, router_term)
     sender.finish()
 
 
@@ -499,12 +525,12 @@
 
 
 class Stream:
-    def __init__(self, hbm, slots, sems, pieces=None):
+    def __init__(self, hbm, slots, sems):
         self.hbm, self.slots, self.sems = hbm, slots, sems
-        self.pieces = pieces
 
     def copies(self, i, out):
-        rows = pl.ds(i * TILE, TILE)
+        tile = self.slots.shape[1]
+        rows = pl.ds(i * tile, tile)
         made = []
         at = 0
         for n, ref in enumerate(self.hbm):
@@ -532,39 +558,50 @@
             copy.wait()
 
 
-def stream_scratch(widths, pieces=1):
+def stream_scratch(widths, pieces=1, tile=TILE):
     scratch = []
     for width in widths:
-        scratch += [pltpu.VMEM((2, TILE, width), BF16), pltpu.SemaphoreType.DMA((2, pieces))]
+        scratch += [pltpu.VMEM((2, tile, width), BF16), pltpu.SemaphoreType.DMA((2, pieces))]
     return scratch
 
 
-def expert_kernel(
-    layer, rows, shared, own0, own1, own2, other0, other1, other2, out, acts, spread,
-    gate, up, down, sems, row_slots, row_sems, out_slots, out_sems, act_slots, act_sems, send, recv, local
-):
+SHARE_POINTS = (2, 5, 10)
+BLOCKS = 8
+
+
+def expert_kernel(layer, rows, shared, *refs):
+    refs = list(refs)
+
+    def take(count):
+        taken = refs[:count]
+        del refs[:count]
+        return taken
+
+    mid = take(0 if layer else 1)
+    own, other, (out, acts, spread), (gate, up, down, sems) = take(3), take(3), take(3), take(4)
+    row_slots, row_sems, act_slots, act_sems, send, recv, local = take(7)
     place = Place()
     met = greet(neighbours(place))
-    sender = Sender(send, recv)
-    width = out.shape[1]
+    sharer = Sender(send, recv)
+    width = gate.shape[1]
     units = gate.shape[0]
-    tiles = rows.shape[0] // TILE
-    weights = load_weights(layer, (own0, own1, own2), (other0, other1, other2), (gate, up, down), sems)
+    weights = load_weights(layer, own, other, (gate, up, down), sems)
     keep = pltpu.make_async_copy(shared.at[place.x], spread.at[place.z, place.y, place.x], local)
     keep.start()
-
-    def share():
-        met()
-        columns = shared.shape[2]
-        orders = ("xyz", "yzx", "zxy")
-        plans = [(spread, order, piece) for order, piece in zip(orders, cut(columns, 2 if layer == 0 else 1))]
-        if layer:
-            plans = [(spread, "zxy", (0, columns))]
-        yield from gather(place, sender, plans, shared.at[place.x], keep.wait)
-
-    job = share()
-    ins, outs, kept = Stream([rows], row_slots, row_sems), Stream([out], out_slots, out_sems), Stream([acts], act_slots, act_sems)
+    ins, kept = Stream([rows], row_slots, row_sems), Stream([acts], act_slots, act_sems)
+    tile_rows = row_slots.shape[1]
+    tiles = rows.shape[0] // tile_rows
     ins.fetch(0)
+    if layer:
+        out_slots, out_sems = refs
+        outs = Stream([out], out_slots, out_sems)
+    else:
+        buffer, *slots = refs[2:]
+        quarter = buffer.shape[3]
+    met()
+    sharing = gather(place, sharer, thirds(spread), shared.at[place.x], keep.wait)
+    next(sharing)
+    step = paced(sharing, SHARE_POINTS)
     for i in range(tiles):
         if i + 1 < tiles:
             ins.fetch(i + 1)
@@ -577,45 +614,78 @@
         up_act = dot_nt(moe_in, up[...])
         hidden = gate_act / (1.0 + jnp.exp(-gate_act)) * up_act
         hidden = hidden * gate_columns(tile[:, width:], units // 2)
+        step()
         if i >= 2:
             kept.stored(i - 2)
-            outs.stored(i - 2)
         act_slots[i % 2, :, :units] = gate_act.astype(BF16)
         act_slots[i % 2, :, units:] = up_act.astype(BF16)
-        out_slots[i % 2] = dot_nn(hidden.astype(BF16), down[...]).astype(BF16)
         kept.store(i)
-        outs.store(i)
-        next(job, None)
-    run(job)
+        made = dot_nn(hidden.astype(BF16), down[...])
+        if layer:
+            if i >= 2:
+                outs.stored(i - 2)
+            out_slots[i % 2] = made.astype(BF16)
+            outs.store(i)
+        else:
+            for n in range(BLOCKS):
+                block = i * BLOCKS + n
+                here = (block // (RING * RING), block // RING % RING, block % RING)
+                buffer[here] = made[n * quarter : (n + 1) * quarter].astype(BF16)
+        step()
+    if layer:
+        run(sharing)
+        for i in (tiles - 2, tiles - 1):
+            outs.stored(i)
+    else:
+        sender = Sender(*refs[:2])
+        run(in_turn([settle_job(place, sender, None, buffer, slots, mid[0], out), sharing]))
+        sender.finish()
     for i in (tiles - 2, tiles - 1):
         kept.stored(i)
-        outs.stored(i)
-    sender.finish()
-
-
-def experts(layer, rows_all, shared, own, other):
+    sharer.finish()
+
+
+def experts(layer, rows_all, shared, mid, own, other):
     quarter = rows_all.shape[3]
     count = RING**3 * quarter
     width = rows_all.shape[4] - GATED
     units = 2 * own[0].shape[1]
     rows = rows_all.reshape(count, width + GATED)
+    tile = TILE if layer else BLOCKS * quarter
+    if layer:
+        mids, out_shape, out_spec = (), (count, width), ANYWHERE
+        tail = stream_scratch((width,))
+    else:
+        mids, out_shape, out_spec = (mid,), (RING, quarter, width), IN_VMEM
+        tail = [
+            *copy_sems(3 + SENDS),
+            pltpu.VMEM((*rows_all.shape[:4], width), BF16),
+            *third_slots(quarter, width),
+        ]
     out, acts, spread = pl.pallas_call(
         functools.partial(expert_kernel, layer),
-        name="experts",
+        name="experts" if layer else "experts_settle",
         out_shape=(
-            jax.ShapeDtypeStruct((count, width), BF16),
+            jax.ShapeDtypeStruct(out_shape, BF16),
             jax.ShapeDtypeStruct((count, 2 * units), BF16),
             jax.ShapeDtypeStruct((RING, RING, RING, quarter, shared.shape[2]), BF16),
         ),
-        in_specs=[ANYWHERE, IN_VMEM] + [ANYWHERE] * 6,
-        out_specs=(ANYWHERE,) * 3,
+        in_specs=[ANYWHERE, IN_VMEM] + [IN_VMEM] * len(mids) + [ANYWHERE] * 6,
+        out_specs=(out_spec, ANYWHERE, ANYWHERE),
         scratch_shapes=[pltpu.VMEM((units, width), BF16)] * 3
         + [pltpu.SemaphoreType.DMA((6,))]
-        + stream_scratch((width + GATED, width, 2 * units))
-        + [*copy_sems(SENDS), pltpu.SemaphoreType.DMA],
+        + stream_scratch((width + GATED, 2 * units), tile=tile)
+        + [*copy_sems(SENDS), pltpu.SemaphoreType.DMA]
+        + tail,
         compiler_params=params(10 + layer),
-    )(rows, shared, *own, *other)
-    return out.reshape(*rows_all.shape[:4], width), acts, spread
+    )(rows, shared, *mids, *own, *other)
+    if layer:
+        out = out.reshape(*rows_all.shape[:4], width)
+    return out, acts, spread
+
+
+SETTLE_POINTS = (3, 6)
+SUM_POINTS = (4, 9)
 
 
 def expert_back_kernel(layer, pieces, rows, *refs):
@@ -627,9 +697,9 @@
         return taken
 
     grads, (acts,), own, other = take(pieces), take(1), take(3), take(3)
-    extra = take(2 if layer else 6)
+    extra = take(4)
     out, grad_in, grad_down = take(3)
-    made = take(1 if layer else 4)
+    made = take(4)
     gate, up, down, sum_in, sum_down, sems = take(6)
     row_slots, row_sems, grad_slots, grad_sems, act_slots, act_sems, out_slots, out_sems, send, recv, local = take(11)
     place = Place()
@@ -637,51 +707,35 @@
     width = grad_in.shape[1]
     units = gate.shape[0]
     tiles = rows.shape[0] // TILE
-    handed = None
-    if layer:
-        met = greet(neighbours(place))
-        sender = Sender(send, recv)
-        partial, mid = extra
-        (settled,) = made
-        buffer, *slots = refs
-        load = pltpu.make_async_copy(partial, buffer, local.at[0])
-        load.start()
-
-        def side():
-            met()
-            yield from settle_job(place, sender, load, buffer, slots, mid, settled)
-
-        job = side()
-    else:
-        met = greet([peer, *neighbours(place, "yz")])
-        upper = place.section == 1
-        sender = Sender(send, recv, upper)
-        first_own, second_own, got_in, got_down = made
-        stacks, (first, second), slots = refs[:4], refs[4:6], refs[6:]
-        loads = [pltpu.make_async_copy(*pair, local.at[i]) for i, pair in enumerate(zip(extra[:4], stacks))]
+    met = greet([peer, *neighbours(place, "yz")])
+    upper = place.section == 1
+    sender = Sender(send, recv, upper)
+    first_own, second_own, got_in, got_down = made
+    first, second, *slots = refs[:-2]
+    loads = [pltpu.make_async_copy(*pair, local.at[i]) for i, pair in enumerate(zip(extra[:2], (first, second)))]
+    for copy in loads:
+        sender.when(copy.start)
+    handing = Sender(refs[-2], refs[-1])
+
+    def side():
+        met()
+        state["handed"] = handing.hand(place.section == 0, [(extra[2], got_in), (extra[3], got_down)], peer)
         for copy in loads:
-            copy.start()
-        handing = Sender(refs[-2], refs[-1])
-        slots = refs[6:-2]
-
-        def side():
-            for copy in loads:
-                copy.wait()
-            pl.when(upper)(lambda: gradient_products(*stacks, first, second))
-            met()
-            state["handed"] = handing.hand(place.section == 0, [(extra[4], got_in), (extra[5], got_down)], peer)
-            yield from reduce(place, sender, gradient_plans(first, second), sort_slots(slots, 2, 2))
-            first_own[...] = first[place.z, place.y]
-            second_own[...] = second[place.z, place.y]
-
-        state = {}
-        job = side()
+            sender.when(copy.wait)
+        yield from in_turn(gradient_reduces(place, sender, first, second, slots))
+        first_own[...] = first[place.z, place.y]
+        second_own[...] = second[place.z, place.y]
+
+    state = {}
+    job = side()
 
     weights = load_weights(layer, own, other, (gate, up, down), sems)
     ins, ups = Stream([rows], row_slots, row_sems), Stream(grads, grad_slots, grad_sems)
     kept, outs = Stream([acts], act_slots, act_sems), Stream([out], out_slots, out_sems)
     for stream in (ins, ups, kept):
         stream.fetch(0)
+    next(job)
+    step = paced(job, SUM_POINTS)
     first_expert = 2 * lax.axis_index("expert")
     for i in range(tiles):
         for stream in (ins, ups, kept):
@@ -712,6 +766,7 @@
         out_slots[i % 2, :, :width] = (dot_nn(d_gate, gate[...]) + dot_nn(d_up, up[...])).astype(BF16)
         out_slots[i % 2, :, width:] = d_gates.astype(BF16)
         outs.store(i)
+        step()
         moe_in = tile[:, :width]
         terms = (
             (sum_in, slice(0, units), dot_tn(d_gate, moe_in)),
@@ -726,13 +781,153 @@
             else:
                 low = grad_in if total is sum_in else grad_down
                 low[at] = (total[at] + term).astype(BF16)
-        next(job, None)
+        step()
     run(job)
     for i in (tiles - 2, tiles - 1):
         outs.stored(i)
     sender.finish()
-    if not layer:
-        state["handed"]()
+    state["handed"]()
+
+
+def expert_back_sum_kernel(layer, pieces, rows, *refs):
+    refs = list(refs)
+
+    def take(count):
+        taken = refs[:count]
+        del refs[:count]
+        return taken
+
+    grads, (acts, mid, gates, pack0, pack1), own, other = take(pieces), take(5), take(3), take(3)
+    above = take(1)[0]
+    d_part, gain_term, router_term, grad_in, grad_down, *settled = take(7)
+    gate, up, down, sems, row_all, grad_all, act_all, hiddens, load_sems = take(9)
+    settle_refs = [take(SETTLE_SCRATCH) for _ in settled]
+    send, recv, buffer, *slots = refs
+    place = Place()
+    met = greet(neighbours(place))
+    sender = Sender(send, recv)
+    parts = [
+        settle_part(part, place, held[:2], above, mid, out, held[2:])
+        for part, (out, held) in enumerate(zip(settled, settle_refs))
+    ]
+    settling = in_turn([job for job, _ in parts])
+    weights = load_weights(layer, own, other, (gate, up, down), sems)
+    quarter = buffer.shape[3]
+    tile_rows = BLOCKS * quarter
+    tiles = rows.shape[0] // tile_rows
+    width = mid.shape[1]
+    units = gate.shape[0]
+
+    def loads(i):
+        at = pl.ds(i * tile_rows, tile_rows)
+        pairs = [(rows.at[at], row_all.at[at]), (acts.at[at], act_all.at[at])]
+        start = 0
+        for ref in grads:
+            pairs.append((ref.at[at], grad_all.at[at, pl.ds(start, ref.shape[1])]))
+            start += ref.shape[1]
+        return [pltpu.make_async_copy(*pair, load_sems.at[i, n]) for n, pair in enumerate(pairs)]
+
+    for i in range(tiles):
+        for load in loads(i):
+            load.start()
+    for copy in weights:
+        copy.wait()
+    met()
+    next(settling)
+    first_expert = 2 * lax.axis_index("expert")
+    for i in range(tiles):
+        if i in SETTLE_POINTS:
+            next(settling)
+        for load in loads(i):
+            load.wait()
+        at = slice(i * tile_rows, (i + 1) * tile_rows)
+        weight = gate_columns(row_all[at, width:], units // 2)
+        back = dot_nt(grad_all[at], down[...])
+        gate_act = act_all[at, :units].astype(F32)
+        up_act = act_all[at, units:].astype(F32)
+        sigmoid = 1.0 / (1.0 + jnp.exp(-gate_act))
+        silu = gate_act * sigmoid
+        hidden = silu * up_act
+        products = hidden * back
+        in_one = lax.broadcasted_iota(jnp.int32, products.shape, 1) < units // 2
+        one = jnp.sum(jnp.where(in_one, products, 0.0), axis=1, keepdims=True)
+        two = jnp.sum(jnp.where(in_one, 0.0, products), axis=1, keepdims=True)
+        lanes = lax.broadcasted_iota(jnp.int32, (products.shape[0], GATED), 1)
+        d_gates = jnp.where(lanes == first_expert, one, jnp.where(lanes == first_expert + 1, two, 0.0))
+        d_hidden = back * weight
+        d_gate = (d_hidden * up_act * sigmoid * (1.0 + gate_act * (1.0 - sigmoid))).astype(BF16)
+        d_up = (d_hidden * silu).astype(BF16)
+        act_all[at, :units] = d_gate
+        act_all[at, units:] = d_up
+        hiddens[at] = (hidden * weight).astype(BF16)
+        d_rows = dot_nn(d_gate, gate[...]) + dot_nn(d_up, up[...])
+        for n in range(BLOCKS):
+            block = i * BLOCKS + n
+            here = (block // (RING * RING), block // RING % RING, block % RING)
+            piece = slice(n * quarter, (n + 1) * quarter)
+            buffer[(*here, slice(None), slice(0, width))] = d_rows[piece].astype(BF16)
+            buffer[(*here, slice(None), slice(width, None))] = d_gates[piece].astype(BF16)
+
+    def products_job():
+        step = 2 * LANES
+        for target, source, inputs in ((grad_in, act_all, row_all), (grad_down, hiddens, grad_all)):
+            for start in range(0, target.shape[0], step):
+                size = min(step, target.shape[0] - start)
+                term = dot_tn(source[:, start : start + size], inputs[:, :width])
+                target[start : start + size] = term.astype(BF16)
+                yield
+
+    summing = reduce(place, sender, thirds(buffer), sort_slots(slots, 3, 3))
+    making = products_job()
+    for count in (2, 2, 1):
+        next(summing)
+        next(settling, None)
+        for _ in range(count):
+            next(making, None)
+    run(in_turn([summing, settling]))
+    run(making)
+    moe_back_rows(layer, place, sender, buffer, mid, gates, pack0, pack1, d_part, gain_term, router_term)
+    sender.finish()
+    for _, settler in parts:
+        settler.finish()
+
+
+def experts_back_sum(layer, rows_all, grads_all, acts, mid, gates, packs, own, other, above, expert_count):
+    quarter = rows_all.shape[3]
+    count = RING**3 * quarter
+    width = rows_all.shape[4] - GATED
+    units = 2 * own[0].shape[1]
+    grads = [g.reshape(count, g.shape[-1]) for g in grads_all]
+    tiles = count // (BLOCKS * quarter)
+    return pl.pallas_call(
+        functools.partial(expert_back_sum_kernel, layer, len(grads)),
+        name="experts_back_sum",
+        out_shape=(
+            jax.ShapeDtypeStruct((RING, quarter, width), BF16),
+            jax.ShapeDtypeStruct((1, width), F32),
+            jax.ShapeDtypeStruct((expert_count, width), F32),
+            jax.ShapeDtypeStruct((2 * units, width), BF16),
+            jax.ShapeDtypeStruct((units, width), BF16),
+            *[jax.ShapeDtypeStruct((RING, quarter, width // 2), BF16)] * 2,
+        ),
+        in_specs=[ANYWHERE] * (2 + len(grads)) + [IN_VMEM] * 4 + [ANYWHERE] * 7,
+        out_specs=(IN_VMEM,) * 7,
+        scratch_shapes=[pltpu.VMEM((units, width), BF16)] * 3
+        + [
+            pltpu.SemaphoreType.DMA((6,)),
+            pltpu.VMEM((count, width + GATED), BF16),
+            pltpu.VMEM((count, width), BF16),
+            pltpu.VMEM((count, 2 * units), BF16),
+            pltpu.VMEM((count, units), BF16),
+            pltpu.SemaphoreType.DMA((tiles, 2 + len(grads))),
+            *settle_scratch(above),
+            *settle_scratch(above),
+            *copy_sems(3 + SENDS),
+            pltpu.VMEM(rows_all.shape, BF16),
+            *third_slots(quarter, width + GATED),
+        ],
+        compiler_params=params(14 + layer, 62 << 20),
+    )(rows_all.reshape(count, width + GATED), *grads, acts, mid, gates, *packs, *own, *other, above)
 
 
 def experts_back(layer, rows_all, grads_all, acts, own, other, extra):
@@ -741,38 +936,24 @@
     width = rows_all.shape[4] - GATED
     units = 2 * own[0].shape[1]
     grads = [g.reshape(count, g.shape[-1]) for g in grads_all]
-    if layer:
-        partial, mid = extra
-        extra = (partial, mid)
-        extra_specs, made_specs = [ANYWHERE, IN_VMEM], (IN_VMEM,)
-        made = (jax.ShapeDtypeStruct((RING, quarter, width), BF16),)
-        scratch = [
-            *copy_sems(3 + SENDS),
-            pltpu.SemaphoreType.DMA((1,)),
-            pltpu.VMEM(partial.shape, BF16),
-            *third_slots(quarter, width),
-        ]
-    else:
-        factors, grads_one, dense = extra
-        first, second = gradient_shapes(dense)
-        normed, proj, heads, mids = factors
-        extra = (normed, proj, heads, mids, *grads_one)
-        extra_specs, made_specs = [ANYWHERE] * 6, (IN_VMEM, IN_VMEM, ANYWHERE, ANYWHERE)
-        made = (
-            jax.ShapeDtypeStruct(first[2:], BF16),
-            jax.ShapeDtypeStruct(second[2:], BF16),
-            jax.ShapeDtypeStruct(grads_one[0].shape, BF16),
-            jax.ShapeDtypeStruct(grads_one[1].shape, BF16),
-        )
-        scratch = [
-            *copy_sems(18),
-            pltpu.SemaphoreType.DMA((4,)),
-            *[pltpu.VMEM(f.shape, BF16) for f in factors],
-            pltpu.VMEM(first, BF16),
-            pltpu.VMEM(second, BF16),
-            *gradient_slots(first, second),
-            *copy_sems(2),
-        ]
+    products, grads_one, dense = extra
+    first, second = gradient_shapes(dense)
+    extra = (*products, *grads_one)
+    extra_specs, made_specs = [ANYWHERE] * 4, (IN_VMEM, IN_VMEM, ANYWHERE, ANYWHERE)
+    made = (
+        jax.ShapeDtypeStruct(first[2:], BF16),
+        jax.ShapeDtypeStruct(second[2:], BF16),
+        jax.ShapeDtypeStruct(grads_one[0].shape, BF16),
+        jax.ShapeDtypeStruct(grads_one[1].shape, BF16),
+    )
+    scratch = [
+        *copy_sems(GRADIENT_SENDS),
+        pltpu.SemaphoreType.DMA((2,)),
+        pltpu.VMEM(first, BF16),
+        pltpu.VMEM(second, BF16),
+        *gradient_slots(first, second),
+        *copy_sems(2),
+    ]
     out, *rest = pl.pallas_call(
         functools.partial(expert_back_kernel, layer, len(grads)),
         name="experts_back",
@@ -843,37 +1024,89 @@
 
 
 def attend_mix_kernel(
-    layer, rows, seg_column, seg_row, pack0, pack1, routes0, routes1, q0, k0, v0, o0, q1, k1, v1, o1,
-    attended, query_raw, key_raw, value_low, mid, gates, rows_all,
-    wq, wk, wv, wo, total, part, own, slots, sems, send, recv, local
+    layer, rows, seg_column, seg_row, pack0, routes0, *refs
 ):
+    refs = list(refs)
+
+    def take(count):
+        taken = refs[:count]
+        del refs[:count]
+        return taken
+
+    if layer:
+        (pack1, routes1), dense_own, dense_other = take(2), take(4), take(4)
+        attended, query_raw, key_raw, value_low, mid, gates, rows_all = take(7)
+    else:
+        dense_own, expert_own = take(4), take(3)
+        attended, query_raw, key_raw, value_low, mid, gates, rows_all, pack1, routes1 = take(9)
+        dense_other, expert_other = take(4), take(3)
+    wq, wk, wv, wo, total, part, own, slots, sems, send, recv, local = take(12)
     place = Place()
-    met = greet(neighbours(place))
+    section = place.section
+    peer = place.peer()
+    met = greet(neighbours(place) if layer else [peer, *neighbours(place)])
     dim = wk.shape[1]
     heads = wq.shape[1] // dim
     step = HEADS_STEP * dim
     steps = heads // HEADS_STEP
 
     def pieces(q, k, v, o):
-        columns = [q.at[:, pl.ds(i * step, step)] for i in range(steps)]
-        return [k, v, *columns, *[o.at[pl.ds(i * step, step)] for i in range(steps)]]
-
-    loads = pull(layer, pieces(q0, k0, v0, o0), pieces(q1, k1, v1, o1), pieces(wq, wk, wv, wo), sems)
+        made = [k, v]
+        for i in range(steps):
+            made += [q.at[:, pl.ds(i * step, step)], o.at[pl.ds(i * step, step)]]
+        return made
+
+    targets = pieces(wq, wk, wv, wo)
+    ours, theirs = pieces(*dense_own), pieces(*dense_other)
+    if layer:
+        loads = pull(layer, ours, theirs, targets, sems)
+
+        def arrive(i):
+            loads[i].wait()
+    else:
+        lower = section == 0
+        loads = [pltpu.make_async_copy(*pair, sems.at[i]) for i, pair in enumerate(zip(ours, targets))]
+        late = [pltpu.make_async_copy(*pair, sems.at[i]) for i, pair in enumerate(zip(theirs, targets))]
+
+        @pl.when(lower)
+        def _():
+            for load in loads:
+                load.start()
+
+        met()
+        pusher = Sender(*refs)
+        first = [pusher.send(pack0, pack1, peer), pusher.send(routes0.at[1 - section], routes1, peer)]
+        pushed = [pusher.send(*pair, peer) for pair in zip(ours, theirs)]
+        for copy in first:
+            copy.wait_recv()
+
+        def prefetch(i):
+            @pl.when(jnp.logical_not(lower))
+            def _():
+                pushed[i].wait_recv()
+                late[i].start()
+
+        def arrive(i):
+            if i + 1 < len(pushed):
+                prefetch(i + 1)
+            loads[i].wait()
+
+        prefetch(0)
     resid = rows[...].astype(F32)
     gain = of_layer(layer, pack0[PACK_ROUTER : PACK_ROUTER + 1], pack1[PACK_ROUTER : PACK_ROUTER + 1]).astype(F32)
     gains = of_layer(layer, pack0[PACK_ROUTER + 2 : PACK_ROUTER + 3], pack1[PACK_ROUTER + 2 : PACK_ROUTER + 3]).astype(F32)
     gain_query, gain_key = gains[:, :dim], gains[:, dim : 2 * dim]
     cosine, sine, allowed = tables(seg_column[...], seg_row[...], dim)
     normed = (resid * inverse_rms(resid) * gain).astype(BF16)
-    loads[0].wait()
+    arrive(0)
     raw = dot_nn(normed, wk[...])
     key_raw[...] = raw
     key = turn(raw * inverse_rms(raw) * gain_key, cosine, sine).astype(BF16)
-    loads[1].wait()
+    arrive(1)
     value = dot_nn(normed, wv[...]).astype(BF16)
     value_low[...] = value
     for i in range(steps):
-        loads[2 + i].wait()
+        arrive(2 + 2 * i)
         raws = dot_nn(normed, wq[:, i * step : (i + 1) * step])
         query_raw[:, i * step : (i + 1) * step] = raws
         for h in range(HEADS_STEP):
@@ -884,7 +1117,7 @@
             probs = (raised / jnp.sum(raised, axis=1, keepdims=True)).astype(BF16)
             at = i * step + h * dim
             attended[:, at : at + dim] = dot_nn(probs, value).astype(BF16)
-        loads[2 + steps + i].wait()
+        arrive(3 + 2 * i)
         piece = dot_nn(attended[:, i * step : (i + 1) * step], wo[i * step : (i + 1) * step])
         if i == 0:
             total[...] = piece
@@ -895,9 +1128,12 @@
         part[i] = total[i * quarter : (i + 1) * quarter].astype(BF16)
         total[i * quarter : (i + 1) * quarter] = resid[i * quarter : (i + 1) * quarter]
     sender = Sender(send, recv)
-    met()
+    if layer:
+        met()
     copies = send_x(place, sender, part, slots)
-    chosen = of_layer(layer, routes0[place.x], routes1[place.x])
+    if not layer:
+        pushed_experts = [pusher.send(*pair, peer) for pair in zip(expert_own, expert_other)]
+    chosen = of_layer(layer, routes0[section, place.x], routes1[place.x])
     lanes = lax.broadcasted_iota(jnp.int32, gates.shape, 1)
     named = chosen[:, 0:1] == lanes
     for i in range(1, chosen.shape[1]):
@@ -917,6 +1153,16 @@
     keep = pltpu.make_async_copy(own, rows_all.at[place.z, place.y, place.x], local)
     keep.start()
     run(gather(place, sender, thirds(rows_all), own, keep.wait))
+    if not layer:
+
+        @pl.when(lower)
+        def _():
+            for copy in pushed:
+                copy.wait_recv()
+
+        for copy in pushed_experts:
+            copy.wait_recv()
+        pusher.finish()
     sender.finish()
 
 
@@ -924,10 +1170,23 @@
     return [pltpu.VMEM(w.shape, BF16) for w in dense]
 
 
-def attend_mix(layer, rows, segs, packs, routes, own, other):
+def attend_mix(layer, rows, segs, pack, routes, own, other):
     count, width = rows.shape
     quarter = count // RING
     dim, inner = own[1].shape[1], own[0].shape[1]
+    pieces = 2 + 2 * (inner // dim // HEADS_STEP)
+
+    def like(array):
+        return jax.ShapeDtypeStruct(array.shape, array.dtype)
+
+    if layer:
+        swapped, swapped_specs, push = (), (), ()
+        inputs = (rows, *segs, pack[0], routes[0], pack[1], routes[1], *own, *other)
+    else:
+        swapped = (like(pack), jax.ShapeDtypeStruct(routes.shape[1:], routes.dtype), *map(like, own), *map(like, other))
+        swapped_specs = (IN_VMEM, IN_VMEM) + (ANYWHERE,) * 7
+        push = copy_sems(2 + pieces + 3)
+        inputs = (rows, *segs, pack, routes, *own, *other)
     return pl.pallas_call(
         functools.partial(attend_mix_kernel, layer),
         name="attend_mix",
@@ -939,21 +1198,23 @@
             jax.ShapeDtypeStruct((quarter, width), F32),
             jax.ShapeDtypeStruct((quarter, GATED), F32),
             jax.ShapeDtypeStruct((RING, RING, RING, quarter, width + GATED), BF16),
+            *swapped,
         ),
-        in_specs=[IN_VMEM] * 7 + [ANYWHERE] * 8,
-        out_specs=(IN_VMEM,) * 6 + (ANYWHERE,),
+        in_specs=[IN_VMEM] * (7 if layer else 5) + [ANYWHERE] * (8 if layer else 7),
+        out_specs=(IN_VMEM,) * 6 + (ANYWHERE,) + swapped_specs,
         scratch_shapes=[
             *weight_scratch(own),
             pltpu.VMEM((count, width), F32),
             pltpu.VMEM((RING, quarter, width), BF16),
             pltpu.VMEM((quarter, width + GATED), BF16),
             pltpu.VMEM((3, quarter, width), BF16),
-            pltpu.SemaphoreType.DMA((2 + 2 * (inner // dim // HEADS_STEP),)),
+            pltpu.SemaphoreType.DMA((pieces,)),
             *copy_sems(3 + SENDS),
             pltpu.SemaphoreType.DMA,
+            *push,
         ],
         compiler_params=params(1 + layer),
-    )(rows, *segs, *packs, *routes, *own, *other)
+    )(*inputs)
 
 
 SMALL = 48
@@ -966,32 +1227,57 @@
     return (RING, RING, width // blocks, proj), (RING, RING, inner // blocks, width)
 
 
-def gradient_plans(first, second):
-    return [(first, "yz", (0, first.shape[-1])), (second, "zy", (0, second.shape[-1]))]
+def gradient_plans(array):
+    one, two = cut(array.shape[-1], 2)
+    return [(array, "yz", one), (array, "zy", two)]
+
+
+GRADIENT_SENDS = 2 * 18
 
 
 def gradient_slots(first, second):
-    return slot_scratch([(first[2], 2, (0, first[3])), (second[2], 2, (0, second[3]))])
-
-
-def gradient_products(normed, proj, heads, mids, first, second):
-    lanes = 128
-
-    def output_blocks(i, _):
-        pair = dot_tn(heads[:, pl.ds(pl.multiple_of(i * lanes, lanes), lanes)], mids[...]).astype(BF16)
-        half = lanes // 2
+    scratch = []
+    for shape in (first, second):
+        one, two = cut(shape[3], 2)
+        scratch += slot_scratch([(shape[2], 2, one), (shape[2], 2, two)])
+    return scratch
+
+
+def gradient_reduces(place, sender, first, second, slots, beside=()):
+    return [
+        reduce(place, sender, gradient_plans(first), sort_slots(slots[:18], 2, 2)),
+        reduce(place, sender, gradient_plans(second), sort_slots(slots[18:], 2, 2), beside),
+    ]
+
+
+def gradient_gathers(place, sender, first, second, beside=()):
+    return [
+        gather(place, sender, gradient_plans(first)),
+        gather(place, sender, gradient_plans(second), None, None, beside),
+    ]
+
+
+LANES = 128
+
+
+def output_products(heads, mids, second):
+    def blocks(i, _):
+        pair = dot_tn(heads[:, pl.ds(pl.multiple_of(i * LANES, LANES), LANES)], mids[...]).astype(BF16)
         at = 2 * i
-        second[lax.div(at, RING), lax.rem(at, RING)] = pair[:half]
-        second[lax.div(at, RING), lax.rem(at, RING) + 1] = pair[half:]
+        second[lax.div(at, RING), lax.rem(at, RING)] = pair[: LANES // 2]
+        second[lax.div(at, RING), lax.rem(at, RING) + 1] = pair[LANES // 2 :]
         return 0
 
-    def input_blocks(i, _):
-        block = dot_tn(normed[:, pl.ds(pl.multiple_of(i * lanes, lanes), lanes)], proj[...])
+    lax.fori_loop(0, heads.shape[1] // LANES, blocks, 0)
+
+
+def input_products(normed, proj, first):
+    def blocks(i, _):
+        block = dot_tn(normed[:, pl.ds(pl.multiple_of(i * LANES, LANES), LANES)], proj[...])
         first[lax.div(i, RING), lax.rem(i, RING)] = block.astype(BF16)
         return 0
 
-    lax.fori_loop(0, heads.shape[1] // lanes, output_blocks, 0)
-    lax.fori_loop(0, normed.shape[1] // lanes, input_blocks, 0)
+    lax.fori_loop(0, normed.shape[1] // LANES, blocks, 0)
 
 
 def attend_back_kernel(
@@ -1003,7 +1289,7 @@
     extra = [refs.pop(0) for _ in range(4 if last else 0)]
     q0, k0, v0, o0, q1, k1, v1, o1, d_input, normed_both, d_proj, heads_both, d_mid_low, smalls = refs[:14]
     refs = refs[14:]
-    wide = [refs.pop(0) for _ in range(4 if last else 0)]
+    wide = [refs.pop(0) for _ in range(4 if last else 2)]
     wq, wk, wv, wo, total, d_mid, d_heads, part, own, slots, sems, send, recv, local, *side = refs
     place = Place()
     peer = place.peer()
@@ -1022,7 +1308,7 @@
             second[place.z, place.y] = second_own[...]
             yield
             met()
-            yield from gather(place, side_sender, gradient_plans(first, second))
+            yield from in_turn(gradient_gathers(place, side_sender, first, second))
 
         job = widen()
     dim = wk.shape[1]
@@ -1124,9 +1410,35 @@
         own[...] = d_rows
         keep = pltpu.make_async_copy(own, d_input.at[place.z, place.y, place.x], local)
         keep.start()
-        run(gather(place, sender, thirds(d_input), own, keep.wait))
+        spread = gather(place, sender, thirds(d_input), own, keep.wait)
+        for _ in range(3):
+            next(spread)
     handed()
     handed_small()
+    if not last:
+        owner = place.section == layer
+        products, copy_out = side[:2], side[2]
+        stores = [pltpu.make_async_copy(*pair, copy_out.at[i]) for i, pair in enumerate(zip(products, wide))]
+
+        @pl.when(owner)
+        def _():
+            output_products(heads_both, d_mid_low, products[1])
+
+        next(spread)
+
+        @pl.when(owner)
+        def _():
+            stores[1].start()
+            input_products(normed_both, d_proj, products[0])
+            stores[0].start()
+
+        run(spread)
+
+        @pl.when(owner)
+        def _():
+            for store in stores:
+                store.wait()
+
     sender.finish()
     if last:
         run(job)
@@ -1136,11 +1448,17 @@
 
 def attend_back(layer, rows, segs, packs, saved, upstream, d_part, terms, extra, own, other):
     last = layer == 0
-    wide, side = (), ()
+    first, second = gradient_shapes(own)
+    wide = tuple(jax.ShapeDtypeStruct(shape, BF16) for shape in (first, second))
+    side = (pltpu.VMEM(first, BF16), pltpu.VMEM(second, BF16), pltpu.SemaphoreType.DMA((2,)))
     if last:
-        first, second = gradient_shapes(own)
-        wide = tuple(jax.ShapeDtypeStruct(shape, BF16) for shape in (first, second, extra[2].shape, extra[3].shape))
-        side = (*copy_sems(18), *copy_sems(2))
+        shapes = (first, second, extra[2].shape, extra[3].shape)
+        wide = tuple(jax.ShapeDtypeStruct(shape, BF16) for shape in shapes)
+        side = (
+            *copy_sems(GRADIENT_SENDS),
+            *copy_sems(2),
+        )
+
     count, width = rows.shape
     quarter = count // RING
     dim, inner = own[1].shape[1], own[0].shape[1]
@@ -1158,7 +1476,7 @@
             *wide,
         ),
         in_specs=[IN_VMEM] * 13 + ([IN_VMEM] * 2 + [ANYWHERE] * 2 if last else []) + [ANYWHERE] * 8,
-        out_specs=(IN_VMEM if last else ANYWHERE,) + (IN_VMEM,) * (7 if last else 5) + (ANYWHERE,) * (2 if last else 0),
+        out_specs=(IN_VMEM if last else ANYWHERE,) + (IN_VMEM,) * (7 if last else 5) + (ANYWHERE,) * 2,
         scratch_shapes=[
             *weight_scratch(own),
             pltpu.VMEM((count, width), F32),
@@ -1177,7 +1495,7 @@
 
 
 def finish_kernel(
-    normed0, proj0, heads0, mids0, small0, small1, first_one, second_one, out0, out1, ig0, ig1,
+    normed0, proj0, heads0, mids0, small0, small1, first_one, second_one, out0, out1a, out1b, ig0, ig1,
     first, second, small_out, outputs, input_grads,
     first_sums, second_sums, normed, proj, heads, mids, terms, passing, small_slots, send, recv, flagged_send,
     flagged_recv, local, *slots
@@ -1196,12 +1514,17 @@
         pl.when(upper)(two.start)
         return one
 
-    pairs = ((small0, small1, terms), (out0, out1, outputs.at[place.section]), (ig0, ig1, input_grads.at[place.section]))
-    kept = [keep(i, *pair) for i, pair in enumerate(pairs)]
+    half = out1a.shape[2]
+    pairs = [(small0, small1, terms), (ig0, ig1, input_grads.at[place.section])]
+    halves_of = []
+    for part, above in enumerate((out1a, out1b)):
+        columns = pl.ds(part * half, half)
+        halves_of.append((out0.at[:, :, columns], above, outputs.at[place.section, :, :, columns]))
+    pairs += halves_of
     loads = ((normed0, normed), (proj0, proj), (heads0, heads), (mids0, mids))
-    loads = [pltpu.make_async_copy(*pair, local.at[3 + i]) for i, pair in enumerate(loads)]
+    loads = [pltpu.make_async_copy(*pair, local.at[4 + i]) for i, pair in enumerate(loads)]
     ready = [
-        pltpu.make_async_copy(*pair, local.at[7 + i]) for i, pair in enumerate(((first_one, first), (second_one, second)))
+        pltpu.make_async_copy(*pair, local.at[8 + i]) for i, pair in enumerate(((first_one, first), (second_one, second)))
     ]
 
     @pl.when(upper)
@@ -1215,10 +1538,10 @@
             copy.start()
         for copy in loads:
             copy.wait()
-        gradient_products(normed, proj, heads, mids, first_sums, second_sums)
-
-    for copy in kept:
-        copy.wait()
+        output_products(heads, mids, second_sums)
+
+    kept = [keep(i, *pair) for i, pair in enumerate(pairs)]
+    kept[0].wait()
     met()
     state = {}
 
@@ -1244,7 +1567,7 @@
 
     def swap_rows():
         state["late"] = [
-            sender.send_either(lower, out1, out0, outputs.at[place.section], peer),
+            *[sender.send_either(lower, high, low, target, peer) for low, high, target in halves_of],
             sender.send_either(lower, ig1, ig0, input_grads.at[place.section], peer),
         ]
         exchange(0, terms[0] + terms[1])
@@ -1252,8 +1575,10 @@
     def second_step():
         exchange(1, collect(0))
 
-    plans = gradient_plans(first_sums, second_sums)
-    run(reduce(place, reducer, plans, sort_slots(slots, 2, 2), (swap_rows, second_step)))
+    first_job, second_job = gradient_reduces(place, reducer, first_sums, second_sums, slots, (swap_rows, second_step))
+    next(second_job)
+    pl.when(lower)(lambda: input_products(normed, proj, first_sums))
+    run(in_turn([first_job, second_job]))
 
     @pl.when(lower)
     def _():
@@ -1261,9 +1586,11 @@
         second[place.z, place.y] = second_sums[place.z, place.y]
 
     beside = (lambda: exchange(2, collect(1)), small_last)
-    run(gather(place, reducer, gradient_plans(first, second), None, None, beside))
+    run(in_turn(gradient_gathers(place, reducer, first, second, beside)))
     for copy in state["late"]:
         copy.wait_recv()
+    for copy in kept[1:]:
+        copy.wait()
 
     @pl.when(upper)
     def _():
@@ -1288,7 +1615,7 @@
             jax.ShapeDtypeStruct(both, BF16),
             jax.ShapeDtypeStruct(both, BF16),
         ),
-        in_specs=[ANYWHERE] * 12,
+        in_specs=[ANYWHERE] * 13,
         out_specs=(IN_VMEM,) * 3 + (ANYWHERE,) * 2,
         scratch_shapes=[
             pltpu.VMEM(first, BF16),
@@ -1297,17 +1624,131 @@
             pltpu.VMEM(smalls[0].shape, F32),
             pltpu.VMEM(smalls[0].shape[1:], F32),
             pltpu.VMEM((3, 4, *smalls[0].shape[1:]), BF16),
-            *copy_sems(2 + 9),
-            *copy_sems(36),
-            pltpu.SemaphoreType.DMA((9,)),
+            *copy_sems(3 + 9),
+            *copy_sems(2 * GRADIENT_SENDS),
+            pltpu.SemaphoreType.DMA((10,)),
             *gradient_slots(first, second),
         ],
         compiler_params=params(9),
     )(*factors, *smalls, *ready, *outs, *input_grads)
 
 
-def swap(vector):
-    return lax.ppermute(vector, "section", [(0, 1), (1, 0)])
+STEPS = 8
+
+
+def widen_kernel(
+    section, first, second, gate_own0, gate_own1, up_own0, up_own1, gate_got0, gate_got1, up_got0, up_got1,
+    down_own0, down_own1, down_got0, down_got1, small, outputs_in, d_inputs_in,
+    query, key, value, output, gate, up, down, router, gain_moe, gain_attn, gain_query, gain_key, outputs, d_inputs
+):
+    inner, dim = query.shape[1], key.shape[1]
+    query[...] = first[:, :inner].astype(F32)
+    key[...] = first[:, inner : inner + dim].astype(F32)
+    value[...] = first[:, inner + dim :].astype(F32)
+    output[...] = second[...].astype(F32)
+    lower = section[0] == 0
+
+    def either(low, high):
+        return jnp.where(lower, low[...].astype(F32), high[...].astype(F32))
+
+    gate[...] = either(gate_own0, gate_own1) + either(gate_got0, gate_got1)
+    up[...] = either(up_own0, up_own1) + either(up_got0, up_got1)
+    down[...] = either(down_own0, down_own1) + either(down_got0, down_got1)
+    outputs[...] = outputs_in[...]
+    d_inputs[...] = d_inputs_in[...].astype(F32)
+
+    @pl.when(pl.program_id(0) == 0)
+    def _():
+        count = router.shape[0]
+        router[...] = small[:count]
+        gain_moe[...] = small[count : count + 1]
+        gain_attn[...] = small[count + 1 : count + 2]
+        gain_query[...] = small[count + 2 : count + 3, :dim]
+        gain_key[...] = small[count + 2 : count + 3, dim : 2 * dim]
+
+
+def widen(section, first, second, expert_grads, small, outputs, d_inputs, dim, expert_count):
+    (in0, down0, got_in0, got_down0), (in1, down1, got_in1, got_down1) = expert_grads
+    width = second.shape[1]
+    inner = first.shape[1] - 2 * dim
+    units = down0.shape[0]
+
+    def rows(count, columns):
+        return pl.BlockSpec((count // STEPS, columns), lambda i, section: (i, 0))
+
+    def either(ahead=0):
+        block = (units // STEPS, width)
+        return [
+            pl.BlockSpec(block, lambda i, section: (jnp.where(section[0] == 0, ahead + i, ahead), 0)),
+            pl.BlockSpec(block, lambda i, section: (jnp.where(section[0] == 1, ahead + i, ahead), 0)),
+        ]
+
+    def whole(*shape):
+        return pl.BlockSpec(shape, lambda i, section: (0,) * len(shape))
+
+    def slab(array):
+        return pl.BlockSpec((*array.shape[:-1], width // STEPS), lambda i, section: (0, 0, 0, i))
+
+    def shape(*dims):
+        return jax.ShapeDtypeStruct(dims, F32)
+
+    return pl.pallas_call(
+        widen_kernel,
+        name="widen",
+        out_shape=(
+            shape(width, inner),
+            shape(width, dim),
+            shape(width, dim),
+            shape(*second.shape),
+            shape(units, width),
+            shape(units, width),
+            shape(units, width),
+            shape(expert_count, width),
+            shape(1, width),
+            shape(1, width),
+            shape(1, dim),
+            shape(1, dim),
+            jax.ShapeDtypeStruct(outputs.shape, BF16),
+            shape(*d_inputs.shape),
+        ),
+        grid_spec=pltpu.PrefetchScalarGridSpec(
+            num_scalar_prefetch=1,
+            grid=(STEPS,),
+            in_specs=[
+                rows(width, first.shape[1]),
+                rows(second.shape[0], width),
+                *either(),
+                *either(STEPS),
+                *either(),
+                *either(STEPS),
+                *either(),
+                *either(),
+                whole(*small.shape),
+                slab(outputs),
+                slab(d_inputs),
+            ],
+            out_specs=(
+                rows(width, inner),
+                rows(width, dim),
+                rows(width, dim),
+                rows(second.shape[0], width),
+                rows(units, width),
+                rows(units, width),
+                rows(units, width),
+                whole(expert_count, width),
+                whole(1, width),
+                whole(1, width),
+                whole(1, dim),
+                whole(1, dim),
+                slab(outputs),
+                slab(d_inputs),
+            ),
+        ),
+        compiler_params=pltpu.CompilerParams(vmem_limit_bytes=VMEM_LIMIT),
+    )(
+        section[None], first, second, in0, in1, in0, in1, got_in0, got_in1, got_in0, got_in1,
+        down0, down1, got_down0, got_down1, small, outputs, d_inputs,
+    )
 
 
 def body(
@@ -1329,7 +1770,6 @@
     w_down,
 ):
     section = lax.axis_index("section")
-    lower = section == 0
     _, group_rows, width = block_input.shape
     expert_count = w_router.shape[2]
     quarter = group_rows // RING
@@ -1346,13 +1786,6 @@
         ],
         axis=0,
     )
-    routes_own = lax.dynamic_index_in_dim(routes[0], section, 0, keepdims=False)
-    routes_other = swap(lax.dynamic_index_in_dim(routes[0], 1 - section, 0, keepdims=False))
-    packs = (pack_own, swap(pack_own))
-    dense_other = tuple(swap(w) for w in dense_own)
-    expert_other = tuple(swap(w) for w in expert_own)
-    chosen = tuple(r.reshape(RING, quarter, r.shape[-1]) for r in (routes_own, routes_other))
-
     def pick(array):
         return lax.dynamic_index_in_dim(array, section, 0, keepdims=False)
 
@@ -1362,27 +1795,34 @@
     segment = pick(segments)
     segs = (segment.reshape(group_rows, 1), segment.reshape(1, group_rows))
 
+    routes = routes[0].reshape(2, RING, quarter, routes.shape[-1])
     rows_in = pick(block_input)
     upstream = quarters(pick(cotangent))
-    edge = 2 * GATED * ((width // GATED) // 3)
-    shared = (upstream[:, :, :edge], upstream[:, :, edge:])
+    shared = (upstream[:, :, : width // 2], upstream[:, :, width // 2 :])
     saved, layer_ins, outs, grads_all = [], [], [], []
     for layer in range(2):
         layer_ins.append(rows_in)
-        *attn_saved, mid, gates, rows_all = attend_mix(layer, rows_in, segs, packs, chosen, dense_own, dense_other)
-        partial, acts, spread = experts(layer, rows_all, shared[layer], expert_own, expert_other)
+        if layer == 0:
+            made = attend_mix(layer, rows_in, segs, pack_own, routes, dense_own, expert_own)
+            packs, routes_other = (pack_own, made[7]), made[8]
+            dense_other, expert_other = made[9:13], made[13:]
+        else:
+            made = attend_mix(layer, rows_in, segs, packs, (routes, routes_other), dense_own, dense_other)
+        attn_saved, (mid, gates, rows_all) = made[:4], made[4:7]
+        made, acts, spread = experts(layer, rows_all, shared[layer], mid, expert_own, expert_other)
         grads_all.append(spread)
         saved.append((attn_saved, mid, gates, rows_all, acts))
         if layer == 0:
-            out = settle_layer(partial, mid)
-            rows_in = out.reshape(group_rows, width)
-            outs.append(out)
+            rows_in = made.reshape(group_rows, width)
+            outs.append(made)
 
     attn_saved, mid, gates, rows_all, acts = saved[1]
-    partial, *grads_one, out = experts_back(1, rows_all, grads_all, acts, expert_own, expert_other, (partial, mid))
-    outs.append(out)
-    d_part, *terms = moe_back(1, partial, mid, gates, packs, expert_count)
-    d_all, *factors_one, smalls_one = attend_back(
+    d_part, *terms, grad_in, grad_down, out_low, out_high = experts_back_sum(
+        1, rows_all, grads_all, acts, mid, gates, packs, expert_own, expert_other, made, expert_count
+    )
+    outs += [out_low, out_high]
+    grads_one = (grad_in, grad_down)
+    d_all, *_, smalls_one, products_first, products_second = attend_back(
         1, layer_ins[1], segs, packs, attn_saved, upstream, d_part, terms[::-1], (), dense_own, dense_other
     )
     upstream = lax.dynamic_index_in_dim(
@@ -1391,7 +1831,7 @@
     input_grads = [None, upstream]
     attn_saved, mid, gates, rows_all, acts = saved[0]
     partial, *grads_zero, first_own, second_own, got_in_one, got_down_one = experts_back(
-        0, rows_all, [d_all], acts, expert_own, expert_other, (factors_one, grads_one, dense_own)
+        0, rows_all, [d_all], acts, expert_own, expert_other, ((products_first, products_second), grads_one, dense_own)
     )
     d_part, *terms = moe_back(0, partial, mid, gates, packs, expert_count)
     input_grads[0], *factors_zero, smalls_zero, first_one, second_one, got_in_zero, got_down_zero = attend_back(
@@ -1402,33 +1842,30 @@
     first, second, small, outputs, d_inputs = finish(
         factors_zero, (smalls_zero, smalls_one), (first_one, second_one), outs, input_grads
     )
-    inner = w_query.shape[2]
-    projections = first.reshape(width, first.shape[-1]).astype(F32)[None]
-
-    def total(index):
-        mine, theirs = [
-            jnp.where(lower, expert_grads[0][i], expert_grads[1][i]).astype(F32) for i in (index, index + 2)
-        ]
-        return mine + theirs
-
-    grad_in, grad_down = total(0), total(1)
+    query, key, value, output, gate, up, down, router, gain_moe, gain_attn, gain_query, gain_key, outputs, d_inputs = widen(
+        section, first.reshape(width, first.shape[-1]), second.reshape(-1, width), expert_grads, small, outputs, d_inputs,
+        dim, expert_count,
+    )
     units = w_gate.shape[3]
-    grad_in = grad_in.reshape(2, 2, units, width)
+
+    def by_expert(array):
+        return array.reshape(1, 2, units, width)
+
     return (
         outputs.reshape(1, 2, group_rows, width),
-        d_inputs.astype(F32).reshape(1, 2, group_rows, width),
-        small[33:34],
-        projections[:, :, :inner],
-        projections[:, :, inner : inner + dim],
-        projections[:, :, inner + dim :],
-        small[34:35, :dim],
-        small[34:35, dim : 2 * dim],
-        second.reshape(inner, width).astype(F32)[None],
-        small[32:33],
-        small[:expert_count].T[None],
-        jnp.swapaxes(grad_in[0], 1, 2)[None],
-        jnp.swapaxes(grad_in[1], 1, 2)[None],
-        grad_down.reshape(1, 2, units, width),
+        d_inputs.reshape(1, 2, group_rows, width),
+        gain_attn,
+        query[None],
+        key[None],
+        value[None],
+        gain_query,
+        gain_key,
+        output[None],
+        gain_moe,
+        router.T[None],
+        jnp.swapaxes(by_expert(gate), 2, 3),
+        jnp.swapaxes(by_expert(up), 2, 3),
+        by_expert(down),
     )
 
 

time: 639 us -> 567 us (0.89)
  Pallas kernels: 576 us -> 546 us
  local copies, waits for them, and re-layouts: 32.2 us -> 7.86 us
  other arithmetic: 13.4 us -> 2.48 us
  waiting for transfers between devices: 10.8 us -> 0 us
    pallas_call x3 -> x4, Pallas kernels: 114 us -> 196 us  [the longest x2 92.5 us: experts(): pl.pallas_call(functools.partial(expert_kernel, layer), name='experts' if...]
    pallas_call x2 -> x1, Pallas kernels: 74.5 us -> 28.3 us  [experts_back(): pl.pallas_call(functools.partial(expert_back_kernel, layer, len(grads)),...]
    pallas_call x2 -> x1, Pallas kernels: 79.6 us -> 43.6 us  [moe_back(): pl.pallas_call(functools.partial(moe_back_kernel, layer), name='moe_back'...]
    pallas_call x1, Pallas kernels: 101 us -> 80.3 us  [finish(): pl.pallas_call(finish_kernel, name='finish', out_shape=(jax.ShapeDtypeStr...]
    slice x7 -> x1, local copies, waits for them, and re-layouts: 18.1 us -> 0.85 us  [body(): shared = (upstream[:, :, :width // 2], upstream[:, :, width // 2:])]
    ppermute x9 -> x0, waiting for transfers between devices: 10.8 us -> none  [swap(): return lax.ppermute(vector, 'section', [(0, 1), (1, 0)])]
    pallas_call x2, Pallas kernels: 101 us -> 92.5 us  [attend_back(): pl.pallas_call(functools.partial(attend_back_kernel, layer), name='attend...]
  transfers between devices with their start and end apart: 9 -> 0, of which waited for: 2 -> 0; matrix products, arithmetic and copies ran while one was open for 1% -> 0% of each run, Pallas kernels for 9% -> 0%
where the time goes in v3:
time: 567 us; the launch traced here: 558 us
  Pallas kernels  546 us (96%)
  local copies, waits for them, and re-layouts  7.86 us (1%)
    pallas_call x2, Pallas kernels, attend_mix(): pl.pallas_call(functools.partial(attend_mix_kernel, layer), name='attend_...  106 us
    pallas_call x2, Pallas kernels, attend_back(): pl.pallas_call(functools.partial(attend_back_kernel, layer), name='attend...  92.5 us
    pallas_call x2, Pallas kernels, experts(): pl.pallas_call(functools.partial(expert_kernel, layer), name='experts' if...  92.5 us
    pallas_call x1, Pallas kernels, experts_back_sum(): pl.pallas_call(functools.partial(expert_back_sum_kernel, layer, len(grads...  84.1 us
    pallas_call x1, Pallas kernels, finish(): pl.pallas_call(finish_kernel, name='finish', out_shape=(jax.ShapeDtypeStr...  80.3 us
    pallas_call x1, Pallas kernels, moe_back(): pl.pallas_call(functools.partial(moe_back_kernel, layer), name='moe_back'...  43.6 us
    pallas_call x1, Pallas kernels, experts_back(): pl.pallas_call(functools.partial(expert_back_kernel, layer, len(grads)),...  28.3 us
    pallas_call x1, Pallas kernels, widen(): pl.pallas_call(widen_kernel, name='widen', out_shape=(shape(width, inner)...  18.9 us

profile of v3, /device:TPU:0, one launch (start us, length us, event | category | flops | bytes accessed | tf_op | source)
XLA Modules:
  0.0 557.6 jit_solution(9993227198135750559)
XLA Ops:
  0.6 0.0 copy-start
  0.7 1.2 fusion.10
  1.9 0.7 copy.34.seg_column
  2.6 0.7 fusion.9
  3.3 1.5 copy.30
  4.8 0.0 copy-done
  4.8 0.8 dynamic-slice_bitcast_fusion.1.rows
  5.5 1.0 constant_dynamic-slice_fusion
  6.6 0.0 copy-start.2
  6.6 0.9 fusion.12
  7.4 1.8 fusion.3.pack0.refs_5_
  9.2 57.4 %attend_mix.2 = (bf16[96,1024]{1,0:T(8,128)(2,1)}, f32[96,1024]{1,0:T(8,128)}, f32[96,128]{1,0:T(8,128)}, bf16[96,128]{1,0:T(8,128)(2,1)}, f32[24,2048]{1,0:T(8,...) custom-call(bf16[96,2048]{1,0:T(8,128)(2,1)} %dynamic-slice_bitcast_, ...), custom_call_target="tpu_custom_call" | custom-call | tf_op jit(solution)/shard_map/attend_mix/pallas_call | solution.py:1190
  66.6 66.5 %experts_settle.1 = (bf16[4,24,2048]{2,1,0:T(8,128)(2,1)}, bf16[1536,768]{1,0:T(8,128)(2,1)}, bf16[4,4,4,24,1024]{4,3,2,1,0:T(8,128)(2,1)}) custom-call(bf16[1536,2176]{1,0:T(8,128)(2,1)} %bitcast.75, bf16[4,24,1024]{2,1,0:T(8,128)(2,1)} %get-tuple-element.173.shared, f32[24,2048]{1,0:T(8,128)} %get-tuple-element.99.refs_0_.mid, ...), custom_call_target="tpu_custom_call" | custom-call | tf_op jit(solution)/shard_map/experts_settle/pallas_call | solution.py:665
  133.1 48.4 %attend_mix.3 = (bf16[96,1024]{1,0:T(8,128)(2,1)}, f32[96,1024]{1,0:T(8,128)}, f32[96,128]{1,0:T(8,128)}, bf16[96,128]{1,0:T(8,128)(2,1)}, f32[24,2048]{1,0:T(8,...) custom-call(bf16[96,2048]{1,0:T(8,128)(2,1)} %bitcast.95, s32[96,1]{1,0:T(8,128)} %copy.34.seg_column, ...), custom_call_target="tpu_custom_call" | custom-call | tf_op jit(solution)/shard_map/attend_mix/pallas_call | solution.py:1190
  181.6 26.0 %experts.1 = (bf16[1536,2048]{1,0:T(8,128)(2,1)}, bf16[1536,768]{1,0:T(8,128)(2,1)}, bf16[4,4,4,24,1024]{4,3,2,1,0:T(8,128)(2,1)}) custom-call(bf16[1536,2176]{1,0:T(8,128)(2,1)} %bitcast.77, bf16[4,24,1024]{2,1,0:T(8,128)(2,1)} %get-tuple-element.172.shared, bf16[2,192,2048]{2,1,0:T(8,128)(2,1)} %bitcast.62, bf16[2,192,2048]{2,1,0:T(8,128)(2,1)} %bitcast.67, ...), custom_call_target="tpu_custom_call" | custom-call | tf_op jit(solution)/shard_map/experts/pallas_call | solution.py:665
  207.5 84.1 %experts_back_sum.1 = (bf16[4,24,2048]{2,1,0:T(8,128)(2,1)}, f32[1,2048]{1,0:T(1,128)}, f32[32,2048]{1,0:T(8,128)}, bf16[768,2048]{1,0:T(8,128)(2,1)}, bf16[384,...) custom-call(bf16[1536,2176]{1,0:T(8,128)(2,1)} %bitcast.78, ...), custom_call_target="tpu_custom_call" | custom-call | tf_op jit(solution)/shard_map/experts_back_sum/pallas_call | solution.py:902
  291.7 49.5 %attend_back.1 = (bf16[4,4,4,24,2048]{4,3,2,1,0:T(8,128)(2,1)}, bf16[192,2048]{1,0:T(8,128)(2,1)}, bf16[192,1280]{1,0:T(8,128)(2,1)}, bf16[192,1024]{1,0:T(8,128...) custom-call(bf16[96,2048]{1,0:T(8,128)(2,1)} %bitcast.96, ...), custom_call_target="tpu_custom_call" | custom-call | tf_op jit(solution)/shard_map/attend_back/pallas_call | solution.py:1466
  341.2 28.3 %experts_back.1 = (bf16[1536,2176]{1,0:T(8,128)(2,1)}, bf16[768,2048]{1,0:T(8,128)(2,1)}, bf16[384,2048]{1,0:T(8,128)(2,1)}, bf16[128,1280]{1,0:T(8,128)(2,1)}, ...) custom-call(bf16[1536,2176]{1,0:T(8,128)(2,1)} %bitcast.76, ...), custom_call_target="tpu_custom_call" | custom-call | tf_op jit(solution)/shard_map/experts_back/pallas_call | solution.py:957
  369.6 43.6 %moe_back.1 = (bf16[4,24,2048]{2,1,0:T(8,128)(2,1)}, f32[1,2048]{1,0:T(1,128)}, f32[32,2048]{1,0:T(8,128)}) custom-call(bf16[4,4,4,24,2176]{4,3,2,1,0:T(8,128)(2,1)} %bitcast.89, f32[24,2048]{1,0:T(8,128)} %get-tuple-element.99.refs_0_.mid, f32[24,128]{1,0:T(8,128)} %get-tuple-element.130.gates, bf16[144,2048]{1,0:T(8,128)(2,1)} %fusion.3.pack0.refs_5_, ...), custom_call_target="tpu_custom_call" | custom-call | tf_op jit(solution)/shard_map/moe_back/pallas_call | solution.py:466
  413.2 1.8 dynamic-slice_bitcast_fusion.upstream.ig1
  415.0 43.0 %attend_back_last.1 = (bf16[4,24,2048]{2,1,0:T(8,128)(2,1)}, bf16[192,2048]{1,0:T(8,128)(2,1)}, bf16[192,1280]{1,0:T(8,128)(2,1)}, bf16[192,1024]{1,0:T(8,128)(2...) custom-call(bf16[96,2048]{1,0:T(8,128)(2,1)} %dynamic-slice_bitcast_, ...), custom_call_target="tpu_custom_call" | custom-call | tf_op jit(solution)/shard_map/attend_back_last/pallas_call | solution.py:1466
  458.0 80.3 %finish.1 = (bf16[4,4,128,1280]{3,2,1,0:T(8,128)(2,1)}, bf16[4,4,64,2048]{3,2,1,0:T(8,128)(2,1)}, f32[48,2048]{1,0:T(8,128)}, bf16[2,4,24,2048]{3,2,1,0:T(8,128)(2,1)}, bf16[2,4,24,2048]{3,2,1,0:T(8,128)(2,1)}) custom-call(bf16[192,2048]{1,0:T(8,128)(2,1)} %get-tuple-element.138.normed0, bf16[192,1280]{1,0:T(8,128)(2,1)} %get-tuple-element.139.proj0, ...), custom_call_target="tpu_custom_call" | custom-call | tf_op jit(solution)/shard_map/finish/pallas_call | solution.py:1608
  538.3 0.0 copy-start.1
  538.3 18.9 %widen.1 = (f32[2048,1024]{1,0:T(8,128)}, f32[2048,128]{1,0:T(8,128)}, f32[2048,128]{1,0:T(8,128)}, f32[1024,2048]{1,0:T(8,128)}, f32[384,2048]{1,0:T(8,128)}, /...) custom-call(s32[1]{0:T(128)} %bitcast.section, ...), custom_call_target="tpu_custom_call" | custom-call | tf_op jit(solution)/shard_map/widen/pallas_call | solution.py:1695
  (2 shorter events, 0.0 us)
Async XLA Ops:
  0.6 4.1 copy-start
  6.6 60.1 %copy-start.2 = (bf16[1,96,2048]{2,1,0:T(8,128)(2,1)}, bf16[1,96,2048]{2,1,0:T(8,128)(2,1)S(1)}, u32[]{:S(2)}) copy-start(bf16[1,96,2048]{2,1,0:T(8,128)(2,1)S(1)} %constant_dynamic-slice_fusion) | copy-start | bytes 1179652
  538.3 18.9 %copy-start.1 = (bf16[2,96,2048]{2,1,0:T(8,128)(2,1)S(1)}, bf16[2,96,2048]{2,1,0:T(8,128)(2,1)}, u32[]{:S(2)}) copy-start(bf16[2,96,2048]{2,1,0:T(8,128)(2,1)} %param.16) | copy-start | bytes 2359300

commit v4 on v3

--- a/solution.py
+++ b/solution.py
@@ -565,125 +565,7 @@
     return scratch
 
 
-SHARE_POINTS = (2, 5, 10)
 BLOCKS = 8
-
-
-def expert_kernel(layer, rows, shared, *refs):
-    refs = list(refs)
-
-    def take(count):
-        taken = refs[:count]
-        del refs[:count]
-        return taken
-
-    mid = take(0 if layer else 1)
-    own, other, (out, acts, spread), (gate, up, down, sems) = take(3), take(3), take(3), take(4)
-    row_slots, row_sems, act_slots, act_sems, send, recv, local = take(7)
-    place = Place()
-    met = greet(neighbours(place))
-    sharer = Sender(send, recv)
-    width = gate.shape[1]
-    units = gate.shape[0]
-    weights = load_weights(layer, own, other, (gate, up, down), sems)
-    keep = pltpu.make_async_copy(shared.at[place.x], spread.at[place.z, place.y, place.x], local)
-    keep.start()
-    ins, kept = Stream([rows], row_slots, row_sems), Stream([acts], act_slots, act_sems)
-    tile_rows = row_slots.shape[1]
-    tiles = rows.shape[0] // tile_rows
-    ins.fetch(0)
-    if layer:
-        out_slots, out_sems = refs
-        outs = Stream([out], out_slots, out_sems)
-    else:
-        buffer, *slots = refs[2:]
-        quarter = buffer.shape[3]
-    met()
-    sharing = gather(place, sharer, thirds(spread), shared.at[place.x], keep.wait)
-    next(sharing)
-    step = paced(sharing, SHARE_POINTS)
-    for i in range(tiles):
-        if i + 1 < tiles:
-            ins.fetch(i + 1)
-        tile = ins.fetched(i)
-        if i == 0:
-            for copy in weights:
-                copy.wait()
-        moe_in = tile[:, :width]
-        gate_act = dot_nt(moe_in, gate[...])
-        up_act = dot_nt(moe_in, up[...])
-        hidden = gate_act / (1.0 + jnp.exp(-gate_act)) * up_act
-        hidden = hidden * gate_columns(tile[:, width:], units // 2)
-        step()
-        if i >= 2:
-            kept.stored(i - 2)
-        act_slots[i % 2, :, :units] = gate_act.astype(BF16)
-        act_slots[i % 2, :, units:] = up_act.astype(BF16)
-        kept.store(i)
-        made = dot_nn(hidden.astype(BF16), down[...])
-        if layer:
-            if i >= 2:
-                outs.stored(i - 2)
-            out_slots[i % 2] = made.astype(BF16)
-            outs.store(i)
-        else:
-            for n in range(BLOCKS):
-                block = i * BLOCKS + n
-                here = (block // (RING * RING), block // RING % RING, block % RING)
-                buffer[here] = made[n * quarter : (n + 1) * quarter].astype(BF16)
-        step()
-    if layer:
-        run(sharing)
-        for i in (tiles - 2, tiles - 1):
-            outs.stored(i)
-    else:
-        sender = Sender(*refs[:2])
-        run(in_turn([settle_job(place, sender, None, buffer, slots, mid[0], out), sharing]))
-        sender.finish()
-    for i in (tiles - 2, tiles - 1):
-        kept.stored(i)
-    sharer.finish()
-
-
-def experts(layer, rows_all, shared, mid, own, other):
-    quarter = rows_all.shape[3]
-    count = RING**3 * quarter
-    width = rows_all.shape[4] - GATED
-    units = 2 * own[0].shape[1]
-    rows = rows_all.reshape(count, width + GATED)
-    tile = TILE if layer else BLOCKS * quarter
-    if layer:
-        mids, out_shape, out_spec = (), (count, width), ANYWHERE
-        tail = stream_scratch((width,))
-    else:
-        mids, out_shape, out_spec = (mid,), (RING, quarter, width), IN_VMEM
-        tail = [
-            *copy_sems(3 + SENDS),
-            pltpu.VMEM((*rows_all.shape[:4], width), BF16),
-            *third_slots(quarter, width),
-        ]
-    out, acts, spread = pl.pallas_call(
-        functools.partial(expert_kernel, layer),
-        name="experts" if layer else "experts_settle",
-        out_shape=(
-            jax.ShapeDtypeStruct(out_shape, BF16),
-            jax.ShapeDtypeStruct((count, 2 * units), BF16),
-            jax.ShapeDtypeStruct((RING, RING, RING, quarter, shared.shape[2]), BF16),
-        ),
-        in_specs=[ANYWHERE, IN_VMEM] + [IN_VMEM] * len(mids) + [ANYWHERE] * 6,
-        out_specs=(out_spec, ANYWHERE, ANYWHERE),
-        scratch_shapes=[pltpu.VMEM((units, width), BF16)] * 3
-        + [pltpu.SemaphoreType.DMA((6,))]
-        + stream_scratch((width + GATED, 2 * units), tile=tile)
-        + [*copy_sems(SENDS), pltpu.SemaphoreType.DMA]
-        + tail,
-        compiler_params=params(10 + layer),
-    )(rows, shared, *mids, *own, *other)
-    if layer:
-        out = out.reshape(*rows_all.shape[:4], width)
-    return out, acts, spread
-
-
 SETTLE_POINTS = (3, 6)
 SUM_POINTS = (4, 9)
 
@@ -799,7 +681,7 @@
 
     grads, (acts, mid, gates, pack0, pack1), own, other = take(pieces), take(5), take(3), take(3)
     above = take(1)[0]
-    d_part, gain_term, router_term, grad_in, grad_down, *settled = take(7)
+    d_part, gain_term, router_term, grad_in, grad_down, *settled = take(6)
     gate, up, down, sems, row_all, grad_all, act_all, hiddens, load_sems = take(9)
     settle_refs = [take(SETTLE_SCRATCH) for _ in settled]
     send, recv, buffer, *slots = refs
@@ -908,10 +790,10 @@
             jax.ShapeDtypeStruct((expert_count, width), F32),
             jax.ShapeDtypeStruct((2 * units, width), BF16),
             jax.ShapeDtypeStruct((units, width), BF16),
-            *[jax.ShapeDtypeStruct((RING, quarter, width // 2), BF16)] * 2,
+            jax.ShapeDtypeStruct((RING, quarter, width // 2), BF16),
         ),
         in_specs=[ANYWHERE] * (2 + len(grads)) + [IN_VMEM] * 4 + [ANYWHERE] * 7,
-        out_specs=(IN_VMEM,) * 7,
+        out_specs=(IN_VMEM,) * 6,
         scratch_shapes=[pltpu.VMEM((units, width), BF16)] * 3
         + [
             pltpu.SemaphoreType.DMA((6,)),
@@ -921,12 +803,11 @@
             pltpu.VMEM((count, units), BF16),
             pltpu.SemaphoreType.DMA((tiles, 2 + len(grads))),
             *settle_scratch(above),
-            *settle_scratch(above),
             *copy_sems(3 + SENDS),
             pltpu.VMEM(rows_all.shape, BF16),
             *third_slots(quarter, width + GATED),
         ],
-        compiler_params=params(14 + layer, 62 << 20),
+        compiler_params=params(14 + layer),
     )(rows_all.reshape(count, width + GATED), *grads, acts, mid, gates, *packs, *own, *other, above)
 
 
@@ -996,10 +877,12 @@
     return jnp.where(lax.axis_index("section") == layer, own, other)
 
 
-def tables(seg_column, seg_row, dim):
-    rows = seg_column.shape[0]
+def tables(seg_row, dim):
+    rows = seg_row.shape[1]
     at_row = lax.broadcasted_iota(jnp.int32, (rows, rows), 0)
     at_column = lax.broadcasted_iota(jnp.int32, (rows, rows), 1)
+    seg_row = seg_row.astype(F32)
+    seg_column = jnp.sum(jnp.where(at_row == at_column, seg_row, 0.0), axis=1, keepdims=True)
     earlier = jnp.sum((seg_row < seg_column).astype(F32), axis=1, keepdims=True)
     position = lax.broadcasted_iota(jnp.int32, (rows, dim), 0).astype(F32) - earlier
     lane = lax.broadcasted_iota(jnp.int32, (rows, dim), 1)
@@ -1021,10 +904,25 @@
 PACK_ROUTER = 128
 PACK_ROWS = 144
 HEADS_STEP = 2
-
-
-def attend_mix_kernel(
-    layer, rows, seg_column, seg_row, pack0, routes0, *refs
+SETTLE_BESIDE = (0, 3)
+WIDEN_POINTS = (0, 1, 3)
+
+
+def fill_pack(pack, router, norm_attn, norm_moe, norm_query, norm_key):
+    count, width = router.shape
+    pack[:count] = router[...]
+    pack[count:PACK_ROUTER] = jnp.zeros((PACK_ROUTER - count, width), BF16)
+    heads = [norm_query[...].astype(F32), norm_key[...].astype(F32)]
+    rest = width - sum(h.shape[1] for h in heads)
+    heads = jnp.concatenate([*heads, jnp.zeros((1, rest), F32)], axis=1)
+    row = lax.broadcasted_iota(jnp.int32, (PACK_ROWS - PACK_ROUTER, width), 0)
+    gains = jnp.where(row == 2, heads, 0.0)
+    gains = jnp.where(row == 1, norm_moe[...].astype(F32), gains)
+    pack[PACK_ROUTER:] = jnp.where(row == 0, norm_attn[...].astype(F32), gains).astype(BF16)
+
+
+def forward_kernel(
+    layer, rows, segments, routes0, upstream, *refs
 ):
     refs = list(refs)
 
@@ -1034,17 +932,26 @@
         return taken
 
     if layer:
-        (pack1, routes1), dense_own, dense_other = take(2), take(4), take(4)
-        attended, query_raw, key_raw, value_low, mid, gates, rows_all = take(7)
+        (pack0, pack1, routes1), dense_own, dense_other, expert_own, expert_other = take(3), take(4), take(4), take(3), take(3)
+        attended, query_raw, key_raw, value_low, mid, gates, rows_all, spread, acts, out = take(10)
     else:
-        dense_own, expert_own = take(4), take(3)
-        attended, query_raw, key_raw, value_low, mid, gates, rows_all, pack1, routes1 = take(9)
-        dense_other, expert_other = take(4), take(3)
+        (router_own, norm_attn, norm_moe, norm_query, norm_key), dense_own, expert_own = take(5), take(4), take(3)
+        attended, query_raw, key_raw, value_low, mid, gates, rows_all, spread, acts, out = take(10)
+        (pack0, pack1, routes1), dense_other, expert_other = take(3), take(4), take(3)
     wq, wk, wv, wo, total, part, own, slots, sems, send, recv, local = take(12)
+    share_send, share_recv, gate, up, down, expert_sems, all_in, act_slots, act_sems, named_all = take(10)
     place = Place()
     section = place.section
+    if not layer:
+        rows = rows.at[section]
+    part_width = rows.shape[1] // 2
+    shared = upstream.at[section, :, :, pl.ds(layer * part_width, part_width)]
     peer = place.peer()
     met = greet(neighbours(place) if layer else [peer, *neighbours(place)])
+    keep_shared = pltpu.make_async_copy(shared.at[place.x], spread.at[place.z, place.y, place.x], local.at[1])
+    keep_shared.start()
+    sharer = Sender(share_send, share_recv)
+    sharing = gather(place, sharer, thirds(spread), shared.at[place.x], keep_shared.wait)
     dim = wk.shape[1]
     heads = wq.shape[1] // dim
     step = HEADS_STEP * dim
@@ -1063,6 +970,9 @@
 
         def arrive(i):
             loads[i].wait()
+
+        fetching = load_weights(layer, expert_own, expert_other, (gate, up, down), expert_sems)
+        met()
     else:
         lower = section == 0
         loads = [pltpu.make_async_copy(*pair, sems.at[i]) for i, pair in enumerate(zip(ours, targets))]
@@ -1073,8 +983,9 @@
             for load in loads:
                 load.start()
 
+        fill_pack(pack0, router_own, norm_attn, norm_moe, norm_query, norm_key)
         met()
-        pusher = Sender(*refs)
+        pusher = Sender(*take(2))
         first = [pusher.send(pack0, pack1, peer), pusher.send(routes0.at[1 - section], routes1, peer)]
         pushed = [pusher.send(*pair, peer) for pair in zip(ours, theirs)]
         for copy in first:
@@ -1092,11 +1003,12 @@
             loads[i].wait()
 
         prefetch(0)
+    next(sharing)
     resid = rows[...].astype(F32)
     gain = of_layer(layer, pack0[PACK_ROUTER : PACK_ROUTER + 1], pack1[PACK_ROUTER : PACK_ROUTER + 1]).astype(F32)
     gains = of_layer(layer, pack0[PACK_ROUTER + 2 : PACK_ROUTER + 3], pack1[PACK_ROUTER + 2 : PACK_ROUTER + 3]).astype(F32)
     gain_query, gain_key = gains[:, :dim], gains[:, dim : 2 * dim]
-    cosine, sine, allowed = tables(seg_column[...], seg_row[...], dim)
+    cosine, sine, allowed = tables(segments[place.section], dim)
     normed = (resid * inverse_rms(resid) * gain).astype(BF16)
     arrive(0)
     raw = dot_nn(normed, wk[...])
@@ -1106,6 +1018,8 @@
     value = dot_nn(normed, wv[...]).astype(BF16)
     value_low[...] = value
     for i in range(steps):
+        if i == steps // 2:
+            next(sharing)
         arrive(2 + 2 * i)
         raws = dot_nn(normed, wq[:, i * step : (i + 1) * step])
         query_raw[:, i * step : (i + 1) * step] = raws
@@ -1128,16 +1042,17 @@
         part[i] = total[i * quarter : (i + 1) * quarter].astype(BF16)
         total[i * quarter : (i + 1) * quarter] = resid[i * quarter : (i + 1) * quarter]
     sender = Sender(send, recv)
-    if layer:
-        met()
     copies = send_x(place, sender, part, slots)
     if not layer:
         pushed_experts = [pusher.send(*pair, peer) for pair in zip(expert_own, expert_other)]
-    chosen = of_layer(layer, routes0[section, place.x], routes1[place.x])
-    lanes = lax.broadcasted_iota(jnp.int32, gates.shape, 1)
-    named = chosen[:, 0:1] == lanes
-    for i in range(1, chosen.shape[1]):
-        named = named | (chosen[:, i : i + 1] == lanes)
+    chosen = of_layer(layer, routes0[section], routes1[...])
+    number = lax.broadcasted_iota(jnp.int32, (GATED, chosen.shape[1]), 0)
+    named = chosen[0:1] == number
+    for i in range(1, chosen.shape[0]):
+        named = named | (chosen[i : i + 1] == number)
+    across = lax.broadcasted_iota(jnp.int32, (GATED, GATED), 0) == lax.broadcasted_iota(jnp.int32, (GATED, GATED), 1)
+    named_all[...] = dot_tn(named.astype(F32).astype(BF16), across.astype(F32).astype(BF16))
+    named = named_all[pl.ds(pl.multiple_of(place.x * quarter, 8), quarter)] > 0.5
     gain = of_layer(layer, pack0[PACK_ROUTER + 1 : PACK_ROUTER + 2], pack1[PACK_ROUTER + 1 : PACK_ROUTER + 2])
     router = of_layer(layer, pack0[:PACK_ROUTER], pack1[:PACK_ROUTER])
     mine = total[pl.ds(pl.multiple_of(place.x * quarter, 8), quarter)]
@@ -1150,19 +1065,77 @@
     gates[...] = weights
     own[:, : moe_in.shape[1]] = moe_in
     own[:, moe_in.shape[1] :] = weights.astype(BF16)
-    keep = pltpu.make_async_copy(own, rows_all.at[place.z, place.y, place.x], local)
+    keep = pltpu.make_async_copy(own, all_in.at[place.z, place.y, place.x], local.at[0])
     keep.start()
-    run(gather(place, sender, thirds(rows_all), own, keep.wait))
+    gathering = gather(place, sender, thirds(all_in), own, keep.wait)
+    for _ in range(3):
+        next(gathering)
     if not layer:
+        for copy in pushed_experts:
+            copy.wait_recv()
+        fetching = load_weights(layer, expert_own, expert_other, (gate, up, down), expert_sems)
+    run(gathering)
+    store = pltpu.make_async_copy(all_in, rows_all, local.at[2])
+    store.start()
+    next(sharing)
+    for copy in fetching:
+        copy.wait()
+    kept = Stream([acts], act_slots, act_sems)
+    if layer:
+        out_slots, out_sems = refs
+        outs = Stream([out], out_slots, out_sems)
+    else:
+        settle_send, settle_recv, buffer, *settle_slots = refs
+    width = gate.shape[1]
+    units = gate.shape[0]
+    tile_rows = BLOCKS * quarter
+    tiles = acts.shape[0] // tile_rows
+    half = BLOCKS // RING
+    for i in range(tiles):
+        at = i * half
+        tile = all_in[at // RING, at % RING : at % RING + half].astype(F32).reshape(tile_rows, width + GATED)
+        moe_in = tile[:, :width].astype(BF16)
+        gate_act = dot_nt(moe_in, gate[...])
+        up_act = dot_nt(moe_in, up[...])
+        hidden = gate_act / (1.0 + jnp.exp(-gate_act)) * up_act
+        hidden = hidden * gate_columns(tile[:, width:], units // 2)
+        if i >= 2:
+            kept.stored(i - 2)
+        act_slots[i % 2, :, :units] = gate_act.astype(BF16)
+        act_slots[i % 2, :, units:] = up_act.astype(BF16)
+        kept.store(i)
+        made = dot_nn(hidden.astype(BF16), down[...])
+        if layer:
+            if i >= 2:
+                outs.stored(i - 2)
+            out_slots[i % 2] = made.astype(BF16)
+            outs.store(i)
+        else:
+            for n in range(BLOCKS):
+                block = i * BLOCKS + n
+                here = (block // (RING * RING), block // RING % RING, block % RING)
+                buffer[here] = made[n * quarter : (n + 1) * quarter].astype(BF16)
+        if i == SHARE_TILE:
+            next(sharing)
+    if layer:
+        run(sharing)
+        for i in (tiles - 2, tiles - 1):
+            outs.stored(i)
+    else:
+        settler = Sender(settle_send, settle_recv)
+        run(in_turn([settle_job(place, settler, None, buffer, settle_slots, mid, out), sharing]))
+        settler.finish()
 
         @pl.when(lower)
         def _():
             for copy in pushed:
                 copy.wait_recv()
 
-        for copy in pushed_experts:
-            copy.wait_recv()
         pusher.finish()
+    for i in (tiles - 2, tiles - 1):
+        kept.stored(i)
+    store.wait()
+    sharer.finish()
     sender.finish()
 
 
@@ -1170,26 +1143,38 @@
     return [pltpu.VMEM(w.shape, BF16) for w in dense]
 
 
-def attend_mix(layer, rows, segs, pack, routes, own, other):
-    count, width = rows.shape
+SHARE_TILE = 4
+
+
+def forward(layer, rows, segments, packs, routes, upstream, own, other, expert_own, expert_other):
+    count, width = rows.shape[-2:]
     quarter = count // RING
     dim, inner = own[1].shape[1], own[0].shape[1]
     pieces = 2 + 2 * (inner // dim // HEADS_STEP)
+    units = 2 * expert_own[0].shape[1]
+    everyone = (RING, RING, RING, quarter)
+    total = RING**3 * quarter
+    tile = BLOCKS * quarter
 
     def like(array):
         return jax.ShapeDtypeStruct(array.shape, array.dtype)
 
     if layer:
+        out, out_spec = (total, width), ANYWHERE
         swapped, swapped_specs, push = (), (), ()
-        inputs = (rows, *segs, pack[0], routes[0], pack[1], routes[1], *own, *other)
+        tail = stream_scratch((width,), tile=tile)
+        inputs = (rows, segments, routes[0], upstream, *packs, routes[1], *own, *other, *expert_own, *expert_other)
     else:
-        swapped = (like(pack), jax.ShapeDtypeStruct(routes.shape[1:], routes.dtype), *map(like, own), *map(like, other))
-        swapped_specs = (IN_VMEM, IN_VMEM) + (ANYWHERE,) * 7
+        out, out_spec = (RING, quarter, width), IN_VMEM
+        pack = jax.ShapeDtypeStruct((PACK_ROWS, width), BF16)
+        swapped = (pack, pack, jax.ShapeDtypeStruct(routes.shape[1:], routes.dtype), *map(like, own), *map(like, expert_own))
+        swapped_specs = (IN_VMEM,) * 3 + (ANYWHERE,) * 7
         push = copy_sems(2 + pieces + 3)
-        inputs = (rows, *segs, pack, routes, *own, *other)
+        tail = [*copy_sems(3 + SENDS), pltpu.VMEM((*everyone, width), BF16), *third_slots(quarter, width)]
+        inputs = (rows, segments, routes, upstream, *packs, *own, *expert_own)
     return pl.pallas_call(
-        functools.partial(attend_mix_kernel, layer),
-        name="attend_mix",
+        functools.partial(forward_kernel, layer),
+        name="forward",
         out_shape=(
             jax.ShapeDtypeStruct((count, inner), BF16),
             jax.ShapeDtypeStruct((count, inner), F32),
@@ -1197,11 +1182,14 @@
             jax.ShapeDtypeStruct((count, dim), BF16),
             jax.ShapeDtypeStruct((quarter, width), F32),
             jax.ShapeDtypeStruct((quarter, GATED), F32),
-            jax.ShapeDtypeStruct((RING, RING, RING, quarter, width + GATED), BF16),
+            jax.ShapeDtypeStruct((*everyone, width + GATED), BF16),
+            jax.ShapeDtypeStruct((*everyone, width // 2), BF16),
+            jax.ShapeDtypeStruct((total, 2 * units), BF16),
+            jax.ShapeDtypeStruct(out, BF16),
             *swapped,
         ),
-        in_specs=[IN_VMEM] * (7 if layer else 5) + [ANYWHERE] * (8 if layer else 7),
-        out_specs=(IN_VMEM,) * 6 + (ANYWHERE,) + swapped_specs,
+        in_specs=[IN_VMEM] * (7 if layer else 9) + [ANYWHERE] * (14 if layer else 7),
+        out_specs=(IN_VMEM,) * 6 + (ANYWHERE,) * 3 + (out_spec,) + swapped_specs,
         scratch_shapes=[
             *weight_scratch(own),
             pltpu.VMEM((count, width), F32),
@@ -1210,8 +1198,15 @@
             pltpu.VMEM((3, quarter, width), BF16),
             pltpu.SemaphoreType.DMA((pieces,)),
             *copy_sems(3 + SENDS),
-            pltpu.SemaphoreType.DMA,
+            pltpu.SemaphoreType.DMA((3,)),
+            *copy_sems(SENDS),
+            *[pltpu.VMEM((units, width), BF16)] * 3,
+            pltpu.SemaphoreType.DMA((6,)),
+            pltpu.VMEM((*everyone, width + GATED), BF16),
+            *stream_scratch((2 * units,), tile=tile),
+            pltpu.VMEM((count, GATED), F32),
             *push,
+            *tail,
         ],
         compiler_params=params(1 + layer),
     )(*inputs)
@@ -1281,25 +1276,46 @@
 
 
 def attend_back_kernel(
-    layer, rows, seg_column, seg_row, pack0, pack1, attended, query_raw, key_raw, value_low, upstream, d_part,
+    layer, rows, segments, pack0, pack1, attended, query_raw, key_raw, value_low, upstream, d_part,
     router_term, moe_gain_term, *refs
 ):
     last = layer == 0
     refs = list(refs)
-    extra = [refs.pop(0) for _ in range(4 if last else 0)]
+    extra = [refs.pop(0) for _ in range(8 if last else 2)]
     q0, k0, v0, o0, q1, k1, v1, o1, d_input, normed_both, d_proj, heads_both, d_mid_low, smalls = refs[:14]
     refs = refs[14:]
-    wide = [refs.pop(0) for _ in range(4 if last else 2)]
+    wide = [refs.pop(0) for _ in range(7 if last else 4)]
     wq, wk, wv, wo, total, d_mid, d_heads, part, own, slots, sems, send, recv, local, *side = refs
     place = Place()
     peer = place.peer()
     met = greet([peer, *neighbours(place)])
+    if last:
+        rows = rows.at[place.section]
+    else:
+        upstream = upstream.at[place.section]
     count = rows.shape[0]
     job = iter(())
+    theirs, ours = pl.ds(count, count), pl.ds(0, count)
     if last:
         upper = place.section == 1
-        first_own, second_own, grad_in, grad_down = extra
-        first, second, got_in, got_down = wide
+        first_own, second_own, grad_in, grad_down, out_zero, out_low, out_high, grad_one = extra
+        first, second, got_in, got_down, outputs, input_grads, second_sum = wide
+        lower = place.section == 0
+        swapper = Sender(side[4], side[5])
+        half = out_low.shape[2]
+        my_rows, my_grads = outputs.at[place.section], input_grads.at[place.section]
+        row_pairs = []
+        for piece, above in enumerate((out_low, out_high)):
+            columns = pl.ds(piece * half, half)
+            row_pairs.append((out_zero.at[:, :, columns], above, my_rows.at[:, :, columns]))
+
+        def keep_rows(index, low, high, target):
+            one, two = (pltpu.make_async_copy(origin, target, side[6].at[index]) for origin in (low, high))
+            pl.when(lower)(one.start)
+            pl.when(upper)(two.start)
+            return one
+
+        kept_rows = [keep_rows(i, *pair) for i, pair in enumerate(row_pairs)]
         side_sender = Sender(side[0], side[1], upper)
         handing = Sender(side[2], side[3])
 
@@ -1311,6 +1327,18 @@
             yield from in_turn(gradient_gathers(place, side_sender, first, second))
 
         job = widen()
+        summer = Sender(side[7], side[8], lower)
+        second_parts, *second_slots = side[9:]
+
+        def sum_second():
+            handed_early()
+            pl.when(lower)(lambda: output_products(heads_both, d_mid_low, second_parts))
+            yield from reduce(place, summer, gradient_plans(second_parts), sort_slots(second_slots, 2, 2))
+            second_sum[...] = second_parts[place.z, place.y]
+
+        summing = sum_second()
+    else:
+        settling, settler = settle_part(1, place, side[3:5], extra[1], extra[0], wide[2], side[5:])
     dim = wk.shape[1]
     heads = wq.shape[1] // dim
     inner = heads * dim
@@ -1334,7 +1362,7 @@
     gain = of_layer(layer, pack0[PACK_ROUTER : PACK_ROUTER + 1], pack1[PACK_ROUTER : PACK_ROUTER + 1]).astype(F32)
     gains = of_layer(layer, pack0[PACK_ROUTER + 2 : PACK_ROUTER + 3], pack1[PACK_ROUTER + 2 : PACK_ROUTER + 3]).astype(F32)
     gain_query, gain_key = gains[:, :dim], gains[:, dim : 2 * dim]
-    cosine, sine, allowed = tables(seg_column[...], seg_row[...], dim)
+    cosine, sine, allowed = tables(segments[place.section], dim)
     normed_both[:count] = (resid * inverse_rms(resid) * gain).astype(BF16)
     raw_key = key_raw[...]
     key = turn(raw_key * inverse_rms(raw_key) * gain_key, cosine, sine).astype(BF16)
@@ -1345,9 +1373,20 @@
     gain_total = jnp.zeros(gain_query.shape, F32)
     handed_grads = None
     for i in range(steps):
-        next(job, None)
+        if i in WIDEN_POINTS:
+            next(job, None)
+        if not last and i in SETTLE_BESIDE:
+            if i == 0:
+                met()
+            next(settling)
         if last and i == 1:
             handed_grads = handing.hand(upper, [(grad_in, got_in), (grad_down, got_down)], peer)
+            handed_early = handing.hand(
+                upper, [(ref.at[ours], ref.at[theirs]) for ref in (heads_both, d_mid_low, normed_both)], peer
+            )
+            swaps = [swapper.send_either(lower, high, low, target, peer) for low, high, target in row_pairs]
+        if last and i == steps - 1:
+            next(summing)
         loads[i].wait()
         d_heads[...] = dot_nt(grad_low, wo[i * step : (i + 1) * step]).astype(BF16)
         for h in range(HEADS_STEP):
@@ -1386,16 +1425,14 @@
     for i in range(RING):
         part[i] = total[i * quarter : (i + 1) * quarter].astype(BF16)
     sender = Sender(send, recv)
-    if not last:
-        met()
     copies = send_x(place, sender, part, slots)
-    theirs = pl.ds(count, count)
-    ours = pl.ds(0, count)
     handed = sender.hand(
         place.section != layer,
-        [(ref.at[ours], ref.at[theirs]) for ref in (normed_both, d_proj, heads_both, d_mid_low)],
+        [(ref.at[ours], ref.at[theirs]) for ref in ((d_proj,) if last else (normed_both, d_proj, heads_both, d_mid_low))],
         peer,
     )
+    if last:
+        next(summing, None)
     mine = resid[:quarter]
     for i in range(1, RING):
         mine = jnp.where(place.x == i, resid[i * quarter : (i + 1) * quarter], mine)
@@ -1406,6 +1443,8 @@
     if last:
         d_input[place.x] = d_rows
         gather_x(place, sender, d_input)
+        swaps.append(swapper.send_either(lower, grad_one, d_input, my_grads, peer))
+        kept_rows.append(keep_rows(2, d_input, grad_one, my_grads))
     else:
         own[...] = d_rows
         keep = pltpu.make_async_copy(own, d_input.at[place.z, place.y, place.x], local)
@@ -1413,6 +1452,7 @@
         spread = gather(place, sender, thirds(d_input), own, keep.wait)
         for _ in range(3):
             next(spread)
+            next(settling, None)
     handed()
     handed_small()
     if not last:
@@ -1432,7 +1472,11 @@
             input_products(normed_both, d_proj, products[0])
             stores[0].start()
 
-        run(spread)
+        run(in_turn([spread, settling]))
+        settler.finish()
+        fetch = pltpu.make_async_copy(d_input.at[place.z, place.y], wide[3], local)
+        fetch.start()
+        fetch.wait()
 
         @pl.when(owner)
         def _():
@@ -1441,25 +1485,40 @@
 
     sender.finish()
     if last:
-        run(job)
         handed_grads()
+        for copy in swaps:
+            copy.wait_recv()
+        for copy in kept_rows:
+            copy.wait()
+        run(in_turn([job, summing]))
+        summer.finish()
+        swapper.finish()
         side_sender.finish()
 
 
-def attend_back(layer, rows, segs, packs, saved, upstream, d_part, terms, extra, own, other):
+def attend_back(layer, rows, segments, packs, saved, upstream, d_part, terms, extra, own, other):
     last = layer == 0
     first, second = gradient_shapes(own)
     wide = tuple(jax.ShapeDtypeStruct(shape, BF16) for shape in (first, second))
     side = (pltpu.VMEM(first, BF16), pltpu.VMEM(second, BF16), pltpu.SemaphoreType.DMA((2,)))
     if last:
-        shapes = (first, second, extra[2].shape, extra[3].shape)
+        both = (2, *d_part.shape)
+        shapes = (first, second, extra[2].shape, extra[3].shape, both, both, second[2:])
         wide = tuple(jax.ShapeDtypeStruct(shape, BF16) for shape in shapes)
         side = (
             *copy_sems(GRADIENT_SENDS),
-            *copy_sems(2),
+            *copy_sems(2 + 3),
+            *copy_sems(3),
+            pltpu.SemaphoreType.DMA((3,)),
+            *copy_sems(18),
+            pltpu.VMEM(second, BF16),
+            *slot_scratch([(second[2], 2, piece) for piece in cut(second[3], 2)]),
         )
-
-    count, width = rows.shape
+    else:
+        wide += (jax.ShapeDtypeStruct((*d_part.shape[:2], d_part.shape[2] // 2), BF16), jax.ShapeDtypeStruct(d_part.shape, BF16))
+        side += tuple(settle_scratch(extra[1]))
+
+    count, width = rows.shape[-2:]
     quarter = count // RING
     dim, inner = own[1].shape[1], own[0].shape[1]
     out = (RING, quarter, width) if layer == 0 else (RING, RING, RING, quarter, width)
@@ -1475,8 +1534,8 @@
             jax.ShapeDtypeStruct((2, SMALL, width), F32),
             *wide,
         ),
-        in_specs=[IN_VMEM] * 13 + ([IN_VMEM] * 2 + [ANYWHERE] * 2 if last else []) + [ANYWHERE] * 8,
-        out_specs=(IN_VMEM if last else ANYWHERE,) + (IN_VMEM,) * (7 if last else 5) + (ANYWHERE,) * 2,
+        in_specs=[IN_VMEM] * 12 + ([IN_VMEM] * 2 + [ANYWHERE] * 2 + [IN_VMEM] * 4 if last else [IN_VMEM, ANYWHERE]) + [ANYWHERE] * 8,
+        out_specs=(IN_VMEM if last else ANYWHERE,) + (IN_VMEM,) * (7 if last else 5) + (ANYWHERE,) * (4 if last else 2) + (IN_VMEM,) * (1 if last else 2),
         scratch_shapes=[
             *weight_scratch(own),
             pltpu.VMEM((count, width), F32),
@@ -1491,20 +1550,19 @@
             *side,
         ],
         compiler_params=params(7 + layer),
-    )(rows, *segs, *packs, *saved, upstream, d_part, *terms, *extra, *own, *other)
+    )(rows, segments, *packs, *saved, upstream, d_part, *terms, *extra, *own, *other)
 
 
 def finish_kernel(
-    normed0, proj0, heads0, mids0, small0, small1, first_one, second_one, out0, out1a, out1b, ig0, ig1,
-    first, second, small_out, outputs, input_grads,
-    first_sums, second_sums, normed, proj, heads, mids, terms, passing, small_slots, send, recv, flagged_send,
+    normed0, proj0, second_sum, small0, small1, first_one, second_one,
+    first, second, small_out,
+    first_sums, normed, proj, terms, passing, small_slots, send, recv, flagged_send,
     flagged_recv, local, *slots
 ):
     place = Place()
     lower = place.section == 0
     upper = place.section == 1
-    peer = place.peer()
-    met = greet([peer, *neighbours(place)])
+    met = greet(neighbours(place))
     sender = Sender(send, recv)
     reducer = Sender(flagged_send, flagged_recv, lower)
 
@@ -1514,17 +1572,11 @@
         pl.when(upper)(two.start)
         return one
 
-    half = out1a.shape[2]
-    pairs = [(small0, small1, terms), (ig0, ig1, input_grads.at[place.section])]
-    halves_of = []
-    for part, above in enumerate((out1a, out1b)):
-        columns = pl.ds(part * half, half)
-        halves_of.append((out0.at[:, :, columns], above, outputs.at[place.section, :, :, columns]))
-    pairs += halves_of
-    loads = ((normed0, normed), (proj0, proj), (heads0, heads), (mids0, mids))
-    loads = [pltpu.make_async_copy(*pair, local.at[4 + i]) for i, pair in enumerate(loads)]
+    pairs = [(small0, small1, terms)]
+    loads = ((normed0, normed), (proj0, proj))
+    loads = [pltpu.make_async_copy(*pair, local.at[1 + i]) for i, pair in enumerate(loads)]
     ready = [
-        pltpu.make_async_copy(*pair, local.at[8 + i]) for i, pair in enumerate(((first_one, first), (second_one, second)))
+        pltpu.make_async_copy(*pair, local.at[3 + i]) for i, pair in enumerate(((first_one, first), (second_one, second)))
     ]
 
     @pl.when(upper)
@@ -1538,7 +1590,7 @@
             copy.start()
         for copy in loads:
             copy.wait()
-        output_products(heads, mids, second_sums)
+        input_products(normed, proj, first_sums)
 
     kept = [keep(i, *pair) for i, pair in enumerate(pairs)]
     kept[0].wait()
@@ -1565,32 +1617,21 @@
     def small_last():
         small_out[...] = collect(2)
 
-    def swap_rows():
-        state["late"] = [
-            *[sender.send_either(lower, high, low, target, peer) for low, high, target in halves_of],
-            sender.send_either(lower, ig1, ig0, input_grads.at[place.section], peer),
-        ]
+    def first_step():
         exchange(0, terms[0] + terms[1])
 
     def second_step():
         exchange(1, collect(0))
 
-    first_job, second_job = gradient_reduces(place, reducer, first_sums, second_sums, slots, (swap_rows, second_step))
-    next(second_job)
-    pl.when(lower)(lambda: input_products(normed, proj, first_sums))
-    run(in_turn([first_job, second_job]))
+    run(reduce(place, reducer, gradient_plans(first_sums), sort_slots(slots, 2, 2), (first_step, second_step)))
 
     @pl.when(lower)
     def _():
         first[place.z, place.y] = first_sums[place.z, place.y]
-        second[place.z, place.y] = second_sums[place.z, place.y]
+        second[place.z, place.y] = second_sum[...]
 
     beside = (lambda: exchange(2, collect(1)), small_last)
     run(in_turn(gradient_gathers(place, reducer, first, second, beside)))
-    for copy in state["late"]:
-        copy.wait_recv()
-    for copy in kept[1:]:
-        copy.wait()
 
     @pl.when(upper)
     def _():
@@ -1601,10 +1642,8 @@
     reducer.finish()
 
 
-def finish(factors, smalls, ready, outs, input_grads):
-    rows, width = factors[0].shape
+def finish(factors, smalls, ready):
     first, second = ready[0].shape, ready[1].shape
-    both = (2, *outs[0].shape)
     return pl.pallas_call(
         finish_kernel,
         name="finish",
@@ -1612,25 +1651,22 @@
             jax.ShapeDtypeStruct(first, BF16),
             jax.ShapeDtypeStruct(second, BF16),
             jax.ShapeDtypeStruct(smalls[0].shape[1:], F32),
-            jax.ShapeDtypeStruct(both, BF16),
-            jax.ShapeDtypeStruct(both, BF16),
         ),
-        in_specs=[ANYWHERE] * 13,
-        out_specs=(IN_VMEM,) * 3 + (ANYWHERE,) * 2,
+        in_specs=[ANYWHERE] * 2 + [IN_VMEM] + [ANYWHERE] * 4,
+        out_specs=(IN_VMEM,) * 3,
         scratch_shapes=[
             pltpu.VMEM(first, BF16),
-            pltpu.VMEM(second, BF16),
-            *[pltpu.VMEM(f.shape, BF16) for f in factors],
+            *[pltpu.VMEM(f.shape, BF16) for f in factors[:2]],
             pltpu.VMEM(smalls[0].shape, F32),
             pltpu.VMEM(smalls[0].shape[1:], F32),
             pltpu.VMEM((3, 4, *smalls[0].shape[1:]), BF16),
-            *copy_sems(3 + 9),
-            *copy_sems(2 * GRADIENT_SENDS),
-            pltpu.SemaphoreType.DMA((10,)),
-            *gradient_slots(first, second),
+            *copy_sems(9),
+            *copy_sems(18 + GRADIENT_SENDS),
+            pltpu.SemaphoreType.DMA((5,)),
+            *slot_scratch([(first[2], 2, piece) for piece in cut(first[3], 2)]),
         ],
         compiler_params=params(9),
-    )(*factors, *smalls, *ready, *outs, *input_grads)
+    )(*factors, *smalls, *ready)
 
 
 STEPS = 8
@@ -1777,71 +1813,50 @@
 
     dense_own = (w_query[0], key_matrix[0], value_matrix[0], w_output[0])
     expert_own = (jnp.swapaxes(w_gate[0], 1, 2), jnp.swapaxes(w_up[0], 1, 2), w_down[0])
-    pack_own = jnp.concatenate(
-        [
-            jnp.pad(w_router[0].T, ((0, PACK_ROUTER - expert_count), (0, 0))),
-            norm_attn,
-            norm_moe,
-            jnp.pad(jnp.concatenate([norm_query, norm_key], axis=1), ((0, PACK_ROWS - PACK_ROUTER - 3), (0, width - 2 * dim))),
-        ],
-        axis=0,
-    )
-    def pick(array):
-        return lax.dynamic_index_in_dim(array, section, 0, keepdims=False)
-
-    def quarters(array):
-        return array.reshape(RING, quarter, array.shape[-1])
-
-    segment = pick(segments)
-    segs = (segment.reshape(group_rows, 1), segment.reshape(1, group_rows))
-
-    routes = routes[0].reshape(2, RING, quarter, routes.shape[-1])
-    rows_in = pick(block_input)
-    upstream = quarters(pick(cotangent))
-    shared = (upstream[:, :, : width // 2], upstream[:, :, width // 2 :])
+    layer_gains = (w_router[0].T, norm_attn, norm_moe, norm_query, norm_key)
+    routes = jnp.swapaxes(routes[0], 1, 2)
+    upstream = cotangent.reshape(2, RING, quarter, width)
+    rows_in = block_input
     saved, layer_ins, outs, grads_all = [], [], [], []
     for layer in range(2):
         layer_ins.append(rows_in)
         if layer == 0:
-            made = attend_mix(layer, rows_in, segs, pack_own, routes, dense_own, expert_own)
-            packs, routes_other = (pack_own, made[7]), made[8]
-            dense_other, expert_other = made[9:13], made[13:]
+            made = forward(layer, rows_in, segments, layer_gains, routes, upstream, dense_own, None, expert_own, None)
+            packs, routes_other = made[10:12], made[12]
+            dense_other, expert_other = made[13:17], made[17:]
         else:
-            made = attend_mix(layer, rows_in, segs, packs, (routes, routes_other), dense_own, dense_other)
-        attn_saved, (mid, gates, rows_all) = made[:4], made[4:7]
-        made, acts, spread = experts(layer, rows_all, shared[layer], mid, expert_own, expert_other)
+            made = forward(
+                layer, rows_in, segments, packs, (routes, routes_other), upstream, dense_own, dense_other,
+                expert_own, expert_other,
+            )
+        attn_saved, (mid, gates, rows_all, spread, acts, made) = made[:4], made[4:10]
         grads_all.append(spread)
         saved.append((attn_saved, mid, gates, rows_all, acts))
         if layer == 0:
             rows_in = made.reshape(group_rows, width)
             outs.append(made)
+    made = made.reshape(RING, RING, RING, quarter, width)
 
     attn_saved, mid, gates, rows_all, acts = saved[1]
-    d_part, *terms, grad_in, grad_down, out_low, out_high = experts_back_sum(
+    d_part, *terms, grad_in, grad_down, out_low = experts_back_sum(
         1, rows_all, grads_all, acts, mid, gates, packs, expert_own, expert_other, made, expert_count
     )
+    grads_one = (grad_in, grad_down)
+    d_all, *_, smalls_one, products_first, products_second, out_high, upstream = attend_back(
+        1, layer_ins[1], segments, packs, attn_saved, upstream, d_part, terms[::-1], (mid, made), dense_own, dense_other
+    )
     outs += [out_low, out_high]
-    grads_one = (grad_in, grad_down)
-    d_all, *_, smalls_one, products_first, products_second = attend_back(
-        1, layer_ins[1], segs, packs, attn_saved, upstream, d_part, terms[::-1], (), dense_own, dense_other
-    )
-    upstream = lax.dynamic_index_in_dim(
-        d_all.reshape(RING * RING, RING, quarter, width), lax.axis_index("expert"), 0, keepdims=False
-    )
-    input_grads = [None, upstream]
     attn_saved, mid, gates, rows_all, acts = saved[0]
     partial, *grads_zero, first_own, second_own, got_in_one, got_down_one = experts_back(
         0, rows_all, [d_all], acts, expert_own, expert_other, ((products_first, products_second), grads_one, dense_own)
     )
     d_part, *terms = moe_back(0, partial, mid, gates, packs, expert_count)
-    input_grads[0], *factors_zero, smalls_zero, first_one, second_one, got_in_zero, got_down_zero = attend_back(
-        0, layer_ins[0], segs, packs, attn_saved, upstream, d_part, terms[::-1],
-        (first_own, second_own, *grads_zero), dense_own, dense_other,
+    _, *factors_zero, smalls_zero, first_one, second_one, got_in_zero, got_down_zero, outputs, d_inputs, second_sum = attend_back(
+        0, layer_ins[0], segments, packs, attn_saved, upstream, d_part, terms[::-1],
+        (first_own, second_own, *grads_zero, *outs, upstream), dense_own, dense_other,
     )
     expert_grads = ((*grads_zero, got_in_zero, got_down_zero), (*grads_one, got_in_one, got_down_one))
-    first, second, small, outputs, d_inputs = finish(
-        factors_zero, (smalls_zero, smalls_one), (first_one, second_one), outs, input_grads
-    )
+    first, second, small = finish((*factors_zero[:2], second_sum), (smalls_zero, smalls_one), (first_one, second_one))
     query, key, value, output, gate, up, down, router, gain_moe, gain_attn, gain_query, gain_key, outputs, d_inputs = widen(
         section, first.reshape(width, first.shape[-1]), second.reshape(-1, width), expert_grads, small, outputs, d_inputs,
         dim, expert_count,

time: 567 us -> 536 us (0.945)
  Pallas kernels: 546 us -> 531 us
  local copies, waits for them, and re-layouts: 7.86 us -> 0 us
    pallas_call x2, Pallas kernels: 92.5 us -> 112 us  [attend_back(): pl.pallas_call(functools.partial(attend_back_kernel, layer), name='attend...]
    pallas_call x1, Pallas kernels: 84.1 us -> 70.3 us  [experts_back_sum(): pl.pallas_call(functools.partial(expert_back_sum_kernel, layer, len(grads...]
    pallas_call x4 -> x2, Pallas kernels: 198 us -> 186 us  [forward(): pl.pallas_call(functools.partial(forward_kernel, layer), name='forward',...]
    pallas_call x1, Pallas kernels: 80.3 us -> 70.8 us  [finish(): pl.pallas_call(finish_kernel, name='finish', out_shape=(jax.ShapeDtypeStr...]
where the time goes in v4:
time: 536 us; the launch traced here: 532 us
  Pallas kernels  531 us (99%)
    pallas_call x2, Pallas kernels, forward(): pl.pallas_call(functools.partial(forward_kernel, layer), name='forward',...  186 us
    pallas_call x2, Pallas kernels, attend_back(): pl.pallas_call(functools.partial(attend_back_kernel, layer), name='attend...  112 us
    pallas_call x1, Pallas kernels, finish(): pl.pallas_call(finish_kernel, name='finish', out_shape=(jax.ShapeDtypeStr...  70.8 us
    pallas_call x1, Pallas kernels, experts_back_sum(): pl.pallas_call(functools.partial(expert_back_sum_kernel, layer, len(grads...  70.3 us
    pallas_call x1, Pallas kernels, moe_back(): pl.pallas_call(functools.partial(moe_back_kernel, layer), name='moe_back'...  44.3 us
    pallas_call x1, Pallas kernels, experts_back(): pl.pallas_call(functools.partial(expert_back_kernel, layer, len(grads)),...  28.3 us
    pallas_call x1, Pallas kernels, widen(): pl.pallas_call(widen_kernel, name='widen', out_shape=(shape(width, inner)...  18.9 us

profile of v4, /device:TPU:0, one launch (start us, length us, event | category | flops | bytes accessed | tf_op | source)
XLA Modules:
  0.0 531.5 jit_solution(14306229565335810125)
XLA Ops:
  0.6 112.5 %forward.2 = (bf16[96,1024]{1,0:T(8,128)(2,1)}, f32[96,1024]{1,0:T(8,128)}, f32[96,128]{1,0:T(8,128)}, bf16[96,128]{1,0:T(8,128)(2,1)}, f32[24,2048]{1,0:T(8,128...) custom-call(bf16[2,96,2048]{2,1,0:T(8,128)(2,1)} %rows.3, ...), custom_call_target="tpu_custom_call" | custom-call | tf_op jit(solution)/shard_map/forward/pallas_call | solution.py:1175
  113.1 73.2 %forward.3 = (bf16[96,1024]{1,0:T(8,128)(2,1)}, f32[96,1024]{1,0:T(8,128)}, f32[96,128]{1,0:T(8,128)}, bf16[96,128]{1,0:T(8,128)(2,1)}, f32[24,2048]{1,0:T(8,128...) custom-call(bf16[96,2048]{1,0:T(8,128)(2,1)} %bitcast.84, ...), custom_call_target="tpu_custom_call" | custom-call | tf_op jit(solution)/shard_map/forward/pallas_call | solution.py:1175
  186.3 70.3 %experts_back_sum.1 = (bf16[4,24,2048]{2,1,0:T(8,128)(2,1)}, f32[1,2048]{1,0:T(1,128)}, f32[32,2048]{1,0:T(8,128)}, bf16[768,2048]{1,0:T(8,128)(2,1)}, bf16[384,...) custom-call(bf16[1536,2176]{1,0:T(8,128)(2,1)} %bitcast.79, bf16[1536,1024]{1,0:T(8,128)(2,1)} %bitcast.86, ...), custom_call_target="tpu_custom_call" | custom-call | tf_op jit(solution)/shard_map/experts_back_sum/pallas_call | solution.py:784
  256.6 59.0 %attend_back.1 = (bf16[4,4,4,24,2048]{4,3,2,1,0:T(8,128)(2,1)}, bf16[192,2048]{1,0:T(8,128)(2,1)}, bf16[192,1280]{1,0:T(8,128)(2,1)}, bf16[192,1024]{1,0:T(8,128...) custom-call(bf16[96,2048]{1,0:T(8,128)(2,1)} %bitcast.85, ...), custom_call_target="tpu_custom_call" | custom-call | tf_op jit(solution)/shard_map/attend_back/pallas_call | solution.py:1525
  315.6 28.3 %experts_back.1 = (bf16[1536,2176]{1,0:T(8,128)(2,1)}, bf16[768,2048]{1,0:T(8,128)(2,1)}, bf16[384,2048]{1,0:T(8,128)(2,1)}, bf16[128,1280]{1,0:T(8,128)(2,1)}, ...) custom-call(bf16[1536,2176]{1,0:T(8,128)(2,1)} %bitcast.78, ...), custom_call_target="tpu_custom_call" | custom-call | tf_op jit(solution)/shard_map/experts_back/pallas_call | solution.py:838
  343.9 44.3 %moe_back.1 = (bf16[4,24,2048]{2,1,0:T(8,128)(2,1)}, f32[1,2048]{1,0:T(1,128)}, f32[32,2048]{1,0:T(8,128)}) custom-call(bf16[4,4,4,24,2176]{4,3,2,1,0:T(8,128)(2,1)} %bitcast.80, f32[24,2048]{1,0:T(8,128)} %get-tuple-element.131.mid, f32[24,128]{1,0:T(8,128)} %get-tuple-element.132.gates, bf16[144,2048]{1,0:T(8,128)(2,1)} %get-tuple-element.93.refs_0_.refs_5_.pack0, ...), custom_call_target="tpu_custom_call" | custom-call | tf_op jit(solution)/shard_map/moe_back/pallas_call | solution.py:466
  388.2 53.4 %attend_back_last.1 = (bf16[4,24,2048]{2,1,0:T(8,128)(2,1)}, bf16[192,2048]{1,0:T(8,128)(2,1)}, bf16[192,1280]{1,0:T(8,128)(2,1)}, bf16[192,1024]{1,0:T(8,128)(2...) custom-call(bf16[2,96,2048]{2,1,0:T(8,128)(2,1)} %rows.3, ...), custom_call_target="tpu_custom_call" | custom-call | tf_op jit(solution)/shard_map/attend_back_last/pallas_call | solution.py:1525
  441.6 70.8 %finish.1 = (bf16[4,4,128,1280]{3,2,1,0:T(8,128)(2,1)}, bf16[4,4,64,2048]{3,2,1,0:T(8,128)(2,1)}, f32[48,2048]{1,0:T(8,128)}) custom-call(bf16[192,2048]{1,0:T(8,128)(2,1)} %get-tuple-element.142.normed0, bf16[192,1280]{1,0:T(8,128)(2,1)} %get-tuple-element.143.proj0, bf16[64,2048]{1,0:T(8,128)(2,1)} %get-tuple-element.144.second_sum, ...), custom_call_target="tpu_custom_call" | custom-call | tf_op jit(solution)/shard_map/finish/pallas_call | solution.py:1647
  512.4 18.9 %widen.1 = (f32[2048,1024]{1,0:T(8,128)}, f32[2048,128]{1,0:T(8,128)}, f32[2048,128]{1,0:T(8,128)}, f32[1024,2048]{1,0:T(8,128)}, f32[384,2048]{1,0:T(8,128)}, /...) custom-call(s32[1]{0:T(128)} %bitcast.section, ...), custom_call_target="tpu_custom_call" | custom-call | tf_op jit(solution)/shard_map/widen/pallas_call | solution.py:1731

commit v5 on v4

--- a/solution.py
+++ b/solution.py
@@ -1093,8 +1093,8 @@
     half = BLOCKS // RING
     for i in range(tiles):
         at = i * half
-        tile = all_in[at // RING, at % RING : at % RING + half].astype(F32).reshape(tile_rows, width + GATED)
-        moe_in = tile[:, :width].astype(BF16)
+        tile = all_in[at // RING, at % RING : at % RING + half].reshape(tile_rows, width + GATED)
+        moe_in = tile[:, :width]
         gate_act = dot_nt(moe_in, gate[...])
         up_act = dot_nt(moe_in, up[...])
         hidden = gate_act / (1.0 + jnp.exp(-gate_act)) * up_act
@@ -1588,13 +1588,20 @@
     def _():
         for copy in loads:
             copy.start()
+        second[place.z, place.y] = second_sum[...]
+
+    kept = [keep(i, *pair) for i, pair in enumerate(pairs)]
+    kept[0].wait()
+    met()
+    spreading = gather(place, reducer, gradient_plans(second))
+    next(spreading)
+
+    @pl.when(lower)
+    def _():
         for copy in loads:
             copy.wait()
         input_products(normed, proj, first_sums)
 
-    kept = [keep(i, *pair) for i, pair in enumerate(pairs)]
-    kept[0].wait()
-    met()
     state = {}
 
     def exchange(step, total):
@@ -1623,15 +1630,15 @@
     def second_step():
         exchange(1, collect(0))
 
-    run(reduce(place, reducer, gradient_plans(first_sums), sort_slots(slots, 2, 2), (first_step, second_step)))
+    summing = reduce(place, reducer, gradient_plans(first_sums), sort_slots(slots, 2, 2), (first_step, second_step))
+    run(in_turn([summing, spreading]))
 
     @pl.when(lower)
     def _():
         first[place.z, place.y] = first_sums[place.z, place.y]
-        second[place.z, place.y] = second_sum[...]
 
     beside = (lambda: exchange(2, collect(1)), small_last)
-    run(in_turn(gradient_gathers(place, reducer, first, second, beside)))
+    run(gather(place, reducer, gradient_plans(first), None, None, beside))
 
     @pl.when(upper)
     def _():

time: 536 us -> 532 us (level)
  no operation moved by 1% of the time
where the time goes in v5:
time: 532 us; the launch traced here: 528 us
  Pallas kernels  527 us (99%)
    pallas_call x2, Pallas kernels, forward(): pl.pallas_call(functools.partial(forward_kernel, layer), name='forward',...  186 us
    pallas_call x2, Pallas kernels, attend_back(): pl.pallas_call(functools.partial(attend_back_kernel, layer), name='attend...  112 us
    pallas_call x1, Pallas kernels, experts_back_sum(): pl.pallas_call(functools.partial(expert_back_sum_kernel, layer, len(grads...  70.3 us
    pallas_call x1, Pallas kernels, finish(): pl.pallas_call(finish_kernel, name='finish', out_shape=(jax.ShapeDtypeStr...  67 us
    pallas_call x1, Pallas kernels, moe_back(): pl.pallas_call(functools.partial(moe_back_kernel, layer), name='moe_back'...  44.3 us
    pallas_call x1, Pallas kernels, experts_back(): pl.pallas_call(functools.partial(expert_back_kernel, layer, len(grads)),...  28.3 us
    pallas_call x1, Pallas kernels, widen(): pl.pallas_call(widen_kernel, name='widen', out_shape=(shape(width, inner)...  18.9 us

profile of v5, /device:TPU:0, one launch (start us, length us, event | category | flops | bytes accessed | tf_op | source)
XLA Modules:
  0.0 527.7 jit_solution(122553359647118190)
XLA Ops:
  0.6 112.5 %forward.2 = (bf16[96,1024]{1,0:T(8,128)(2,1)}, f32[96,1024]{1,0:T(8,128)}, f32[96,128]{1,0:T(8,128)}, bf16[96,128]{1,0:T(8,128)(2,1)}, f32[24,2048]{1,0:T(8,128...) custom-call(bf16[2,96,2048]{2,1,0:T(8,128)(2,1)} %rows.3, ...), custom_call_target="tpu_custom_call" | custom-call | tf_op jit(solution)/shard_map/forward/pallas_call | solution.py:1175
  113.1 73.2 %forward.3 = (bf16[96,1024]{1,0:T(8,128)(2,1)}, f32[96,1024]{1,0:T(8,128)}, f32[96,128]{1,0:T(8,128)}, bf16[96,128]{1,0:T(8,128)(2,1)}, f32[24,2048]{1,0:T(8,128...) custom-call(bf16[96,2048]{1,0:T(8,128)(2,1)} %bitcast.84, ...), custom_call_target="tpu_custom_call" | custom-call | tf_op jit(solution)/shard_map/forward/pallas_call | solution.py:1175
  186.3 70.3 %experts_back_sum.1 = (bf16[4,24,2048]{2,1,0:T(8,128)(2,1)}, f32[1,2048]{1,0:T(1,128)}, f32[32,2048]{1,0:T(8,128)}, bf16[768,2048]{1,0:T(8,128)(2,1)}, bf16[384,...) custom-call(bf16[1536,2176]{1,0:T(8,128)(2,1)} %bitcast.79, bf16[1536,1024]{1,0:T(8,128)(2,1)} %bitcast.86, ...), custom_call_target="tpu_custom_call" | custom-call | tf_op jit(solution)/shard_map/experts_back_sum/pallas_call | solution.py:784
  256.6 59.0 %attend_back.1 = (bf16[4,4,4,24,2048]{4,3,2,1,0:T(8,128)(2,1)}, bf16[192,2048]{1,0:T(8,128)(2,1)}, bf16[192,1280]{1,0:T(8,128)(2,1)}, bf16[192,1024]{1,0:T(8,128...) custom-call(bf16[96,2048]{1,0:T(8,128)(2,1)} %bitcast.85, ...), custom_call_target="tpu_custom_call" | custom-call | tf_op jit(solution)/shard_map/attend_back/pallas_call | solution.py:1525
  315.6 28.3 %experts_back.1 = (bf16[1536,2176]{1,0:T(8,128)(2,1)}, bf16[768,2048]{1,0:T(8,128)(2,1)}, bf16[384,2048]{1,0:T(8,128)(2,1)}, bf16[128,1280]{1,0:T(8,128)(2,1)}, ...) custom-call(bf16[1536,2176]{1,0:T(8,128)(2,1)} %bitcast.78, ...), custom_call_target="tpu_custom_call" | custom-call | tf_op jit(solution)/shard_map/experts_back/pallas_call | solution.py:838
  343.9 44.3 %moe_back.1 = (bf16[4,24,2048]{2,1,0:T(8,128)(2,1)}, f32[1,2048]{1,0:T(1,128)}, f32[32,2048]{1,0:T(8,128)}) custom-call(bf16[4,4,4,24,2176]{4,3,2,1,0:T(8,128)(2,1)} %bitcast.80, f32[24,2048]{1,0:T(8,128)} %get-tuple-element.131.mid, f32[24,128]{1,0:T(8,128)} %get-tuple-element.132.gates, bf16[144,2048]{1,0:T(8,128)(2,1)} %get-tuple-element.93.refs_0_.refs_5_.pack0, ...), custom_call_target="tpu_custom_call" | custom-call | tf_op jit(solution)/shard_map/moe_back/pallas_call | solution.py:466
  388.2 53.4 %attend_back_last.1 = (bf16[4,24,2048]{2,1,0:T(8,128)(2,1)}, bf16[192,2048]{1,0:T(8,128)(2,1)}, bf16[192,1280]{1,0:T(8,128)(2,1)}, bf16[192,1024]{1,0:T(8,128)(2...) custom-call(bf16[2,96,2048]{2,1,0:T(8,128)(2,1)} %rows.3, ...), custom_call_target="tpu_custom_call" | custom-call | tf_op jit(solution)/shard_map/attend_back_last/pallas_call | solution.py:1525
  441.6 67.0 %finish.1 = (bf16[4,4,128,1280]{3,2,1,0:T(8,128)(2,1)}, bf16[4,4,64,2048]{3,2,1,0:T(8,128)(2,1)}, f32[48,2048]{1,0:T(8,128)}) custom-call(bf16[192,2048]{1,0:T(8,128)(2,1)} %get-tuple-element.142.normed0, bf16[192,1280]{1,0:T(8,128)(2,1)} %get-tuple-element.143.proj0, bf16[64,2048]{1,0:T(8,128)(2,1)} %get-tuple-element.144.second_sum, ...), custom_call_target="tpu_custom_call" | custom-call | tf_op jit(solution)/shard_map/finish/pallas_call | solution.py:1654
  508.6 18.9 %widen.1 = (f32[2048,1024]{1,0:T(8,128)}, f32[2048,128]{1,0:T(8,128)}, f32[2048,128]{1,0:T(8,128)}, f32[1024,2048]{1,0:T(8,128)}, f32[384,2048]{1,0:T(8,128)}, /...) custom-call(s32[1]{0:T(128)} %bitcast.section, ...), custom_call_target="tpu_custom_call" | custom-call | tf_op jit(solution)/shard_map/widen/pallas_call | solution.py:1738
